TPU v7x, 256 devices: a whole 4x4x8 slice. The times are simulated.
256 devices in a mesh: tm: 4 (over z_hi), height: 16 (over z_lo, y, core), pair: 4 (over x).
Axes of the slice: x: 4, y: 4, z: 8 (z_hi: 4, z_lo: 2; z = z_hi * 2 + z_lo), core: 2. Of those that a mesh axis runs over, the one named last changes fastest.
Arguments:
- query_tokens: bfloat16 [4, 4, 32, 12, 32, 1536], P('pair', 'tm', 'height'), may hold values from -6.5 to 6.5
- key_tokens: bfloat16 [4, 4, 32, 12, 32, 1536], P('pair', 'tm', 'height'), may hold values from -6.5 to 6.5
- value_tokens: bfloat16 [4, 4, 32, 12, 32, 1536], P('pair', 'tm', 'height'), may hold values from -6 to 6
- head_weight: bfloat16 [1536, 64], replicated, may hold values from -0.15625 to 0.15625
- target_noise: bfloat16 [4, 4, 32, 12, 32, 64], P('pair', 'tm', 'height'), may hold values from -13 to 13
- far_owner: int32 [4, 4, 32, 12, 1], P('pair', 'tm', 'height'), may hold values from 0 to 15; in each aligned block of 24 rows (0 to 23, 24 to 47, ..., all dimensions but the last counted through in order) at most 2 rows name the same one
- far_offset: int32 [4, 4, 32, 12, 1], P('pair', 'tm', 'height'), may hold values from 0 to 23
- timestep: int32 [2], replicated, may hold values from 0 to 999
- labels: int32 [2], replicated, may hold values from 0 to 100
Outputs:
- weighted_error: bfloat16 [4, 4, 32, 12, 32, 64], P('pair', 'tm', 'height')
- clip_loss: float32 [4], P('pair')
- pair_margin: float32 [4], P('pair')
Inputs may be any that keep to these rules, and one draw needn't show every extreme that they name: `far_owner`: among the 24 query tiles of one index of height (aligned blocks of rows), at most 2 references name one owner; the far tiles of one query tile have different owners.
All inputs are finite; a program needn't handle non-finite values.
Results may differ from a plain program's by a relative error of at most 0.0027.
Values may be sent and summed in bfloat16 or wider, within the bound.
No kernel may reach another device: no remote copies, remote signals or barrier semaphores. Data moves between devices by JAX's collectives and lax.ppermute only.
A program may use at most 256 MiB of HBM per device.

v0:
```python
import math

import jax
import jax.numpy as jnp
from jax import lax
from jax.sharding import PartitionSpec as P

HEADS = 12
HD = 128
RATERS = 100


def with_halo(value, sides, width):
    for axis, dim in sides:
        peers, length = (lax.axis_size(axis), value.shape[dim])
        up = [(i, (i + 1) % peers) for i in range(peers - 1)]
        down = [(j, i) for i, j in up]
        last = lax.slice_in_dim(value, length - width, length, axis=dim)
        initial = lax.slice_in_dim(value, 0, width, axis=dim)
        before = lax.ppermute(last, axis, up)
        after = lax.ppermute(initial, axis, down)
        value = jnp.concatenate([before, value, after], axis=dim)
    return value


def from_partner(value, axis, stride):
    mask = 2**stride
    pairs = [(source, source ^ mask) for source in range(lax.axis_size(axis))]
    return lax.ppermute(value, axis, pairs)


def body(
    query_tokens,
    key_tokens,
    value_tokens,
    head_weight,
    target_noise,
    far_owner,
    far_offset,
    timestep,
    labels,
):
    rows_dev = query_tokens.shape[2]
    columns = query_tokens.shape[3]
    tile_len = query_tokens.shape[4]
    inner = query_tokens.shape[5]
    patch = target_noise.shape[5]
    far_count = far_owner.shape[4]
    heads = HEADS
    head_dim = HD
    height_size = lax.axis_size("height")
    frame_total = lax.axis_size("tm")
    row_total = rows_dev * height_size
    tiles_dev = rows_dev * columns
    slots = max(2, 3 * tiles_dev * far_count // (2 * height_size))
    pair_count = columns // 2
    keyval = jnp.concatenate([key_tokens, value_tokens], axis=5)
    extended = with_halo(keyval, (("tm", 1), ("height", 2)), 1)
    extended = extended[0]
    frame_global = lax.axis_index("tm") + jnp.arange(3) - 1
    frame_ok = (frame_global >= 0) & (frame_global < frame_total)
    row_global = lax.axis_index("height") * rows_dev + jnp.arange(rows_dev + 2) - 1
    row_ok = (row_global >= 0) & (row_global < row_total)
    ref_count = tiles_dev * far_count
    owners = far_owner.reshape(ref_count)
    offsets = far_offset.reshape(ref_count)
    ref_ids = jnp.arange(ref_count)
    payload = offsets + 1
    earlier = ref_ids[:, None] > ref_ids[None, :]
    same_owner = owners[:, None] == owners[None, :]
    rank = jnp.sum((earlier & same_owner).astype(jnp.int32), axis=1)
    slot_id = owners * slots + rank
    onehot = slot_id[:, None] == jnp.arange(height_size * slots)[None, :]
    requests = jnp.sum(jnp.where(onehot, payload[:, None], 0), axis=0).reshape(height_size, slots)
    local_tiles = keyval.reshape(tiles_dev, tile_len, 2 * inner)
    asked = lax.all_to_all(requests, "height", split_axis=0, concat_axis=0, tiled=True)
    wanted = jnp.maximum(asked - 1, 0)
    picked = local_tiles[wanted]
    picked = jnp.where((asked > 0)[:, :, None, None], picked, jnp.zeros((), picked.dtype))
    fetched = lax.all_to_all(picked, "height", split_axis=0, concat_axis=0, tiled=True)
    fetched = fetched.reshape(height_size * slots, tile_len, 2 * inner)
    far_tiles = fetched[slot_id].reshape(tiles_dev, far_count, tile_len, 2 * inner)
    queries_local = query_tokens.reshape(rows_dev, pair_count, 2 * tile_len, heads, head_dim)
    score_scale = 1.0 / math.sqrt(head_dim)
    pair_ids = jnp.arange(pair_count)
    has_left = pair_ids > 0
    has_right = pair_ids < pair_count - 1
    query_side = jnp.arange(2)
    side_tiles = 9
    near_count = 9 + 18 + 9
    key_tiles = near_count + 2 * far_count

    def attend_row(row):
        centre = lax.dynamic_slice_in_dim(extended, row, 3, 1).reshape(
            3, 3, pair_count, 2, tile_len, 2 * inner
        )
        left = jnp.roll(centre[:, :, :, 1], 1, axis=2)
        right = jnp.roll(centre[:, :, :, 0], -1, axis=2)
        far_block = lax.dynamic_slice_in_dim(far_tiles, row * columns, columns, 0).reshape(
            pair_count, 2, far_count, tile_len, 2 * inner
        )
        query_block = queries_local[row]
        left_keys = left[..., :inner].reshape(3, 3, pair_count, tile_len, heads, head_dim)
        left_vals = left[..., inner:].reshape(3, 3, pair_count, tile_len, heads, head_dim)
        right_keys = right[..., :inner].reshape(3, 3, pair_count, tile_len, heads, head_dim)
        right_vals = right[..., inner:].reshape(3, 3, pair_count, tile_len, heads, head_dim)
        centre_keys = centre[..., :inner].reshape(3, 3, pair_count, 2, tile_len, heads, head_dim)
        centre_vals = centre[..., inner:].reshape(3, 3, pair_count, 2, tile_len, heads, head_dim)
        far_keys = far_block[..., :inner].reshape(
            pair_count, 2, far_count, tile_len, heads, head_dim
        )
        far_vals = far_block[..., inner:].reshape(
            pair_count, 2, far_count, tile_len, heads, head_dim
        )
        qrows = 2 * tile_len
        score_left = jnp.einsum(
            "pqhd,fgpkhd->phqfgk", query_block, left_keys, preferred_element_type=jnp.float32
        ).reshape(pair_count, heads, qrows, side_tiles * tile_len)
        score_centre = jnp.einsum(
            "pqhd,fgpjkhd->phqfgjk", query_block, centre_keys, preferred_element_type=jnp.float32
        ).reshape(pair_count, heads, qrows, 18 * tile_len)
        score_right = jnp.einsum(
            "pqhd,fgpkhd->phqfgk", query_block, right_keys, preferred_element_type=jnp.float32
        ).reshape(pair_count, heads, qrows, side_tiles * tile_len)
        score_far = jnp.einsum(
            "pqhd,pjnkhd->phqjnk", query_block, far_keys, preferred_element_type=jnp.float32
        ).reshape(pair_count, heads, qrows, 2 * far_count * tile_len)
        scores = (
            jnp.concatenate([score_left, score_centre, score_right, score_far], axis=3)
            * score_scale
        )
        near_ok = frame_ok[:, None] & lax.dynamic_slice_in_dim(row_ok, row, 3)[None, :]
        left_ok = near_ok[None, None] & (
            has_left[:, None, None, None] & (query_side == 0)[None, :, None, None]
        )
        right_ok = near_ok[None, None] & (
            has_right[:, None, None, None] & (query_side == 1)[None, :, None, None]
        )
        centre_ok = jnp.broadcast_to(near_ok[None, None, :, :, None], (pair_count, 2, 3, 3, 2))
        far_ok = jnp.broadcast_to(
            (query_side[:, None, None] == query_side[None, :, None])[None],
            (pair_count, 2, 2, far_count),
        )
        tile_ok = jnp.concatenate(
            [
                left_ok.reshape(pair_count, 2, 9),
                centre_ok.reshape(pair_count, 2, 18),
                right_ok.reshape(pair_count, 2, 9),
                far_ok.reshape(pair_count, 2, 2 * far_count),
            ],
            axis=2,
        )
        token_ok = jnp.broadcast_to(
            tile_ok[:, :, None, :, None], (pair_count, 2, tile_len, key_tiles, tile_len)
        ).reshape(pair_count, qrows, key_tiles * tile_len)
        scores = jnp.where(token_ok[:, None], scores, -1e30)
        top_score = jnp.max(scores, axis=3, keepdims=True)
        weights = jnp.exp(scores - top_score)
        total = jnp.sum(weights, axis=3)
        rounded = weights.astype(jnp.bfloat16)
        cut_one = side_tiles * tile_len
        cut_two = cut_one + 18 * tile_len
        cut_three = cut_two + side_tiles * tile_len
        round_left = rounded[..., :cut_one].reshape(pair_count, heads, qrows, 3, 3, tile_len)
        round_centre = rounded[..., cut_one:cut_two].reshape(
            pair_count, heads, qrows, 3, 3, 2, tile_len
        )
        round_right = rounded[..., cut_two:cut_three].reshape(
            pair_count, heads, qrows, 3, 3, tile_len
        )
        round_far = rounded[..., cut_three:].reshape(
            pair_count, heads, qrows, 2, far_count, tile_len
        )
        mixed = jnp.einsum(
            "phqfgk,fgpkhd->pqhd", round_left, left_vals, preferred_element_type=jnp.float32
        )
        mixed = mixed + jnp.einsum(
            "phqfgjk,fgpjkhd->pqhd", round_centre, centre_vals, preferred_element_type=jnp.float32
        )
        mixed = mixed + jnp.einsum(
            "phqfgk,fgpkhd->pqhd", round_right, right_vals, preferred_element_type=jnp.float32
        )
        mixed = mixed + jnp.einsum(
            "phqjnk,pjnkhd->pqhd", round_far, far_vals, preferred_element_type=jnp.float32
        )
        mixed = mixed / jnp.transpose(total, (0, 2, 1))[:, :, :, None]
        return mixed.astype(jnp.bfloat16).reshape(columns, tile_len, inner)

    attended = lax.map(attend_row, jnp.arange(rows_dev))
    attended = attended.reshape(tiles_dev * tile_len, inner)
    prediction = jnp.dot(attended, head_weight, preferred_element_type=jnp.float32)
    error = prediction - target_noise.reshape(tiles_dev * tile_len, patch).astype(jnp.float32)
    pair_slot = lax.axis_index("pair") // 2
    step_weight = 0.5 + (timestep[pair_slot].astype(jnp.float32) + 1.0) / 1000.0
    weighted_error = (
        (jnp.sqrt(step_weight) * error).astype(jnp.bfloat16).reshape(target_noise.shape)
    )
    total_sum = lax.psum(jnp.sum(error * error), ("tm", "height"))
    count = frame_total * row_total * columns * tile_len * patch
    clip_loss = (step_weight * total_sum / count).reshape(1)
    partner = from_partner(clip_loss, "pair", 0)
    second_clip = lax.axis_index("pair") % 2 == 1
    difference = jnp.where(second_clip, clip_loss - partner, partner - clip_loss)
    strength = 2.0 * labels[pair_slot].astype(jnp.float32) / RATERS - 1.0
    pair_margin = strength * difference
    return (weighted_error, clip_loss, pair_margin)


def solution(mesh):
    placed = (
        P("pair", "tm", "height", None, None, None),
        P("pair", "tm", "height", None, None, None),
        P("pair", "tm", "height", None, None, None),
        P(),
        P("pair", "tm", "height", None, None, None),
        P("pair", "tm", "height", None, None),
        P("pair", "tm", "height", None, None),
        P(),
        P(),
    )
    return jax.shard_map(
        body,
        mesh=mesh,
        in_specs=placed,
        out_specs=(P("pair", "tm", "height", None, None, None), P("pair"), P("pair")),
        check_vma=False,
    )
```

profile of v0, /device:TPU:128, one launch (start us, length us, event | category | flops | bytes accessed | tf_op | source)
XLA Modules:
  0.0 1200.0 jit_solution(3395533934873190770)
XLA Ops:
  0.7 3.5 constant_dynamic-update-slice_fusion.2
  9.1 4.6 collective-permute-start.1
  15.4 204.0 %all_to_all.14 = s32[16,1,2]{2,1,0:T(1,128)S(1)} all-to-all(s32[16,1,2]{2,1,0:T(1,128)S(1)} %bitcast.198), channel_id=1, replica_groups=mesh['tm'=4,'height'=16,'pair'=4] {'height'}, dimensions={0} | all-to-all | bytes 256 | tf_op jit(solution)/shard_map/all_to_all | solution.py:76
  219.8 6.0 gather_fusion
  225.8 5.9 broadcast_select_fusion
  231.7 4.6 all-to-all-start.1
  236.4 6.7 pad_maximum_fusion.2
  243.0 5.5 fusion.53
  248.5 5.0 collective-permute-start.2
  267.0 19.6 %maximum_bitcast_fusion = bf16[3,4,12,32,3072]{4,3,2,1,0:T(8,128)(2,1)} fusion(bf16[1,3,1,12,32,3072]{5,4,3,2,1,0:T(8,128)(2,1)} %collective-permute-done.3, bf16[1,1,2,12,32,3072]{5,4,3,2,1,0:T(8,128)(2,1)} %collective-permute-done.1, bf16[1,1,2,12,32,3072]{5,4,3,2,1,0:T(8,128)(2,1)} %constant_dynamic-update-slice_fusion.1, ...), kind=kLoop, calls=%fused_computation.71 | loop fusion | flops 56623104 | bytes 56623104 | tf_op jit(solution)/shard_map/squeeze | solution.py:59
  286.6 37.8 %all-to-all-done.1 = bf16[16,2,32,3072]{3,2,1,0:T(8,128)(2,1)} async-done(((bf16[16,2,32,3072]{3,2,1,0:T(8,128)(2,1)}), bf16[16,2,32,3072]{3,2,1,0:T(8,128)(2,1)}, u32[]{:S(2)}, u32[]{:S(2)}) %all-to-all-start.1) | async-done | bytes 6291488 | tf_op jit(solution)/shard_map/all_to_all | solution.py:80
  324.4 5.9 gather_fusion.1
  330.3 643.3 %while.13 = (s32[]{:T(128)}, bf16[2,12,32,1536]{3,2,1,0:T(8,128)(2,1)}, s32[2]{0:T(128)S(1)}, bf16[3,4,12,32,3072]{4,3,2,1,0:T(8,128)(2,1)}, pred[4]{0:T(512)(12...) while((s32[]{:T(128)}, ...), condition=%wide.region_5.6_spmd.clone.clone, body=%wide.region_2.5_spmd.clone.clone.sunk | while | flops 2959149824 | bytes 565041664 | solution.py:189
  358.2 4.5 broadcast_in_dim.160
  364.6 10.1 constant_dynamic-slice_fusion.5
  374.8 9.5 slice_bitcast_fusion.3
  384.2 4.1 copy-done.1
  388.3 8.3 slice.193
  398.2 8.6 fusion.109
  406.8 10.4 reshape.488
  418.4 8.6 fusion.110
  427.0 8.3 slice.191
  436.9 8.6 pad_maximum_fusion.4
  445.5 10.4 reshape.486
  456.0 8.5 fusion.106
  476.0 15.4 %fusion.107 = (bf16[3,3,6,2,32,1536]{5,4,3,2,1,0:T(8,128)(2,1)}, bf16[3,3,6,2,32,1536]{5,4,3,2,1,0:T(8,128)(2,1)}) fusion(bf16[3,3,6,2,32,3072]{5,4,3,2,1,0:T(8,128)(2,1)} %bitcast.184), kind=kLoop, calls=%fused_computation.98.clone.1 | loop fusion | bytes 42467328 | tf_op jit(solution)/shard_map/while/body/eval_jaxpr/slice | solution.py:108
  491.4 19.9 %reshape.487 = bf16[3,3,6,2,32,12,128]{6,5,4,3,2,1,0:T(8,128)(2,1)} reshape(bf16[3,3,6,2,32,1536]{5,4,3,2,1,0:T(8,128)(2,1)} %get-tuple-element.297) | data formatting | bytes 21233664 | tf_op jit(solution)/shard_map/while/body/eval_jaxpr/reshape | solution.py:107
  511.3 12.4 %fusion.108 = f32[6,12,64,3,3,2,32]{2,6,5,4,3,1,0:T(8,128)} fusion(bf16[3,3,6,2,32,12,128]{6,5,4,3,2,1,0:T(8,128)(2,1)} %reshape.487, bf16[2,6,64,12,128]{4,2,3,1,0:T(8,128)(2,1)S(1)} %get-tuple-element.349, s32[]{:T(128)S(6)} %select_n.93), kind=kOutput, calls=%fused_computation.18.clone.1 | convolution fusion | flops 679477248 | bytes 22413316 | tf_op jit(solution)/shard_map/while/body/eval_jaxpr/pqhd,fgpjkhd->phqfgjk/dot_general | solution.py:119
  523.7 28.3 %fusion.111 = (f32[6,12,64]{2,1,0:T(8,128)S(1)}, bf16[6,12,64,1216]{2,3,1,0:T(8,128)(2,1)}) fusion(f32[6,12,64,64]{2,3,1,0:T(8,128)} %convolution_bitcast_fusion.2, f32[6,12,64,288]{2,3,1,0:T(8,128)} %bitcast.189, f32[6,12,64,576]{2,3,1,0:T(8,128)} %bitcast.186, f32[6,12,64,288]{2,3,1,0:T(8,128)} %bitcast.188, pred[6,64,1216]{1,2,0:T(8,128)(4,1)S(1)} %copy-done.2), kind=kOutput, calls=%fused_computation.96.clone.1 | output fusion | flops 44827840 | bytes 34105344 | tf_op jit(solution)/shard_map/while/body/eval_jaxpr/sub | solution.py:158
  552.0 9.3 slice.194
  561.3 19.9 %reshape.492 = bf16[3,3,6,2,32,12,128]{6,5,4,3,2,1,0:T(8,128)(2,1)} reshape(bf16[3,3,6,2,32,1536]{5,4,3,2,1,0:T(8,128)(2,1)} %get-tuple-element.309) | data formatting | bytes 21233664 | tf_op jit(solution)/shard_map/while/body/eval_jaxpr/reshape | solution.py:108
  581.2 12.8 %fusion.114 = f32[6,12,128,64,1,1,1]{2,3,6,5,4,1,0:T(8,128)} fusion(bf16[6,12,64,3,3,2,32]{2,6,5,4,3,1,0:T(8,128)(2,1)} %bitcast.185, bf16[3,3,6,2,32,12,128]{6,5,4,3,2,1,0:T(8,128)(2,1)} %reshape.492), kind=kOutput, calls=%fused_computation.16.clone.1 | convolution fusion | flops 679477248 | bytes 18284544 | tf_op jit(solution)/shard_map/while/body/eval_jaxpr/phqfgjk,fgpjkhd->pqhd/dot_general | solution.py:177
  594.1 9.9 fusion.112
  604.0 10.5 reshape.491
  614.5 8.5 fusion.113
  628.9 3.7 fusion.115
  632.6 10.5 reshape.494
  643.0 11.1 fusion.116
  668.6 4.5 broadcast_in_dim.160
  675.1 10.1 constant_dynamic-slice_fusion.5
  685.2 9.5 slice_bitcast_fusion.3
  694.6 4.1 copy-done.1
  698.7 8.3 slice.193
  708.6 8.6 fusion.109
  717.2 10.4 reshape.488
  728.8 8.6 fusion.110
  737.4 8.3 slice.191
  747.3 8.6 pad_maximum_fusion.4
  755.9 10.4 reshape.486
  766.4 8.5 fusion.106
  786.4 15.4 %fusion.107 = (bf16[3,3,6,2,32,1536]{5,4,3,2,1,0:T(8,128)(2,1)}, bf16[3,3,6,2,32,1536]{5,4,3,2,1,0:T(8,128)(2,1)}) fusion(bf16[3,3,6,2,32,3072]{5,4,3,2,1,0:T(8,128)(2,1)} %bitcast.184), kind=kLoop, calls=%fused_computation.98.clone.1 | loop fusion | bytes 42467328 | tf_op jit(solution)/shard_map/while/body/eval_jaxpr/slice | solution.py:108
  801.8 19.9 %reshape.487 = bf16[3,3,6,2,32,12,128]{6,5,4,3,2,1,0:T(8,128)(2,1)} reshape(bf16[3,3,6,2,32,1536]{5,4,3,2,1,0:T(8,128)(2,1)} %get-tuple-element.297) | data formatting | bytes 21233664 | tf_op jit(solution)/shard_map/while/body/eval_jaxpr/reshape | solution.py:107
  821.7 12.4 %fusion.108 = f32[6,12,64,3,3,2,32]{2,6,5,4,3,1,0:T(8,128)} fusion(bf16[3,3,6,2,32,12,128]{6,5,4,3,2,1,0:T(8,128)(2,1)} %reshape.487, bf16[2,6,64,12,128]{4,2,3,1,0:T(8,128)(2,1)S(1)} %get-tuple-element.349, s32[]{:T(128)S(6)} %select_n.93), kind=kOutput, calls=%fused_computation.18.clone.1 | convolution fusion | flops 679477248 | bytes 22413316 | tf_op jit(solution)/shard_map/while/body/eval_jaxpr/pqhd,fgpjkhd->phqfgjk/dot_general | solution.py:119
  834.1 28.3 %fusion.111 = (f32[6,12,64]{2,1,0:T(8,128)S(1)}, bf16[6,12,64,1216]{2,3,1,0:T(8,128)(2,1)}) fusion(f32[6,12,64,64]{2,3,1,0:T(8,128)} %convolution_bitcast_fusion.2, f32[6,12,64,288]{2,3,1,0:T(8,128)} %bitcast.189, f32[6,12,64,576]{2,3,1,0:T(8,128)} %bitcast.186, f32[6,12,64,288]{2,3,1,0:T(8,128)} %bitcast.188, pred[6,64,1216]{1,2,0:T(8,128)(4,1)S(1)} %copy-done.2), kind=kOutput, calls=%fused_computation.96.clone.1 | output fusion | flops 44827840 | bytes 34105344 | tf_op jit(solution)/shard_map/while/body/eval_jaxpr/sub | solution.py:158
  862.4 9.3 slice.194
  871.7 19.9 %reshape.492 = bf16[3,3,6,2,32,12,128]{6,5,4,3,2,1,0:T(8,128)(2,1)} reshape(bf16[3,3,6,2,32,1536]{5,4,3,2,1,0:T(8,128)(2,1)} %get-tuple-element.309) | data formatting | bytes 21233664 | tf_op jit(solution)/shard_map/while/body/eval_jaxpr/reshape | solution.py:108
  891.7 12.8 %fusion.114 = f32[6,12,128,64,1,1,1]{2,3,6,5,4,1,0:T(8,128)} fusion(bf16[6,12,64,3,3,2,32]{2,6,5,4,3,1,0:T(8,128)(2,1)} %bitcast.185, bf16[3,3,6,2,32,12,128]{6,5,4,3,2,1,0:T(8,128)(2,1)} %reshape.492), kind=kOutput, calls=%fused_computation.16.clone.1 | convolution fusion | flops 679477248 | bytes 18284544 | tf_op jit(solution)/shard_map/while/body/eval_jaxpr/phqfgjk,fgpjkhd->pqhd/dot_general | solution.py:177
  904.5 9.9 fusion.112
  914.4 10.5 reshape.491
  924.9 8.5 fusion.113
  939.3 3.7 fusion.115
  943.0 10.5 reshape.494
  953.4 11.1 fusion.116
  976.8 214.9 %psum.7 = f32[]{:T(128)} all-reduce(f32[]{:T(128)} %get-tuple-element.222), channel_id=1, replica_groups=mesh['tm'=4,'height'=16,'pair'=4] {'tm','height'}, use_global_device_ids=true, to_apply=%region_7.8 | all-reduce | flops 1 | bytes 8 | tf_op jit(solution)/shard_map/psum | solution.py:198
  (144 shorter events, 95.4 us)
Async XLA Ops:
  0.6 973.0 %copy-start = (bf16[1536,64]{0,1:T(8,128)(2,1)S(1)}, bf16[1536,64]{0,1:T(8,128)(2,1)}, u32[]{:S(2)}) copy-start(bf16[1536,64]{0,1:T(8,128)(2,1)} %param.14) | copy-start | bytes 589828
  0.6 3.5 copy-start.3
  0.7 13.6 %copy-start.6 = (s32[1,1,2,12,1]{3,4,2,1,0:T(1,128)S(1)}, s32[1,1,2,12,1]{3,4,2,1,0:T(1,128)}, u32[]{:S(2)}) copy-start(s32[1,1,2,12,1]{3,4,2,1,0:T(1,128)} %param.16) | copy-start | bytes 292
  0.7 13.6 %copy-start.7 = (s32[1,1,2,12,1]{3,4,2,1,0:T(1,128)S(1)}, s32[1,1,2,12,1]{3,4,2,1,0:T(1,128)}, u32[]{:S(2)}) copy-start(s32[1,1,2,12,1]{3,4,2,1,0:T(1,128)} %param.17) | copy-start | bytes 292
  5.8 230.6 %collective-permute-start = (bf16[1,1,2,12,32,3072]{5,4,3,2,1,0:T(8,128)(2,1)}, bf16[1,1,2,12,32,3072]{5,4,3,2,1,0:T(8,128)(2,1)}, u32[]{:S(2)}, u32[]{:S(2)}) collective-permute-start(bf16[1,1,2,12,32,3072]{5,4,3,2,1,0:T(8,128)(2,1)} %constant_dynamic-update-slice_fusion.1), channel_id=1, source_target_pairs={{0,64},{64,128},{128,192},{1,65},{65,129},{129,193},{2,66},{66,130... | collective-permute-start | bytes 14155784 | tf_op jit(solution)/shard_map/ppermute | solution.py:20
  9.1 227.2 %collective-permute-start.1 = (bf16[1,1,2,12,32,3072]{5,4,3,2,1,0:T(8,128)(2,1)}, bf16[1,1,2,12,32,3072]{5,4,3,2,1,0:T(8,128)(2,1)}, u32[]{:S(2)}, u32[]{:S(2)}) collective-permute-start(bf16[1,1,2,12,32,3072]{5,4,3,2,1,0:T(8,128)(2,1)} %constant_dynamic-update-slice_fusion.1), channel_id=1, source_target_pairs={{64,0},{128,64},{192,128},{65,1},{129,65},{193,129},{66,2},{130,66... | collective-permute-start | bytes 14155784 | tf_op jit(solution)/shard_map/ppermute | solution.py:21
  231.7 92.7 %all-to-all-start.1 = ((bf16[16,2,32,3072]{3,2,1,0:T(8,128)(2,1)}), bf16[16,2,32,3072]{3,2,1,0:T(8,128)(2,1)}, u32[]{:S(2)}, u32[]{:S(2)}) async-start(bf16[16,2,32,3072]{3,2,1,0:T(8,128)(2,1)} %broadcast_select_fusion), calls=%async_computation.1 | async-start | bytes 12582912 | tf_op jit(solution)/shard_map/all_to_all | solution.py:80
  243.0 11.8 copy-start.8
  243.0 13.2 %copy-start.4 = (bf16[1,1,2,12,32,1536]{5,4,3,2,1,0:T(8,128)(2,1)S(1)}, bf16[1,1,2,12,32,1536]{5,4,3,2,1,0:T(8,128)(2,1)}, u32[]{:S(2)}) copy-start(bf16[1,1,2,12,32,1536]{5,4,3,2,1,0:T(8,128)(2,1)} %param.11) | copy-start | bytes 7077892
  248.5 15.4 %collective-permute-start.2 = (bf16[1,3,1,12,32,3072]{5,4,3,2,1,0:T(8,128)(2,1)}, bf16[1,3,1,12,32,3072]{5,4,3,2,1,0:T(8,128)(2,1)}, u32[]{:S(2)}, u32[]{:S(2)}) collective-permute-start(bf16[1,3,1,12,32,3072]{5,4,3,2,1,0:T(8,128)(2,1)} %get-tuple-element.220), channel_id=1, source_target_pairs={{0,4},{4,8},{8,12},{12,16},{16,20},{20,24},{24,28},{28,32},{32,36}... | collective-permute-start | bytes 21233672 | tf_op jit(solution)/shard_map/ppermute | solution.py:20
  253.5 13.5 %collective-permute-start.3 = (bf16[1,3,1,12,32,3072]{5,4,3,2,1,0:T(8,128)(2,1)}, bf16[1,3,1,12,32,3072]{5,4,3,2,1,0:T(8,128)(2,1)}, u32[]{:S(2)}, u32[]{:S(2)}) collective-permute-start(bf16[1,3,1,12,32,3072]{5,4,3,2,1,0:T(8,128)(2,1)} %get-tuple-element.221), channel_id=1, source_target_pairs={{4,0},{8,4},{12,8},{16,12},{20,16},{24,20},{28,24},{32,28},{36,32}... | collective-permute-start | bytes 21233672 | tf_op jit(solution)/shard_map/ppermute | solution.py:21
  256.2 5.6 copy-start.5
  256.2 6.5 copy-start.9
  352.8 2.8 copy-start.10
  352.9 3.3 copy-start.12
  374.7 13.6 %copy-start.1 = (bf16[3,3,12,32,3072]{4,3,2,1,0:T(8,128)(2,1)}, bf16[3,3,12,32,3072]{4,3,2,1,0:T(8,128)(2,1)S(1)}, u32[]{:S(2)}) copy-start(bf16[3,3,12,32,3072]{4,3,2,1,0:T(8,128)(2,1)S(1)} %constant_dynamic-slice_fusion.5) | copy-start | bytes 63700996 | tf_op jit(solution)/shard_map/while
  511.3 12.4 %copy-start.2 = (pred[6,64,1216]{1,2,0:T(8,128)(4,1)S(1)}, pred[6,64,1216]{1,2,0:T(8,128)(4,1)}, u32[]{:S(2)}) copy-start(pred[6,64,1216]{1,2,0:T(8,128)(4,1)} %copy.138) | copy-start | bytes 1400836 | tf_op jit(solution)/shard_map/while
  654.1 9.1 copy-start.11
  654.1 9.1 copy-start.13
  663.3 2.8 copy-start.10
  663.3 3.3 copy-start.12
  685.2 13.6 %copy-start.1 = (bf16[3,3,12,32,3072]{4,3,2,1,0:T(8,128)(2,1)}, bf16[3,3,12,32,3072]{4,3,2,1,0:T(8,128)(2,1)S(1)}, u32[]{:S(2)}) copy-start(bf16[3,3,12,32,3072]{4,3,2,1,0:T(8,128)(2,1)S(1)} %constant_dynamic-slice_fusion.5) | copy-start | bytes 63700996 | tf_op jit(solution)/shard_map/while
  821.7 12.4 %copy-start.2 = (pred[6,64,1216]{1,2,0:T(8,128)(4,1)S(1)}, pred[6,64,1216]{1,2,0:T(8,128)(4,1)}, u32[]{:S(2)}) copy-start(pred[6,64,1216]{1,2,0:T(8,128)(4,1)} %copy.138) | copy-start | bytes 1400836 | tf_op jit(solution)/shard_map/while
  964.5 9.1 copy-start.11
  964.5 9.1 copy-start.13
  1192.3 3.7 collective-permute-start.4
where the time goes:
time: 1210 us; the launch traced here: 1200 us
  blocking collectives  419 us (35%)
  local copies, waits for them, and re-layouts  418 us (35%)
  matrix products  139 us (11%)
  other arithmetic  125 us (10%)
  waiting for transfers between devices  40.9 us (3%)
  loops' own time  29.5 us (2%)
  starting transfers between devices  21.7 us (2%)
    psum x1, blocking collectives, body(): total_sum = lax.psum(jnp.sum(error * error), ('tm', 'height'))  215 us
    all_to_all x1, blocking collectives, body(): lax.all_to_all(requests, 'height', split_axis=0, concat_axis=0, tiled=True)  204 us
    sub x2, other arithmetic, attend_row(): weights = jnp.exp(scores - top_score)  56.6 us
    reshape x2, local copies, waits for them, and re-layouts, attend_row(): centre[..., :inner].reshape(3, 3, pair_count, 2, tile_len, heads, head_dim)  39.8 us
    reshape x2, local copies, waits for them, and re-layouts, attend_row(): centre[..., inner:].reshape(3, 3, pair_count, 2, tile_len, heads, head_dim)  39.8 us
    all_to_all x1, waiting for transfers between devices, body(): lax.all_to_all(picked, 'height', split_axis=0, concat_axis=0, tiled=True)  37.8 us
    slice x2, local copies, waits for them, and re-layouts, attend_row(): centre[..., inner:].reshape(3, 3, pair_count, 2, tile_len, heads, head_dim)  30.8 us
    another operation x1, loops' own time, body(): attended = lax.map(attend_row, jnp.arange(rows_dev))  29.5 us
  transfers between devices with their start and end apart: 6, of which 2 were waited for; matrix products, arithmetic and copies ran while one was open for 5% of the time, Pallas kernels for 0%

commit v1 on v0

v1 whole, which is shorter than its diff:
```python
import functools
import math

import jax
import jax.numpy as jnp
from jax import lax
from jax.experimental import pallas as pl
from jax.experimental.pallas import tpu as pltpu
from jax.sharding import PartitionSpec as P

HEADS = 12
HD = 128
PATCH = 64
TILE = 32
RATERS = 100
SLOTS = 2
NEG = -1e30
FACTOR = math.log2(math.e) / math.sqrt(HD)
LSE_ROWS = 16
MIB = 1 << 20

NT = (((1,), (1,)), ((), ()))
NN = (((1,), (0,)), ((), ()))


def dot(a, b, dims):
    return lax.dot_general(a, b, dims, preferred_element_type=jnp.float32)


def lane_iota(shape):
    return lax.broadcasted_iota(jnp.int32, shape, 1)


def window_kernel(groups, columns, edge_ref, *refs):
    q_refs = refs[:groups]
    k_refs = refs[groups : groups + 3]
    v_refs = refs[groups + 3 : groups + 6]
    wt_ref = refs[groups + 6]
    p_refs = refs[groups + 7 : 2 * groups + 7]
    l_refs = refs[2 * groups + 7 : 3 * groups + 7]
    acc_refs = refs[3 * groups + 7 :]
    step = pl.program_id(0)
    span = 4 * TILE
    rows = 2 * TILE * groups

    @pl.when(step == 0)
    def _():
        for acc in acc_refs:
            acc[...] = jnp.zeros_like(acc)

    key_tile = lane_iota((rows, span)) // TILE
    query_tile = (lax.broadcasted_iota(jnp.int32, (rows, span), 0) // TILE) % 2
    biases = {}
    pairs = columns // 2
    for pair in range(pairs):
        first = min(max(2 * pair - 1, 0), columns - 4)
        shift = 2 * pair - first
        if shift not in biases:
            near = jnp.abs(key_tile - query_tile - shift) <= 1
            base = jnp.where(near, 0.0, NEG)
            biases[shift] = (base + edge_ref[0], base, base + edge_ref[1])
    for half in range(2):
        lanes = slice(half * HD, half * HD + HD)
        head = 2 * step + half
        wt = wt_ref[:, lanes]
        for pair in range(pairs):
            first = min(max(2 * pair - 1, 0), columns - 4)
            bias = biases[2 * pair - first]
            tokens = slice(2 * TILE * pair, 2 * TILE * (pair + 1))
            keys = slice(TILE * first, TILE * (first + 4))
            queries = [q[tokens, lanes] for q in q_refs]
            query = queries[0] if groups == 1 else jnp.concatenate(queries, axis=0)
            scores = [dot(query, k_refs[i][keys, lanes], NT) + bias[i] for i in range(3)]
            top = jnp.max(jnp.maximum(jnp.maximum(scores[0], scores[1]), scores[2]), axis=1, keepdims=True)
            weights = [jnp.exp2((s - top) * FACTOR) for s in scores]
            total = jnp.sum(weights[0] + weights[1] + weights[2], axis=1, keepdims=True)
            mixed = sum(dot(weights[i].astype(jnp.bfloat16), v_refs[i][keys, lanes], NN) for i in range(3))
            mixed = (mixed * (1.0 / total)).astype(jnp.bfloat16)
            projected = dot(wt, mixed, NT)
            lse = top * FACTOR + jnp.log2(total)
            for g in range(groups):
                part = slice(2 * TILE * g, 2 * TILE * (g + 1))
                p_refs[g][PATCH * half : PATCH * (half + 1), tokens] = projected[:, part]
                acc = acc_refs[g]
                held = acc[tokens, :]
                acc[tokens, :] = jnp.where(lane_iota(held.shape) == head, lse[part], held)

    @pl.when(step == pl.num_programs(0) - 1)
    def _():
        for g in range(groups):
            l_refs[g][...] = jnp.transpose(acc_refs[g][...])[:LSE_ROWS, :]


def window_attention(edge, queries, query_block, keys, values, wt, columns):
    groups = len(queries)
    tokens = columns * TILE
    inner = wt.shape[1]
    steps = inner // (2 * HD)

    def block(row):
        return pl.BlockSpec((tokens, 2 * HD), lambda i, row=row: (row, i))

    specs = [pl.BlockSpec(memory_space=pltpu.SMEM)]
    specs += [block(query_block) for _ in queries]
    specs += [block(row) for _, row in keys] + [block(row) for _, row in values]
    specs += [pl.BlockSpec((PATCH, 2 * HD), lambda i: (0, i))]
    operands = [edge, *queries, *[a for a, _ in keys], *[a for a, _ in values], wt]
    heads = inner // HD
    flops = 2 * groups * tokens * heads * 12 * TILE * HD * 2
    out = pl.pallas_call(
        functools.partial(window_kernel, groups, columns),
        grid=(steps,),
        in_specs=specs,
        out_specs=[pl.BlockSpec((2 * PATCH, tokens), lambda i: (i, 0))] * groups
        + [pl.BlockSpec((LSE_ROWS, tokens), lambda i: (0, 0))] * groups,
        out_shape=[jax.ShapeDtypeStruct((heads * PATCH, tokens), jnp.float32)] * groups
        + [jax.ShapeDtypeStruct((LSE_ROWS, tokens), jnp.float32)] * groups,
        scratch_shapes=[pltpu.VMEM((tokens, 128), jnp.float32)] * groups,
        compiler_params=pltpu.CompilerParams(vmem_limit_bytes=32 * MIB),
        cost_estimate=pl.CostEstimate(flops=flops, bytes_accessed=8 * MIB, transcendentals=flops // 512),
    )(*operands)
    return out[:groups], out[groups:]


def far_kernel(per_step, heads, index_ref, query_ref, key_ref, value_ref, wbd_ref, out_ref):
    step = pl.program_id(0)
    upper = lax.broadcasted_iota(jnp.int32, (2 * TILE, 2 * HD), 0) // TILE
    right = lane_iota((2 * TILE, 2 * HD)) // HD
    own_half = upper == right
    lane = lane_iota((TILE, 128))
    for s in range(per_step):
        tile = index_ref[step * per_step + s]
        start = pl.multiple_of(tile * TILE, TILE)
        rows = slice(s * TILE, (s + 1) * TILE)
        scores = []
        for j in range(heads // 2):
            lanes = slice(2 * j * HD, 2 * (j + 1) * HD)
            query = query_ref[rows, lanes]
            stacked = jnp.concatenate([query, query], axis=0)
            stacked = jnp.where(own_half, stacked, jnp.zeros_like(stacked))
            scores.append(dot(stacked, key_ref[pl.ds(start, TILE), lanes], NT))
        scores = jnp.concatenate(scores, axis=0)
        top = jnp.max(scores, axis=1, keepdims=True)
        weights = jnp.exp2((scores - top) * FACTOR)
        total = jnp.sum(weights, axis=1, keepdims=True)
        rounded = weights.astype(jnp.bfloat16)
        inverse = 1.0 / total
        lse = top * FACTOR + jnp.log2(total)
        sums = jnp.zeros((TILE, 128), jnp.float32)
        for j in range(heads // 2):
            lanes = slice(2 * j * HD, 2 * (j + 1) * HD)
            pair = slice(2 * j * TILE, 2 * (j + 1) * TILE)
            mixed = dot(rounded[pair], value_ref[pl.ds(start, TILE), lanes], NN) * inverse[pair]
            mixed = jnp.concatenate([mixed[:TILE, :HD], mixed[TILE:, HD:]], axis=1).astype(jnp.bfloat16)
            lanes_out = slice(2 * j * PATCH, 2 * (j + 1) * PATCH)
            out_ref[rows, lanes_out] = dot(mixed, wbd_ref[:, lanes_out], NN).astype(jnp.bfloat16)
            for half in range(2):
                head = 2 * j + half
                sums = jnp.where(lane % LSE_ROWS == head, lse[head * TILE : (head + 1) * TILE], sums)
        high = sums.astype(jnp.bfloat16).astype(jnp.float32)
        middle = (sums - high).astype(jnp.bfloat16).astype(jnp.float32)
        low = sums - high - middle
        parts = jnp.where(lane < LSE_ROWS, high, jnp.where(lane < 2 * LSE_ROWS, middle, low))
        out_ref[rows, heads * PATCH :] = parts.astype(jnp.bfloat16)


def far_attention(index, received, key, value, wbd):
    count = index.shape[0]
    inner = key.shape[1]
    heads = inner // HD
    per_step = 4
    width = heads * PATCH + 128
    return pl.pallas_call(
        functools.partial(far_kernel, per_step, heads),
        grid_spec=pltpu.PrefetchScalarGridSpec(
            num_scalar_prefetch=1,
            grid=(count // per_step,),
            in_specs=[
                pl.BlockSpec((per_step * TILE, inner), lambda i, _: (i, 0)),
                pl.BlockSpec(key.shape, lambda i, _: (0, 0)),
                pl.BlockSpec(value.shape, lambda i, _: (0, 0)),
                pl.BlockSpec(wbd.shape, lambda i, _: (0, 0)),
            ],
            out_specs=pl.BlockSpec((per_step * TILE, width), lambda i, _: (i, 0)),
        ),
        out_shape=jax.ShapeDtypeStruct((count * TILE, width), jnp.bfloat16),
        compiler_params=pltpu.CompilerParams(vmem_limit_bytes=40 * MIB),
        cost_estimate=pl.CostEstimate(flops=1 << 33, bytes_accessed=9 * MIB, transcendentals=1 << 20),
    )(index, received, key, value, wbd)


def log_sum(*parts):
    top = functools.reduce(jnp.maximum, parts)
    return top + jnp.log2(sum(jnp.exp2(p - top) for p in parts))


def weighted_sum(weights, projected, heads):
    return sum(weights[h : h + 1, :] * projected[PATCH * h : PATCH * (h + 1), :] for h in range(heads))


def base_kernel(heads, p_ref, l_ref, far_ref, p_out, l_out):
    far = jnp.transpose(far_ref[...].astype(jnp.float32))
    at = heads * PATCH
    far_lse = far[at : at + LSE_ROWS] + far[at + LSE_ROWS : at + 2 * LSE_ROWS]
    far_lse = far_lse + far[at + 2 * LSE_ROWS : at + 3 * LSE_ROWS]
    own_lse = l_ref[...]
    both = log_sum(own_lse, far_lse)
    own_weight = jnp.exp2(own_lse - both)
    far_weight = jnp.exp2(far_lse - both)
    l_out[...] = both
    for h in range(heads):
        rows = slice(PATCH * h, PATCH * (h + 1))
        p_out[rows, :] = own_weight[h : h + 1, :] * p_ref[rows, :] + far_weight[h : h + 1, :] * far[rows, :]


def whole(kernel, out_shape, cost, *operands, smem=0):
    specs = [pl.BlockSpec(memory_space=pltpu.SMEM)] * smem
    specs += [pl.BlockSpec(memory_space=pltpu.VMEM)] * (len(operands) - smem)
    return pl.pallas_call(
        kernel,
        in_specs=specs,
        out_specs=jax.tree.map(lambda _: pl.BlockSpec(memory_space=pltpu.VMEM), out_shape),
        out_shape=out_shape,
        compiler_params=pltpu.CompilerParams(vmem_limit_bytes=32 * MIB),
        cost_estimate=pl.CostEstimate(flops=cost, bytes_accessed=2 * MIB, transcendentals=1 << 14),
    )(*operands)


def scale_kernel(heads, pu, lu, bu, ou, pd, ld, bd, od, up_out, down_out):
    for p, l, b, o, out in ((pu, lu, bu, ou, up_out), (pd, ld, bd, od, down_out)):
        lse = l[...]
        weights = jnp.exp2(lse - log_sum(lse, b[...], o[...]))
        out[:PATCH, :] = weighted_sum(weights, p, heads)
        out[PATCH:, :] = lse


def final_kernel(heads, chunks, scalars, *refs):
    target = refs[4 * chunks]
    error_out, sum_out = refs[4 * chunks + 1 :]
    total = jnp.zeros((1, 1), jnp.float32)
    for c in range(chunks):
        p, l, above, below = refs[4 * c : 4 * c + 4]
        lse = l[...]
        sums = log_sum(lse, above[PATCH:, :] + scalars[1], below[PATCH:, :] + scalars[2])
        out = weighted_sum(jnp.exp2(lse - sums), p, heads) + above[:PATCH, :] + below[:PATCH, :]
        prediction = jnp.transpose(out)
        tokens = prediction.shape[0]
        rows = slice(c * tokens, (c + 1) * tokens)
        error = prediction - target[rows, :].astype(jnp.float32)
        error_out[rows, :] = (scalars[0] * error).astype(jnp.bfloat16)
        total = total + jnp.sum(error * error, keepdims=True)
    sum_out[...] = jnp.broadcast_to(total, sum_out.shape)


def body(
    query_tokens,
    key_tokens,
    value_tokens,
    head_weight,
    target_noise,
    far_owner,
    far_offset,
    timestep,
    labels,
):
    _, _, rows_dev, columns, tile_len, inner = query_tokens.shape
    tiles = rows_dev * columns
    heads = inner // HD
    row_tokens = columns * tile_len
    tokens = rows_dev * row_tokens
    pairs_n, frames_n, height_n = (lax.axis_size(a) for a in ("pair", "tm", "height"))
    frame = lax.axis_index("tm")
    height = lax.axis_index("height")

    up_frames = [(i, i + 1) for i in range(frames_n - 1)]
    down_frames = [(i + 1, i) for i in range(frames_n - 1)]
    up_rows = [(i, i + 1) for i in range(height_n - 1)]
    down_rows = [(i + 1, i) for i in range(height_n - 1)]

    query = query_tokens.reshape(tokens, inner)
    key = key_tokens.reshape(tokens, inner)
    value = value_tokens.reshape(tokens, inner)

    last = jnp.concatenate([key[row_tokens:], value[row_tokens:]], axis=0)
    initial = jnp.concatenate([key[:row_tokens], value[:row_tokens]], axis=0)
    halo_before = lax.ppermute(last, "height", up_rows)
    halo_after = lax.ppermute(initial, "height", down_rows)

    owners = far_owner.reshape(tiles)
    offsets = far_offset.reshape(tiles)
    ids = jnp.arange(tiles)
    earlier = (ids[:, None] > ids[None, :]) & (owners[:, None] == owners[None, :])
    slot = owners * SLOTS + jnp.sum(earlier.astype(jnp.int32), axis=1)
    slot_count = height_n * SLOTS
    chosen = slot[:, None] == jnp.arange(slot_count)[None, :]
    source = jnp.sum(jnp.where(chosen, ids[:, None], 0), axis=0)
    marks = jnp.broadcast_to(offsets.astype(jnp.bfloat16)[:, None, None], (tiles, tile_len, 128))
    payload = jnp.concatenate([query.reshape(tiles, tile_len, inner), marks], axis=2)[source]
    received = lax.all_to_all(payload, "height", split_axis=0, concat_axis=0, tiled=True)

    from_below = []
    from_above = []
    for r in range(rows_dev):
        part = query[r * row_tokens : (r + 1) * row_tokens]
        from_below.append(lax.ppermute(part, "tm", up_frames))
        from_above.append(lax.ppermute(part, "tm", down_frames))

    wt = jnp.transpose(head_weight)
    paired = head_weight.reshape(heads // 2, 2, HD, PATCH)
    wbd = jnp.zeros((2, HD, heads // 2, 2, PATCH), head_weight.dtype)
    for half in range(2):
        wbd = wbd.at[half, :, :, half, :].set(jnp.transpose(paired[:, half], (1, 0, 2)))
    wbd = wbd.reshape(2 * HD, heads * PATCH)

    first_edge = jnp.where(height == 0, NEG, 0.0).astype(jnp.float32)
    last_edge = jnp.where(height == height_n - 1, NEG, 0.0).astype(jnp.float32)
    zero = jnp.zeros((), jnp.float32)

    def attend(r, queries, block):
        before = (halo_before, 0, halo_before, 1) if r == 0 else (key, r - 1, value, r - 1)
        after = (halo_after, 0, halo_after, 1) if r == rows_dev - 1 else (key, r + 1, value, r + 1)
        edge = jnp.stack([first_edge if r == 0 else zero, last_edge if r == rows_dev - 1 else zero])
        keys = [before[:2], (key, r), after[:2]]
        values = [before[2:], (value, r), after[2:]]
        return window_attention(edge, queries, block, keys, values, wt, columns)

    own = []
    for r in range(rows_dev):
        (p,), (l,) = attend(r, [query], r)
        own.append((p, l))

    index = received[:, 0, inner].astype(jnp.int32)
    returned = far_attention(index, received.reshape(slot_count * tile_len, inner + 128), key, value, wbd)
    width = returned.shape[1]
    returned = lax.all_to_all(
        returned.reshape(slot_count, tile_len, width), "height", split_axis=0, concat_axis=0, tiled=True
    )
    far = returned[slot].reshape(tokens, width)

    base = []
    for r in range(rows_dev):
        p, l = own[r]
        shapes = [jax.ShapeDtypeStruct(p.shape, p.dtype), jax.ShapeDtypeStruct(l.shape, l.dtype)]
        base.append(
            whole(
                functools.partial(base_kernel, heads),
                shapes,
                1 << 22,
                p,
                l,
                far[r * row_tokens : (r + 1) * row_tokens],
            )
        )
    base_lse = jnp.concatenate([l for _, l in base], axis=1)
    base_below = lax.ppermute(base_lse, "tm", up_frames)
    base_above = lax.ppermute(base_lse, "tm", down_frames)

    swap = [(i, i + 2) for i in range(frames_n - 2)] + [(i + 2, i) for i in range(frames_n - 2)]
    low = frame < frames_n - 2
    final_args = []
    for r in range(rows_dev):
        cols = slice(r * row_tokens, (r + 1) * row_tokens)
        (pd, pu), (ld, lu) = attend(r, [from_below[r], from_above[r]], 0)
        other = lax.ppermute(jnp.where(low, lu, ld), "tm", swap)
        other_u = jnp.where(low, other, NEG)
        other_d = jnp.where(low, NEG, other)
        shape = jax.ShapeDtypeStruct((PATCH + LSE_ROWS, row_tokens), jnp.float32)
        to_above, to_below = whole(
            functools.partial(scale_kernel, heads),
            [shape, shape],
            1 << 22,
            pu,
            lu,
            base_above[:, cols],
            other_u,
            pd,
            ld,
            base_below[:, cols],
            other_d,
        )
        got_below = lax.ppermute(to_above, "tm", up_frames)
        got_above = lax.ppermute(to_below, "tm", down_frames)
        final_args += [*base[r], got_above, got_below]

    pair = lax.axis_index("pair")
    pair_slot = pair // 2
    step_weight = 0.5 + (timestep[pair_slot].astype(jnp.float32) + 1.0) / 1000.0
    no_above = jnp.where(frame == frames_n - 1, NEG, 0.0).astype(jnp.float32)
    no_below = jnp.where(frame == 0, NEG, 0.0).astype(jnp.float32)
    scalars = jnp.stack([jnp.sqrt(step_weight), no_above, no_below])
    error, squares = whole(
        functools.partial(final_kernel, heads, rows_dev),
        [jax.ShapeDtypeStruct((tokens, PATCH), jnp.bfloat16), jax.ShapeDtypeStruct((8, 128), jnp.float32)],
        1 << 22,
        scalars,
        *final_args,
        target_noise.reshape(tokens, PATCH),
        smem=1,
    )
    weighted_error = error.reshape(target_noise.shape)

    devices = pairs_n * frames_n * height_n
    spread = jnp.broadcast_to(squares[:1], (devices, 128))
    gathered = lax.all_to_all(spread, ("pair", "tm", "height"), split_axis=0, concat_axis=0, tiled=True)
    sums = jnp.sum(gathered.reshape(pairs_n, frames_n * height_n, 128)[:, :, 0], axis=1)
    count = frames_n * height_n * tokens * PATCH
    mine = sums[pair]
    partner = sums[pair ^ 1]
    clip_loss = step_weight * mine / count
    partner_loss = step_weight * partner / count
    difference = jnp.where(pair % 2 == 1, clip_loss - partner_loss, partner_loss - clip_loss)
    strength = 2.0 * labels[pair_slot].astype(jnp.float32) / RATERS - 1.0
    return (weighted_error, clip_loss.reshape(1), (strength * difference).reshape(1))


def solution(mesh):
    placed = (
        P("pair", "tm", "height", None, None, None),
        P("pair", "tm", "height", None, None, None),
        P("pair", "tm", "height", None, None, None),
        P(),
        P("pair", "tm", "height", None, None, None),
        P("pair", "tm", "height", None, None),
        P("pair", "tm", "height", None, None),
        P(),
        P(),
    )
    return jax.shard_map(
        body,
        mesh=mesh,
        in_specs=placed,
        out_specs=(P("pair", "tm", "height", None, None, None), P("pair"), P("pair")),
        check_vma=False,
    )
```

time: 1210 us -> 490 us (0.40)
  the two profiles are of different devices: /device:TPU:128 before, /device:TPU:1 now
where the time goes in v1:
time: 490 us; the launch traced here: 489 us
  starting transfers between devices  208 us (42%)
  Pallas kernels  176 us (36%)
  waiting for transfers between devices  58.1 us (12%)
  local copies, waits for them, and re-layouts  29.6 us (6%)
  other arithmetic  10.9 us (2%)
  between operations  6.11 us (1%)
    pallas_call x4, Pallas kernels, window_attention(): pl.pallas_call(functools.partial(window_kernel, groups, columns), grid=(s...  137 us
    all_to_all x1, starting transfers between devices, body(): lax.all_to_all(spread, ('pair', 'tm', 'height'), split_axis=0, concat_axi...  82.1 us
    ppermute x2, starting transfers between devices, body(): other = lax.ppermute(jnp.where(low, lu, ld), 'tm', swap)  43.8 us
    pallas_call x1, Pallas kernels, far_attention(): pl.pallas_call(functools.partial(far_kernel, per_step, heads), grid_spec=...  35.4 us
    ppermute x2, starting transfers between devices, body(): from_below.append(lax.ppermute(part, 'tm', up_frames))  34.8 us
    all_to_all x1, waiting for transfers between devices, body(): lax.all_to_all(payload, 'height', split_axis=0, concat_axis=0, tiled=True)  22.7 us
    ppermute x2, waiting for transfers between devices, body(): from_above.append(lax.ppermute(part, 'tm', down_frames))  22.3 us
    all_to_all x1, waiting for transfers between devices, body(): lax.all_to_all(spread, ('pair', 'tm', 'height'), split_axis=0, concat_axi...  11.6 us
  transfers between devices with their start and end apart: 17, of which 5 were waited for; matrix products, arithmetic and copies ran while one was open for 4% of the time, Pallas kernels for 36%

profile of v1, /device:TPU:1, one launch (start us, length us, event | category | flops | bytes accessed | tf_op | source)
XLA Modules:
  0.0 488.7 jit_solution(13353868296828599266)
XLA Ops:
  0.6 0.7 convert_reduce_fusion.1
  1.4 0.5 broadcast.135
  1.9 1.3 multiply_reduce_fusion
  3.4 0.2 convert_reduce_fusion
  3.5 0.1 select_reduce_fusion
  3.7 0.1 broadcast_in_dim.24
  3.8 1.9 pad_maximum_fusion
  5.7 2.6 gather_fusion
  8.3 7.6 %all-to-all-start = ((bf16[32,32,1664]{2,1,0:T(8,128)(2,1)}), bf16[32,32,1664]{2,1,0:T(8,128)(2,1)}, u32[]{:S(2)}, u32[]{:S(2)}) async-start(bf16[32,32,1664]{2,1,0:T(8,128)(2,1)} %gather_fusion), calls=%async_computation | async-start | bytes 6815744 | tf_op jit(solution)/shard_map/all_to_all | solution.py:299
  15.9 1.2 fusion.6
  17.1 0.9 copy-done.1
  18.0 1.2 fusion.5
  19.2 1.6 pad_maximum_fusion.1
  20.9 3.7 collective-permute-start
  24.5 1.7 fusion.4
  26.2 5.8 %collective-permute-start.1 = (bf16[384,1536]{1,0:T(8,128)(2,1)}, bf16[384,1536]{1,0:T(8,128)(2,1)}, u32[]{:S(2)}, u32[]{:S(2)}) collective-permute-start(bf16[384,1536]{1,0:T(8,128)(2,1)} %bitcast.23), channel_id=1, source_target_pairs={{0,64},{64,128},{128,192},{1,65},{65,129},{129,193},{2,66},{66,130... | collective-permute-start | bytes 3538952 | tf_op jit(solution)/shard_map/ppermute | solution.py:305
  32.0 0.3 fusion.8
  32.4 1.9 copy.39
  34.3 2.4 reshape.261.wbd_ref
  36.7 22.7 %all-to-all-done = bf16[32,32,1664]{2,1,0:T(8,128)(2,1)} async-done(((bf16[32,32,1664]{2,1,0:T(8,128)(2,1)}), bf16[32,32,1664]{2,1,0:T(8,128)(2,1)}, u32[]{:S(2)}, u32[]{:S(2)}) %all-to-all-start) | async-done | bytes 3407904 | tf_op jit(solution)/shard_map/all_to_all | solution.py:299
  59.4 1.5 fusion.index_ref
  60.9 1.7 copy-done.2
  62.6 35.4 %shard_map.113 = bf16[1024,896]{1,0:T(8,128)(2,1)S(1)} custom-call(s32[32]{0:T(128)S(1)} %fusion.index_ref, bf16[1024,1664]{1,0:T(8,128)(2,1)} %bitcast.12.query_ref, bf16[768,1536]{1,0:T(8,128)(2,1)S(1)} %bitcast.63, bf16[768,1536]{1,0:T(8,128)(2,1)S(1)} %bitcast.54, bf16[256,768]{1,0:T(8,128)(2,1)S(1)} %reshape.261.wbd_ref), custom_call_target="tpu_custom_call" | custom-call | flops 8589934592 | bytes 9437184 | tf_op jit(solution)/shard_map/pallas_call | solution.py:173
  98.0 1.3 copy-done.8
  99.3 10.9 %all-to-all-start.1 = ((bf16[32,32,896]{2,1,0:T(8,128)(2,1)}), bf16[32,32,896]{2,1,0:T(8,128)(2,1)}, u32[]{:S(2)}, u32[]{:S(2)}) async-start(bf16[32,32,896]{2,1,0:T(8,128)(2,1)} %bitcast.81), calls=%async_computation.1 | async-start | bytes 3670016 | tf_op jit(solution)/shard_map/all_to_all | solution.py:335
  110.3 3.2 pad_maximum_fusion.2
  113.4 2.0 collective-permute-start.3
  115.5 1.3 collective-permute-start.2
  116.8 29.0 %collective-permute-start.9 = (bf16[384,1536]{1,0:T(8,128)(2,1)}, bf16[384,1536]{1,0:T(8,128)(2,1)}, u32[]{:S(2)}, u32[]{:S(2)}) collective-permute-start(bf16[384,1536]{1,0:T(8,128)(2,1)} %bitcast.28), channel_id=1, source_target_pairs={{0,64},{64,128},{128,192},{1,65},{65,129},{129,193},{2,66},{66,130... | collective-permute-start | bytes 3538952 | tf_op jit(solution)/shard_map/ppermute | solution.py:305
  145.8 1.3 collective-permute-start.10
  147.4 22.3 %collective-permute-done.2.refs_1_ = bf16[384,1536]{1,0:T(8,128)(2,1)} collective-permute-done((bf16[384,1536]{1,0:T(8,128)(2,1)}, bf16[384,1536]{1,0:T(8,128)(2,1)}, u32[]{:S(2)}, u32[]{:S(2)}) %collective-permute-start.2) | collective-permute-done | bytes 1179680 | tf_op jit(solution)/shard_map/ppermute | solution.py:306
  169.6 1.7 copy-done.3
  171.3 34.4 %shard_map.115 = (f32[768,384]{1,0:T(8,128)S(1)}, f32[768,384]{1,0:T(8,128)S(1)}, f32[16,384]{1,0:T(8,128)S(1)}, f32[16,384]{1,0:T(8,128)S(1)}) custom-call(f32[2]{0:T(128)S(1)} %pad_maximum_fusion.4.edge_ref, bf16[384,1536]{1,0:T(8,128)(2,1)} %collective-permute-done.1.refs_0_, bf16[384,1536]{1,0:T(8,128)(2,1)} %collective-permute-done.2.refs_1_, ...), custom_call_target="tpu_custom_call" | custom-call | flops 1811939328 | bytes 8388608 | tf_op jit(solution)/shard_map/pallas_call | solution.py:110
  205.7 1.0 copy-done.13
  206.8 1.1 copy-done.15
  207.9 20.5 %collective-permute-start.5 = (f32[16,384]{1,0:T(8,128)S(1)}, f32[16,384]{1,0:T(8,128)S(1)}, u32[]{:S(2)}, u32[]{:S(2)}) collective-permute-start(f32[16,384]{1,0:T(8,128)S(1)} %broadcast_select_fusion.5), channel_id=1, source_target_pairs={{0,128},{64,192},{128,0},{192,64},{1,129},{65,193},{129,1},{193,65... | collective-permute-start | bytes 73736 | tf_op jit(solution)/shard_map/ppermute | solution.py:364
  228.5 34.3 %shard_map.119 = (f32[768,384]{1,0:T(8,128)S(1)}, f32[768,384]{1,0:T(8,128)S(1)}, f32[16,384]{1,0:T(8,128)S(1)}, f32[16,384]{1,0:T(8,128)S(1)}) custom-call(f32[2]{0:T(128)S(1)} %pad_maximum_fusion.5.edge_ref, bf16[384,1536]{1,0:T(8,128)(2,1)} %collective-permute-done.9.refs_0_, bf16[384,1536]{1,0:T(8,128)(2,1)} %collective-permute-done.10.refs_1_, ...), custom_call_target="tpu_custom_call" | custom-call | flops 1811939328 | bytes 8388608 | tf_op jit(solution)/shard_map/pallas_call | solution.py:110
  262.8 23.3 %collective-permute-start.11 = (f32[16,384]{1,0:T(8,128)S(1)}, f32[16,384]{1,0:T(8,128)S(1)}, u32[]{:S(2)}, u32[]{:S(2)}) collective-permute-start(f32[16,384]{1,0:T(8,128)S(1)} %broadcast_select_fusion.4), channel_id=1, source_target_pairs={{0,128},{64,192},{128,0},{192,64},{1,129},{65,193},{129,1},{193,65... | collective-permute-start | bytes 73736 | tf_op jit(solution)/shard_map/ppermute | solution.py:364
  286.1 34.3 %shard_map.112 = (f32[768,384]{1,0:T(8,128)S(1)}, f32[16,384]{1,0:T(8,128)S(1)}) custom-call(f32[2]{0:T(128)S(1)} %pad_maximum_fusion.4.edge_ref, bf16[768,1536]{1,0:T(8,128)(2,1)S(1)} %bitcast.73, bf16[768,1536]{1,0:T(8,128)(2,1)} %collective-permute-done.refs_1_.refs_4_.refs_2_.refs_5_, bf16[768,1536]{1,0:T(8,128)(2,1)S(1)} %bitcast.68, ...), custom_call_target="tpu_custom_call" | custom-call | flops 905969664 | bytes 8388608 | tf_op jit(solution)/shard_map/pallas_call | solution.py:110
  320.4 1.0 copy-done.19
  321.5 34.4 %shard_map.116 = (f32[768,384]{1,0:T(8,128)S(1)}, f32[16,384]{1,0:T(8,128)S(1)}) custom-call(f32[2]{0:T(128)S(1)} %pad_maximum_fusion.5.edge_ref, bf16[768,1536]{1,0:T(8,128)(2,1)S(1)} %bitcast.74, bf16[768,1536]{1,0:T(8,128)(2,1)S(1)} %bitcast.70, bf16[768,1536]{1,0:T(8,128)(2,1)S(1)} %bitcast.71, ...), custom_call_target="tpu_custom_call" | custom-call | flops 905969664 | bytes 8388608 | tf_op jit(solution)/shard_map/pallas_call | solution.py:110
  355.8 1.0 copy-done.17
  356.9 3.5 gather_fusion.1
  360.4 1.5 fusion.7
  361.9 0.4 shard_map.114
  362.3 0.4 shard_map.117
  362.7 1.4 collective-permute-start.4
  364.2 4.9 %collective-permute-start.6 = (f32[16,768]{1,0:T(8,128)S(1)}, f32[16,768]{1,0:T(8,128)S(1)}, u32[]{:S(2)}, u32[]{:S(2)}) collective-permute-start(f32[16,768]{1,0:T(8,128)S(1)} %constant_dynamic-update-slice_fusion), channel_id=1, source_target_pairs={{0,64},{64,128},{128,192},{1,65},{65,129},{129,193},{2,66},{66,130... | collective-permute-start | bytes 147464 | tf_op jit(solution)/shard_map/ppermute | solution.py:355
  369.1 1.1 collective-permute-done.6
  370.2 0.2 shard_map.118
  370.5 1.3 collective-permute-start.7
  371.8 5.2 %collective-permute-start.8 = (f32[80,384]{1,0:T(8,128)S(1)}, f32[80,384]{1,0:T(8,128)S(1)}, u32[]{:S(2)}, u32[]{:S(2)}) collective-permute-start(f32[80,384]{1,0:T(8,128)S(1)} %get-tuple-element.61), channel_id=1, source_target_pairs={{0,64},{64,128},{128,192},{1,65},{65,129},{129,193},{2,66},{66,130... | collective-permute-start | bytes 368648 | tf_op jit(solution)/shard_map/ppermute | solution.py:381
  377.0 0.8 shard_map.120
  377.8 1.4 collective-permute-start.12
  379.2 6.1 %collective-permute-start.13 = (f32[80,384]{1,0:T(8,128)S(1)}, f32[80,384]{1,0:T(8,128)S(1)}, u32[]{:S(2)}, u32[]{:S(2)}) collective-permute-start(f32[80,384]{1,0:T(8,128)S(1)} %get-tuple-element.68), channel_id=1, source_target_pairs={{0,64},{64,128},{128,192},{1,65},{65,129},{129,193},{2,66},{66,130... | collective-permute-start | bytes 368648 | tf_op jit(solution)/shard_map/ppermute | solution.py:381
  385.3 0.6 dynamic_slice.12
  386.7 0.4 collective-permute-done.13.refs_7_
  387.2 1.6 shard_map.121
  388.7 0.7 broadcast_in_dim.43
  389.5 82.1 %all-to-all-start.2 = ((f32[256,1,128]{2,1,0:T(1,128)}), f32[256,1,128]{2,1,0:T(1,128)S(1)}, u32[]{:S(2)}, u32[]{:S(2)}) async-start(f32[256,1,128]{2,1,0:T(1,128)} %broadcast_in_dim.43), calls=%async_computation.2 | async-start | bytes 262144 | tf_op jit(solution)/shard_map/all_to_all | solution.py:404
  471.5 0.6 dynamic_slice.14
  472.8 11.6 %all-to-all-done.2 = f32[256,1,128]{2,1,0:T(1,128)S(1)} async-done(((f32[256,1,128]{2,1,0:T(1,128)}), f32[256,1,128]{2,1,0:T(1,128)S(1)}, u32[]{:S(2)}, u32[]{:S(2)}) %all-to-all-start.2) | async-done | bytes 131104 | tf_op jit(solution)/shard_map/all_to_all | solution.py:404
  484.4 0.1 slice_reduce_fusion
  484.5 0.6 fusion.11
  (76 shorter events, 0.8 us)
Async XLA Ops:
  8.3 7.6 %copy-start = (bf16[1,1,2,12,32,1536]{5,4,3,2,1,0:T(8,128)(2,1)S(1)}, bf16[1,1,2,12,32,1536]{5,4,3,2,1,0:T(8,128)(2,1)}, u32[]{:S(2)}) copy-start(bf16[1,1,2,12,32,1536]{5,4,3,2,1,0:T(8,128)(2,1)} %param.15) | copy-start | bytes 7077892
  8.3 51.1 %all-to-all-start = ((bf16[32,32,1664]{2,1,0:T(8,128)(2,1)}), bf16[32,32,1664]{2,1,0:T(8,128)(2,1)}, u32[]{:S(2)}, u32[]{:S(2)}) async-start(bf16[32,32,1664]{2,1,0:T(8,128)(2,1)} %gather_fusion), calls=%async_computation | async-start | bytes 6815744 | tf_op jit(solution)/shard_map/all_to_all | solution.py:299
  15.9 2.1 copy-start.1
  19.2 5.3 %copy-start.5 = (bf16[1,1,2,12,32,1536]{5,4,3,2,1,0:T(8,128)(2,1)S(1)}, bf16[1,1,2,12,32,1536]{5,4,3,2,1,0:T(8,128)(2,1)}, u32[]{:S(2)}) copy-start(bf16[1,1,2,12,32,1536]{5,4,3,2,1,0:T(8,128)(2,1)} %param.13) | copy-start | bytes 7077892
  20.9 11.1 %copy-start.7 = (bf16[1536,64]{0,1:T(8,128)(2,1)S(1)}, bf16[1536,64]{0,1:T(8,128)(2,1)}, u32[]{:S(2)}) copy-start(bf16[1536,64]{0,1:T(8,128)(2,1)} %param.16) | copy-start | bytes 589828
  20.9 148.8 %collective-permute-start = (bf16[768,1536]{1,0:T(8,128)(2,1)}, bf16[768,1536]{1,0:T(8,128)(2,1)}, u32[]{:S(2)}, u32[]{:S(2)}) collective-permute-start(bf16[768,1536]{1,0:T(8,128)(2,1)} %pad_maximum_fusion.1), channel_id=1, source_target_pairs={{0,4},{4,8},{8,12},{12,16},{16,20},{20,24},{24,28},{28,32},{32,36}... | collective-permute-start | bytes 7077896 | tf_op jit(solution)/shard_map/ppermute | solution.py:286
  26.2 119.6 %collective-permute-start.1 = (bf16[384,1536]{1,0:T(8,128)(2,1)}, bf16[384,1536]{1,0:T(8,128)(2,1)}, u32[]{:S(2)}, u32[]{:S(2)}) collective-permute-start(bf16[384,1536]{1,0:T(8,128)(2,1)} %bitcast.23), channel_id=1, source_target_pairs={{0,64},{64,128},{128,192},{1,65},{65,129},{129,193},{2,66},{66,130... | collective-permute-start | bytes 3538952 | tf_op jit(solution)/shard_map/ppermute | solution.py:305
  60.9 1.7 copy-start.2
  98.0 1.3 copy-start.8
  99.3 257.6 %all-to-all-start.1 = ((bf16[32,32,896]{2,1,0:T(8,128)(2,1)}), bf16[32,32,896]{2,1,0:T(8,128)(2,1)}, u32[]{:S(2)}, u32[]{:S(2)}) async-start(bf16[32,32,896]{2,1,0:T(8,128)(2,1)} %bitcast.81), calls=%async_computation.1 | async-start | bytes 3670016 | tf_op jit(solution)/shard_map/all_to_all | solution.py:335
  113.4 115.0 %collective-permute-start.3 = (bf16[768,1536]{1,0:T(8,128)(2,1)}, bf16[768,1536]{1,0:T(8,128)(2,1)}, u32[]{:S(2)}, u32[]{:S(2)}) collective-permute-start(bf16[768,1536]{1,0:T(8,128)(2,1)} %pad_maximum_fusion.2), channel_id=1, source_target_pairs={{4,0},{8,4},{12,8},{16,12},{20,16},{24,20},{28,24},{32,28},{36,32}... | collective-permute-start | bytes 7077896 | tf_op jit(solution)/shard_map/ppermute | solution.py:287
  115.5 54.2 %collective-permute-start.2 = (bf16[384,1536]{1,0:T(8,128)(2,1)}, bf16[384,1536]{1,0:T(8,128)(2,1)}, u32[]{:S(2)}, u32[]{:S(2)}) collective-permute-start(bf16[384,1536]{1,0:T(8,128)(2,1)} %bitcast.23), channel_id=1, source_target_pairs={{64,0},{128,64},{192,128},{65,1},{129,65},{193,129},{66,2},{130,66... | collective-permute-start | bytes 3538952 | tf_op jit(solution)/shard_map/ppermute | solution.py:306
  116.8 111.7 %collective-permute-start.9 = (bf16[384,1536]{1,0:T(8,128)(2,1)}, bf16[384,1536]{1,0:T(8,128)(2,1)}, u32[]{:S(2)}, u32[]{:S(2)}) collective-permute-start(bf16[384,1536]{1,0:T(8,128)(2,1)} %bitcast.28), channel_id=1, source_target_pairs={{0,64},{64,128},{128,192},{1,65},{65,129},{129,193},{2,66},{66,130... | collective-permute-start | bytes 3538952 | tf_op jit(solution)/shard_map/ppermute | solution.py:305
  145.8 82.6 %collective-permute-start.10 = (bf16[384,1536]{1,0:T(8,128)(2,1)}, bf16[384,1536]{1,0:T(8,128)(2,1)}, u32[]{:S(2)}, u32[]{:S(2)}) collective-permute-start(bf16[384,1536]{1,0:T(8,128)(2,1)} %bitcast.28), channel_id=1, source_target_pairs={{64,0},{128,64},{192,128},{65,1},{129,65},{193,129},{66,2},{130,66... | collective-permute-start | bytes 3538952 | tf_op jit(solution)/shard_map/ppermute | solution.py:306
  169.6 1.7 copy-start.3
  171.3 57.1 %copy-start.4 = (bf16[1,1,2,12,32,1536]{5,4,3,2,1,0:T(8,128)(2,1)S(1)}, bf16[1,1,2,12,32,1536]{5,4,3,2,1,0:T(8,128)(2,1)}, u32[]{:S(2)}) copy-start(bf16[1,1,2,12,32,1536]{5,4,3,2,1,0:T(8,128)(2,1)} %param.14) | copy-start | bytes 7077892
  205.7 1.0 copy-start.13
  206.8 1.1 copy-start.15
  207.9 78.2 %copy-start.6 = (bf16[1,1,2,12,32,1536]{5,4,3,2,1,0:T(8,128)(2,1)S(1)}, bf16[1,1,2,12,32,1536]{5,4,3,2,1,0:T(8,128)(2,1)}, u32[]{:S(2)}) copy-start(bf16[1,1,2,12,32,1536]{5,4,3,2,1,0:T(8,128)(2,1)} %param.13) | copy-start | bytes 7077892
  207.9 149.0 %collective-permute-start.5 = (f32[16,384]{1,0:T(8,128)S(1)}, f32[16,384]{1,0:T(8,128)S(1)}, u32[]{:S(2)}, u32[]{:S(2)}) collective-permute-start(f32[16,384]{1,0:T(8,128)S(1)} %broadcast_select_fusion.5), channel_id=1, source_target_pairs={{0,128},{64,192},{128,0},{192,64},{1,129},{65,193},{129,1},{193,65... | collective-permute-start | bytes 73736 | tf_op jit(solution)/shard_map/ppermute | solution.py:364
  262.8 57.6 %copy-start.9 = (f32[768,384]{1,0:T(8,128)}, f32[768,384]{1,0:T(8,128)S(1)}, u32[]{:S(2)}) copy-start(f32[768,384]{1,0:T(8,128)S(1)} %get-tuple-element.66.pd) | copy-start | bytes 3538948
  262.8 57.6 %copy-start.11 = (f32[768,384]{1,0:T(8,128)}, f32[768,384]{1,0:T(8,128)S(1)}, u32[]{:S(2)}) copy-start(f32[768,384]{1,0:T(8,128)S(1)} %get-tuple-element.63.pu) | copy-start | bytes 3538948
  262.8 101.3 %collective-permute-start.11 = (f32[16,384]{1,0:T(8,128)S(1)}, f32[16,384]{1,0:T(8,128)S(1)}, u32[]{:S(2)}, u32[]{:S(2)}) collective-permute-start(f32[16,384]{1,0:T(8,128)S(1)} %broadcast_select_fusion.4), channel_id=1, source_target_pairs={{0,128},{64,192},{128,0},{192,64},{1,129},{65,193},{129,1},{193,65... | collective-permute-start | bytes 73736 | tf_op jit(solution)/shard_map/ppermute | solution.py:364
  320.4 1.0 copy-start.19
  355.8 1.0 copy-start.17
  356.9 5.0 %copy-start.20 = (f32[768,384]{1,0:T(8,128)S(1)}, f32[768,384]{1,0:T(8,128)}, u32[]{:S(2)}) copy-start(f32[768,384]{1,0:T(8,128)} %copy-done.19) | copy-start | bytes 3538948
  360.4 1.9 copy-start.18
  361.9 8.3 %copy-start.14 = (f32[768,384]{1,0:T(8,128)S(1)}, f32[768,384]{1,0:T(8,128)}, u32[]{:S(2)}) copy-start(f32[768,384]{1,0:T(8,128)} %copy-done.13) | copy-start | bytes 3538948
  361.9 8.3 %copy-start.16 = (f32[768,384]{1,0:T(8,128)S(1)}, f32[768,384]{1,0:T(8,128)}, u32[]{:S(2)}) copy-start(f32[768,384]{1,0:T(8,128)} %copy-done.15) | copy-start | bytes 3538948
  362.3 14.7 %copy-start.10 = (f32[768,384]{1,0:T(8,128)S(1)}, f32[768,384]{1,0:T(8,128)}, u32[]{:S(2)}) copy-start(f32[768,384]{1,0:T(8,128)} %copy-done.9) | copy-start | bytes 3538948
  362.3 14.7 %copy-start.12 = (f32[768,384]{1,0:T(8,128)S(1)}, f32[768,384]{1,0:T(8,128)}, u32[]{:S(2)}) copy-start(f32[768,384]{1,0:T(8,128)} %copy-done.11) | copy-start | bytes 3538948
  362.7 6.4 %collective-permute-start.4 = (f32[16,768]{1,0:T(8,128)S(1)}, f32[16,768]{1,0:T(8,128)S(1)}, u32[]{:S(2)}, u32[]{:S(2)}) collective-permute-start(f32[16,768]{1,0:T(8,128)S(1)} %constant_dynamic-update-slice_fusion), channel_id=1, source_target_pairs={{64,0},{128,64},{192,128},{65,1},{129,65},{193,129},{66,2},{130,66... | collective-permute-start | bytes 147464 | tf_op jit(solution)/shard_map/ppermute | solution.py:356
  364.2 6.1 %collective-permute-start.6 = (f32[16,768]{1,0:T(8,128)S(1)}, f32[16,768]{1,0:T(8,128)S(1)}, u32[]{:S(2)}, u32[]{:S(2)}) collective-permute-start(f32[16,768]{1,0:T(8,128)S(1)} %constant_dynamic-update-slice_fusion), channel_id=1, source_target_pairs={{0,64},{64,128},{128,192},{1,65},{65,129},{129,193},{2,66},{66,130... | collective-permute-start | bytes 147464 | tf_op jit(solution)/shard_map/ppermute | solution.py:355
  370.2 15.1 %copy-start.22 = (s32[2]{0:T(128)S(1)}, s32[2]{0:T(128)}, u32[]{:S(2)}) copy-start(s32[2]{0:T(128)} %param.20) | copy-start | bytes 28
  370.2 16.9 %copy-start.21 = (bf16[1,1,2,12,32,64]{5,4,3,2,1,0:T(8,128)(2,1)S(1)}, bf16[1,1,2,12,32,64]{5,4,3,2,1,0:T(8,128)(2,1)}, u32[]{:S(2)}) copy-start(bf16[1,1,2,12,32,64]{5,4,3,2,1,0:T(8,128)(2,1)} %param.17) | copy-start | bytes 294916
  370.5 16.3 %collective-permute-start.7 = (f32[80,384]{1,0:T(8,128)S(1)}, f32[80,384]{1,0:T(8,128)S(1)}, u32[]{:S(2)}, u32[]{:S(2)}) collective-permute-start(f32[80,384]{1,0:T(8,128)S(1)} %get-tuple-element.60), channel_id=1, source_target_pairs={{64,0},{128,64},{192,128},{65,1},{129,65},{193,129},{66,2},{130,66... | collective-permute-start | bytes 368648 | tf_op jit(solution)/shard_map/ppermute | solution.py:382
  371.8 15.0 %collective-permute-start.8 = (f32[80,384]{1,0:T(8,128)S(1)}, f32[80,384]{1,0:T(8,128)S(1)}, u32[]{:S(2)}, u32[]{:S(2)}) collective-permute-start(f32[80,384]{1,0:T(8,128)S(1)} %get-tuple-element.61), channel_id=1, source_target_pairs={{0,64},{64,128},{128,192},{1,65},{65,129},{129,193},{2,66},{66,130... | collective-permute-start | bytes 368648 | tf_op jit(solution)/shard_map/ppermute | solution.py:381
  377.8 93.8 %copy-start.23 = (s32[2]{0:T(128)S(1)}, s32[2]{0:T(128)}, u32[]{:S(2)}) copy-start(s32[2]{0:T(128)} %param.21) | copy-start | bytes 28
  377.8 9.0 %collective-permute-start.12 = (f32[80,384]{1,0:T(8,128)}, f32[80,384]{1,0:T(8,128)S(1)}, u32[]{:S(2)}, u32[]{:S(2)}) collective-permute-start(f32[80,384]{1,0:T(8,128)} %get-tuple-element.67), channel_id=1, source_target_pairs={{64,0},{128,64},{192,128},{65,1},{129,65},{193,129},{66,2},{130,66... | collective-permute-start | bytes 368648 | tf_op jit(solution)/shard_map/ppermute | solution.py:382
  379.2 8.0 %collective-permute-start.13 = (f32[80,384]{1,0:T(8,128)S(1)}, f32[80,384]{1,0:T(8,128)S(1)}, u32[]{:S(2)}, u32[]{:S(2)}) collective-permute-start(f32[80,384]{1,0:T(8,128)S(1)} %get-tuple-element.68), channel_id=1, source_target_pairs={{0,64},{64,128},{128,192},{1,65},{65,129},{129,193},{2,66},{66,130... | collective-permute-start | bytes 368648 | tf_op jit(solution)/shard_map/ppermute | solution.py:381
  389.5 94.9 %all-to-all-start.2 = ((f32[256,1,128]{2,1,0:T(1,128)}), f32[256,1,128]{2,1,0:T(1,128)S(1)}, u32[]{:S(2)}, u32[]{:S(2)}) async-start(f32[256,1,128]{2,1,0:T(1,128)} %broadcast_in_dim.43), calls=%async_computation.2 | async-start | bytes 262144 | tf_op jit(solution)/shard_map/all_to_all | solution.py:404

commit v2 on v1

v2 whole, which is shorter than its diff:
```python
import functools
import math

import jax
import jax.numpy as jnp
from jax import lax
from jax.experimental import pallas as pl
from jax.experimental.pallas import tpu as pltpu
from jax.sharding import PartitionSpec as P

HEADS = 12
HD = 128
PATCH = 64
TILE = 32
RATERS = 100
SLOTS = 2
NEG = -1e30
FACTOR = math.log2(math.e) / math.sqrt(HD)
LSE_ROWS = 16
MIB = 1 << 20

NT = (((1,), (1,)), ((), ()))
NN = (((1,), (0,)), ((), ()))


def dot(a, b, dims):
    return lax.dot_general(a, b, dims, preferred_element_type=jnp.float32)


def lane_iota(shape):
    return lax.broadcasted_iota(jnp.int32, shape, 1)


def window_kernel(groups, columns, edge_ref, *refs):
    q_refs = refs[:groups]
    k_refs = refs[groups : groups + 3]
    v_refs = refs[groups + 3 : groups + 6]
    wt_ref = refs[groups + 6]
    p_refs = refs[-3 * groups : -2 * groups]
    l_refs = refs[-2 * groups : -groups]
    acc_refs = refs[-groups:]
    step = pl.program_id(0)
    span = 4 * TILE
    rows = 2 * TILE * groups

    @pl.when(step == 0)
    def _():
        for acc in acc_refs:
            acc[...] = jnp.zeros_like(acc)

    key_tile = lane_iota((rows, span)) // TILE
    query_tile = (lax.broadcasted_iota(jnp.int32, (rows, span), 0) // TILE) % 2
    biases = {}
    pairs = columns // 2
    for pair in range(pairs):
        first = min(max(2 * pair - 1, 0), columns - 4)
        shift = 2 * pair - first
        if shift not in biases:
            near = jnp.abs(key_tile - query_tile - shift) <= 1
            base = jnp.where(near, 0.0, NEG)
            biases[shift] = (base + edge_ref[0], base, base + edge_ref[1])
    for half in range(2):
        lanes = slice(half * HD, half * HD + HD)
        wt = wt_ref[:, lanes]
        scores = []
        for pair in range(pairs):
            first = min(max(2 * pair - 1, 0), columns - 4)
            bias = biases[2 * pair - first]
            tokens = slice(2 * TILE * pair, 2 * TILE * (pair + 1))
            keys = slice(TILE * first, TILE * (first + 4))
            queries = [q[tokens, lanes] for q in q_refs]
            query = queries[0] if groups == 1 else jnp.concatenate(queries, axis=0)
            raw = dot(query, jnp.concatenate([k[keys, lanes] for k in k_refs], axis=0), NT)
            scores.append([raw[:, span * i : span * (i + 1)] + bias[i] for i in range(3)])
        tops = [jnp.max(functools.reduce(jnp.maximum, s), axis=1, keepdims=True) for s in scores]
        weights = [[jnp.exp2((x - top) * FACTOR) for x in s] for s, top in zip(scores, tops)]
        totals = [jnp.sum(sum(w), axis=1, keepdims=True) for w in weights]
        mixed = []
        for pair, weight in enumerate(weights):
            first = min(max(2 * pair - 1, 0), columns - 4)
            keys = slice(TILE * first, TILE * (first + 4))
            rounded = jnp.concatenate([w.astype(jnp.bfloat16) for w in weight], axis=1)
            mixed.append(dot(rounded, jnp.concatenate([v[keys, lanes] for v in v_refs], axis=0), NN))
        mixed = [(m * (1.0 / total)).astype(jnp.bfloat16) for m, total in zip(mixed, totals)]
        projected = [dot(wt, m, NT) for m in mixed]
        for pair in range(pairs):
            tokens = slice(2 * TILE * pair, 2 * TILE * (pair + 1))
            lse = tops[pair] * FACTOR + jnp.log2(totals[pair])
            for g in range(groups):
                part = slice(2 * TILE * g, 2 * TILE * (g + 1))
                p_refs[g][PATCH * half : PATCH * (half + 1), tokens] = projected[pair][:, part]
                held = acc_refs[g][tokens, :]
                mark = lane_iota(held.shape) == 2 * step + half
                acc_refs[g][tokens, :] = jnp.where(mark, lse[part], held)

    @pl.when(step == pl.num_programs(0) - 1)
    def _():
        for g in range(groups):
            l_refs[g][...] = jnp.transpose(acc_refs[g][...])[:LSE_ROWS, :]


def window_attention(edge, queries, query_block, keys, values, wt, columns, after=()):
    groups = len(queries)
    tokens = columns * TILE
    inner = wt.shape[1]
    steps = inner // (2 * HD)

    def block(row):
        return pl.BlockSpec((tokens, 2 * HD), lambda i, row=row: (row, i))

    specs = [pl.BlockSpec(memory_space=pltpu.SMEM)]
    specs += [block(query_block) for _ in queries]
    specs += [block(row) for _, row in keys] + [block(row) for _, row in values]
    specs += [pl.BlockSpec((PATCH, 2 * HD), lambda i: (0, i))]
    specs += [pl.BlockSpec(memory_space=pl.ANY)] * len(after)
    operands = [edge, *queries, *[a for a, _ in keys], *[a for a, _ in values], wt, *after]
    heads = inner // HD
    flops = 2 * groups * tokens * heads * 12 * TILE * HD * 2
    out = pl.pallas_call(
        functools.partial(window_kernel, groups, columns),
        grid=(steps,),
        in_specs=specs,
        out_specs=[pl.BlockSpec((2 * PATCH, tokens), lambda i: (i, 0))] * groups
        + [pl.BlockSpec((LSE_ROWS, tokens), lambda i: (0, 0))] * groups,
        out_shape=[jax.ShapeDtypeStruct((heads * PATCH, tokens), jnp.float32)] * groups
        + [jax.ShapeDtypeStruct((LSE_ROWS, tokens), jnp.float32)] * groups,
        scratch_shapes=[pltpu.VMEM((tokens, 128), jnp.float32)] * groups,
        compiler_params=pltpu.CompilerParams(vmem_limit_bytes=56 * MIB),
        cost_estimate=pl.CostEstimate(flops=1, bytes_accessed=1, transcendentals=0),
    )(*operands)
    return out[:groups], out[groups:]


def far_kernel(per_step, heads, index_ref, query_ref, key_ref, value_ref, wbd_ref, out_ref, lse_ref):
    step = pl.program_id(0)
    upper = lax.broadcasted_iota(jnp.int32, (2 * TILE, 2 * HD), 0) // TILE
    right = lane_iota((2 * TILE, 2 * HD)) // HD
    own_half = upper == right
    lane = lane_iota((TILE, 128))
    slots = range(per_step)
    pairs = range(heads // 2)
    starts = [pl.multiple_of(index_ref[step * per_step + s] * TILE, TILE) for s in slots]
    scores = []
    for s in slots:
        parts = []
        for j in pairs:
            lanes = slice(2 * j * HD, 2 * (j + 1) * HD)
            query = query_ref[s * TILE : (s + 1) * TILE, lanes]
            stacked = jnp.concatenate([query, query], axis=0)
            stacked = jnp.where(own_half, stacked, jnp.zeros_like(stacked))
            parts.append(dot(stacked, key_ref[pl.ds(starts[s], TILE), lanes], NT))
        scores.append(jnp.concatenate(parts, axis=0))
    tops = [jnp.max(x, axis=1, keepdims=True) for x in scores]
    weights = [jnp.exp2((x - top) * FACTOR) for x, top in zip(scores, tops)]
    totals = [jnp.sum(w, axis=1, keepdims=True) for w in weights]
    rounded = [w.astype(jnp.bfloat16) for w in weights]
    inverse = [1.0 / total for total in totals]
    lses = [top * FACTOR + jnp.log2(total) for top, total in zip(tops, totals)]
    mixed = []
    for s in slots:
        for j in pairs:
            lanes = slice(2 * j * HD, 2 * (j + 1) * HD)
            pair = slice(2 * j * TILE, 2 * (j + 1) * TILE)
            both = dot(rounded[s][pair], value_ref[pl.ds(starts[s], TILE), lanes], NN) * inverse[s][pair]
            mixed.append(jnp.concatenate([both[:TILE, :HD], both[TILE:, HD:]], axis=1).astype(jnp.bfloat16))
    for j in pairs:
        lanes = slice(2 * j * PATCH, 2 * (j + 1) * PATCH)
        stacked = jnp.concatenate([mixed[s * (heads // 2) + j] for s in slots], axis=0)
        out_ref[:, lanes] = dot(stacked, wbd_ref[:, lanes], NN).astype(jnp.bfloat16)
    sums = []
    for s in slots:
        column = jnp.zeros((TILE, 128), jnp.float32)
        for head in range(heads):
            column = jnp.where(lane == head, lses[s][head * TILE : (head + 1) * TILE], column)
        sums.append(column)
    turned = jnp.transpose(jnp.concatenate(sums, axis=0))[:LSE_ROWS]
    for o in range(per_step // SLOTS):
        lse_ref[o] = turned[:, o * SLOTS * TILE : (o + 1) * SLOTS * TILE]


def far_attention(index, received, key, value, wbd):
    count = index.shape[0]
    inner = key.shape[1]
    heads = inner // HD
    per_step = 4
    width = heads * PATCH
    return pl.pallas_call(
        functools.partial(far_kernel, per_step, heads),
        grid_spec=pltpu.PrefetchScalarGridSpec(
            num_scalar_prefetch=1,
            grid=(count // per_step,),
            in_specs=[
                pl.BlockSpec((per_step * TILE, inner), lambda i, _: (i, 0)),
                pl.BlockSpec(key.shape, lambda i, _: (0, 0)),
                pl.BlockSpec(value.shape, lambda i, _: (0, 0)),
                pl.BlockSpec(wbd.shape, lambda i, _: (0, 0)),
            ],
            out_specs=[
                pl.BlockSpec((per_step * TILE, width), lambda i, _: (i, 0)),
                pl.BlockSpec((per_step // SLOTS, LSE_ROWS, SLOTS * TILE), lambda i, _: (i, 0, 0)),
            ],
        ),
        out_shape=[
            jax.ShapeDtypeStruct((count * TILE, width), jnp.bfloat16),
            jax.ShapeDtypeStruct((count // SLOTS, LSE_ROWS, SLOTS * TILE), jnp.float32),
        ],
        compiler_params=pltpu.CompilerParams(vmem_limit_bytes=56 * MIB),
        cost_estimate=pl.CostEstimate(flops=1, bytes_accessed=1, transcendentals=0),
    )(index, received, key, value, wbd)


def log_sum(*parts):
    top = functools.reduce(jnp.maximum, parts)
    return top + jnp.log2(sum(jnp.exp2(p - top) for p in parts))


def weighted_sum(weights, projected, heads):
    return sum(weights[h : h + 1, :] * projected[PATCH * h : PATCH * (h + 1), :] for h in range(heads))


def base_kernel(row_tiles, slot_ref, far_ref, *refs):
    own_refs = refs[:-2]
    far_out, base_out = refs[-2:]
    for r, own_ref in enumerate(own_refs):
        for c in range(row_tiles):
            slot = slot_ref[r * row_tiles + c]
            held = far_ref[slot // SLOTS]
            far = jnp.where(slot % SLOTS == 0, held[:, :TILE], held[:, TILE:])
            lanes = slice((r * row_tiles + c) * TILE, (r * row_tiles + c + 1) * TILE)
            far_out[:, lanes] = far
            base_out[:, lanes] = log_sum(own_ref[:, c * TILE : (c + 1) * TILE], far)


def tie(value, after):
    def kernel(*refs):
        pass

    anywhere = pl.BlockSpec(memory_space=pl.ANY)
    return pl.pallas_call(
        kernel,
        in_specs=[anywhere] * (1 + len(after)),
        out_specs=anywhere,
        out_shape=jax.ShapeDtypeStruct(value.shape, value.dtype),
        input_output_aliases={0: 0},
    )(value, *after)


def merge_kernel(heads, chunks, base, far_l, far_p, *refs):
    out = refs[-1]
    for c in range(chunks):
        p, l = refs[2 * c : 2 * c + 2]
        tokens = l.shape[1]
        cols = slice(c * tokens, (c + 1) * tokens)
        far = jnp.transpose(far_p[cols, :].astype(jnp.float32))
        own_weight = jnp.exp2(l[...] - base[:, cols])
        far_weight = jnp.exp2(far_l[:, cols] - base[:, cols])
        for h in range(heads):
            rows = slice(PATCH * h, PATCH * (h + 1))
            out[rows, cols] = own_weight[h : h + 1, :] * p[rows, :] + far_weight[h : h + 1, :] * far[rows, :]


def whole(kernel, out_shape, cost, *operands, smem=0):
    specs = [pl.BlockSpec(memory_space=pltpu.SMEM)] * smem
    specs += [pl.BlockSpec(memory_space=pltpu.VMEM)] * (len(operands) - smem)
    return pl.pallas_call(
        kernel,
        in_specs=specs,
        out_specs=jax.tree.map(lambda _: pl.BlockSpec(memory_space=pltpu.VMEM), out_shape),
        out_shape=out_shape,
        compiler_params=pltpu.CompilerParams(vmem_limit_bytes=56 * MIB),
        cost_estimate=pl.CostEstimate(flops=1, bytes_accessed=1, transcendentals=0),
    )(*operands)


def scale_kernel(heads, chunks, flags, other, *refs):
    up_out, down_out = refs[-2:]
    for side, out in enumerate((up_out, down_out)):
        base = refs[2 * chunks * 2 + side]
        for c in range(chunks):
            p, l = refs[2 * (chunks * side + c) : 2 * (chunks * side + c) + 2]
            tokens = l.shape[1]
            cols = slice(c * tokens, (c + 1) * tokens)
            lse = l[...]
            weights = jnp.exp2(lse - log_sum(lse, base[:, cols], other[:, cols] + flags[side]))
            out[:PATCH, cols] = weighted_sum(weights, p, heads)
            out[PATCH:, cols] = lse


def final_kernel(heads, scalars, p, l, above, below, target, error_out, sum_out):
    lse = l[...]
    sums = log_sum(lse, above[PATCH:, :] + scalars[1], below[PATCH:, :] + scalars[2])
    out = weighted_sum(jnp.exp2(lse - sums), p, heads) + above[:PATCH, :] + below[:PATCH, :]
    error = jnp.transpose(out) - target[...].astype(jnp.float32)
    error_out[...] = (scalars[0] * error).astype(jnp.bfloat16)
    sum_out[...] = jnp.broadcast_to(jnp.sum(error * error, keepdims=True), sum_out.shape)


def body(
    query_tokens,
    key_tokens,
    value_tokens,
    head_weight,
    target_noise,
    far_owner,
    far_offset,
    timestep,
    labels,
):
    _, _, rows_dev, columns, tile_len, inner = query_tokens.shape
    tiles = rows_dev * columns
    heads = inner // HD
    row_tokens = columns * tile_len
    tokens = rows_dev * row_tokens
    pairs_n, frames_n, height_n = (lax.axis_size(a) for a in ("pair", "tm", "height"))
    frame = lax.axis_index("tm")
    height = lax.axis_index("height")

    up_frames = [(i, i + 1) for i in range(frames_n - 1)]
    down_frames = [(i + 1, i) for i in range(frames_n - 1)]
    up_rows = [(i, i + 1) for i in range(height_n - 1)]
    down_rows = [(i + 1, i) for i in range(height_n - 1)]

    query = query_tokens.reshape(tokens, inner)
    key = key_tokens.reshape(tokens, inner)
    value = value_tokens.reshape(tokens, inner)

    last = jnp.concatenate([key[row_tokens:], value[row_tokens:]], axis=0)
    initial = jnp.concatenate([key[:row_tokens], value[:row_tokens]], axis=0)
    halo_before = lax.ppermute(last, "height", up_rows)
    halo_after = lax.ppermute(initial, "height", down_rows)

    owners = far_owner.reshape(tiles)
    offsets = far_offset.reshape(tiles)
    ids = jnp.arange(tiles)
    earlier = (ids[:, None] > ids[None, :]) & (owners[:, None] == owners[None, :])
    slot = owners * SLOTS + jnp.sum(earlier.astype(jnp.int32), axis=1)
    slot_count = height_n * SLOTS
    chosen = slot[:, None] == jnp.arange(slot_count)[None, :]
    source = jnp.sum(jnp.where(chosen, ids[:, None], 0), axis=0)
    marks = jnp.broadcast_to(offsets.astype(jnp.bfloat16)[:, None, None], (tiles, tile_len, 128))
    payload = jnp.concatenate([query.reshape(tiles, tile_len, inner), marks], axis=2)[source]
    received = lax.all_to_all(payload, "height", split_axis=0, concat_axis=0, tiled=True)

    from_below = lax.ppermute(query, "tm", up_frames)
    from_above = lax.ppermute(query, "tm", down_frames)

    wt = jnp.transpose(head_weight)
    paired = head_weight.reshape(heads // 2, 2, HD, PATCH)
    wbd = jnp.zeros((2, HD, heads // 2, 2, PATCH), head_weight.dtype)
    for half in range(2):
        wbd = wbd.at[half, :, :, half, :].set(jnp.transpose(paired[:, half], (1, 0, 2)))
    wbd = wbd.reshape(2 * HD, heads * PATCH)

    first_edge = jnp.where(height == 0, NEG, 0.0).astype(jnp.float32)
    last_edge = jnp.where(height == height_n - 1, NEG, 0.0).astype(jnp.float32)
    zero = jnp.zeros((), jnp.float32)

    def attend(r, queries, block, first=()):
        before = (halo_before, 0, halo_before, 1) if r == 0 else (key, r - 1, value, r - 1)
        after = (halo_after, 0, halo_after, 1) if r == rows_dev - 1 else (key, r + 1, value, r + 1)
        edge = jnp.stack([first_edge if r == 0 else zero, last_edge if r == rows_dev - 1 else zero])
        keys = [before[:2], (key, r), after[:2]]
        values = [before[2:], (value, r), after[2:]]
        return window_attention(edge, queries, block, keys, values, wt, columns, first)

    own, ups, downs = [], [], []
    for r in range(rows_dev):
        ps, ls = attend(r, [query, from_below, from_above], r)
        for held, p, l in zip((own, downs, ups), ps, ls):
            held.append((p, l))

    index = received[:, 0, inner].astype(jnp.int32)
    received = received.reshape(slot_count * tile_len, inner + 128)
    far_p, far_l = far_attention(index, received, key, value, wbd)
    far_l = lax.all_to_all(far_l, "height", split_axis=0, concat_axis=0, tiled=True)
    flat = jax.ShapeDtypeStruct((LSE_ROWS, tokens), jnp.float32)
    far_l, base_lse = whole(
        functools.partial(base_kernel, columns), [flat, flat], 0, slot, far_l, *[l for _, l in own], smem=1
    )
    base_below = lax.ppermute(base_lse, "tm", up_frames)
    base_above = lax.ppermute(base_lse, "tm", down_frames)

    swap = [(i, i + 2) for i in range(frames_n - 2)] + [(i + 2, i) for i in range(frames_n - 2)]
    low = frame < frames_n - 2
    width = far_p.shape[1]
    far_p = tie(far_p, [from_below, from_above])
    far_p = lax.all_to_all(
        far_p.reshape(slot_count, tile_len, width), "height", split_axis=0, concat_axis=0, tiled=True
    )
    base_p = whole(
        functools.partial(merge_kernel, heads, rows_dev),
        jax.ShapeDtypeStruct((width, tokens), jnp.float32),
        0,
        base_lse,
        far_l,
        far_p[slot].reshape(tokens, width),
        *[a for part in own for a in part],
    )
    lse_u = jnp.concatenate([l for _, l in ups], axis=1)
    lse_d = jnp.concatenate([l for _, l in downs], axis=1)
    other = lax.ppermute(jnp.where(low, lse_u, lse_d), "tm", swap)
    flags = jnp.where(low, jnp.array([0.0, NEG]), jnp.array([NEG, 0.0])).astype(jnp.float32)
    shape = jax.ShapeDtypeStruct((PATCH + LSE_ROWS, tokens), jnp.float32)
    to_above, to_below = whole(
        functools.partial(scale_kernel, heads, rows_dev),
        [shape, shape],
        0,
        flags,
        other,
        *[a for part in ups + downs for a in part],
        base_above,
        base_below,
        smem=1,
    )
    got_below = lax.ppermute(to_above, "tm", up_frames)
    got_above = lax.ppermute(to_below, "tm", down_frames)

    pair = lax.axis_index("pair")
    pair_slot = pair // 2
    step_weight = 0.5 + (timestep[pair_slot].astype(jnp.float32) + 1.0) / 1000.0
    no_above = jnp.where(frame == frames_n - 1, NEG, 0.0).astype(jnp.float32)
    no_below = jnp.where(frame == 0, NEG, 0.0).astype(jnp.float32)
    scalars = jnp.stack([jnp.sqrt(step_weight), no_above, no_below])
    error, squares = whole(
        functools.partial(final_kernel, heads),
        [jax.ShapeDtypeStruct((tokens, PATCH), jnp.bfloat16), jax.ShapeDtypeStruct((pairs_n * frames_n * height_n, 128), jnp.float32)],
        1 << 22,
        scalars,
        base_p,
        base_lse,
        got_above,
        got_below,
        target_noise.reshape(tokens, PATCH),
        smem=1,
    )
    weighted_error = error.reshape(target_noise.shape)

    gathered = lax.all_to_all(squares, ("pair", "tm", "height"), split_axis=0, concat_axis=0, tiled=True)
    sums = jnp.sum(gathered.reshape(pairs_n, frames_n * height_n, 128)[:, :, 0], axis=1)
    count = frames_n * height_n * tokens * PATCH
    mine = sums[pair]
    partner = sums[pair ^ 1]
    clip_loss = step_weight * mine / count
    partner_loss = step_weight * partner / count
    difference = jnp.where(pair % 2 == 1, clip_loss - partner_loss, partner_loss - clip_loss)
    strength = 2.0 * labels[pair_slot].astype(jnp.float32) / RATERS - 1.0
    return (weighted_error, clip_loss.reshape(1), (strength * difference).reshape(1))


def solution(mesh):
    placed = (
        P("pair", "tm", "height", None, None, None),
        P("pair", "tm", "height", None, None, None),
        P("pair", "tm", "height", None, None, None),
        P(),
        P("pair", "tm", "height", None, None, None),
        P("pair", "tm", "height", None, None),
        P("pair", "tm", "height", None, None),
        P(),
        P(),
    )
    return jax.shard_map(
        body,
        mesh=mesh,
        in_specs=placed,
        out_specs=(P("pair", "tm", "height", None, None, None), P("pair"), P("pair")),
        check_vma=False,
    )
```

time: 490 us -> 297 us (0.61)
  Pallas kernels: 176 us -> 54.7 us
  starting transfers between devices: 208 us -> 112 us
  waiting for transfers between devices: 58.1 us -> 93 us
  local copies, waits for them, and re-layouts: 29.6 us -> 17 us
    pallas_call x4 -> x2, Pallas kernels: 137 us -> 30.9 us  [window_attention(): pl.pallas_call(functools.partial(window_kernel, groups, columns), grid=(s...]
    all_to_all x1, waiting for transfers between devices: 22.7 us -> 71.6 us  [body(): lax.all_to_all(payload, 'height', split_axis=0, concat_axis=0, tiled=True)]
    ppermute x6 -> x3, starting transfers between devices: 81.2 us -> 32.8 us  [the longest x1 24.5 us: body(): other = lax.ppermute(jnp.where(low, lse_u, lse_d), 'tm', swap)]
    all_to_all x2 -> x3, starting transfers between devices: 93 us -> 57.2 us  [the longest x1 27.2 us: body(): lax.all_to_all(far_p.reshape(slot_count, tile_len, width), 'height', spli...]
    pallas_call x1, Pallas kernels: 35.4 us -> 11.5 us  [far_attention(): pl.pallas_call(functools.partial(far_kernel, per_step, heads), grid_spec=...]
    ppermute x6 -> x3, waiting for transfers between devices: 22.3 us -> 0.01 us  [the longest x1 0.01 us: body(): from_above = lax.ppermute(query, 'tm', down_frames)]
    pallas_call x5 -> x4, Pallas kernels: 3.29 us -> 12.3 us  [whole(): pl.pallas_call(kernel, in_specs=specs, out_specs=jax.tree.map(lambda _: p...]
    ppermute x2 -> x1, starting transfers between devices: 11.3 us -> 5.08 us  [body(): got_below = lax.ppermute(to_above, 'tm', up_frames)]
  transfers between devices with their start and end apart: 17 -> 13, of which waited for: 5 -> 4; matrix products, arithmetic and copies ran while one was open for 4% -> 6% of each run, Pallas kernels for 36% -> 17%
where the time goes in v2:
time: 297 us; the launch traced here: 296 us
  starting transfers between devices  112 us (38%)
  waiting for transfers between devices  93 us (31%)
  Pallas kernels  54.7 us (18%)
  local copies, waits for them, and re-layouts  17 us (6%)
  other arithmetic  13.5 us (5%)
  between operations  5.99 us (2%)
    all_to_all x1, waiting for transfers between devices, body(): lax.all_to_all(payload, 'height', split_axis=0, concat_axis=0, tiled=True)  71.6 us
    pallas_call x2, Pallas kernels, window_attention(): pl.pallas_call(functools.partial(window_kernel, groups, columns), grid=(s...  30.9 us
    all_to_all x1, starting transfers between devices, body(): lax.all_to_all(far_p.reshape(slot_count, tile_len, width), 'height', spli...  27.2 us
    ppermute x1, starting transfers between devices, body(): other = lax.ppermute(jnp.where(low, lse_u, lse_d), 'tm', swap)  24.5 us
    all_to_all x1, starting transfers between devices, body(): lax.all_to_all(squares, ('pair', 'tm', 'height'), split_axis=0, concat_ax...  17 us
    all_to_all x1, starting transfers between devices, body(): lax.all_to_all(far_l, 'height', split_axis=0, concat_axis=0, tiled=True)  13.1 us
    pallas_call x4, Pallas kernels, whole(): pl.pallas_call(kernel, in_specs=specs, out_specs=jax.tree.map(lambda _: p...  12.3 us
    all_to_all x1, waiting for transfers between devices, body(): lax.all_to_all(squares, ('pair', 'tm', 'height'), split_axis=0, concat_ax...  11.6 us
  transfers between devices with their start and end apart: 13, of which 4 were waited for; matrix products, arithmetic and copies ran while one was open for 6% of the time, Pallas kernels for 17%

profile of v2, /device:TPU:1, one launch (start us, length us, event | category | flops | bytes accessed | tf_op | source)
XLA Modules:
  0.0 296.4 jit_solution(2040014514541803701)
XLA Ops:
  0.6 0.7 convert_reduce_fusion.1
  1.3 0.1 convert_element_type.29
  1.4 0.5 broadcast.131
  1.9 1.3 multiply_reduce_fusion
  3.3 0.1 reshape.212
  3.4 0.2 convert_reduce_fusion
  3.6 0.1 select_reduce_fusion
  3.7 0.1 broadcast_in_dim.14
  3.8 1.9 pad_maximum_fusion
  5.7 2.7 gather_fusion
  8.3 7.6 %all-to-all-start = ((bf16[32,32,1664]{2,1,0:T(8,128)(2,1)}), bf16[32,32,1664]{2,1,0:T(8,128)(2,1)}, u32[]{:S(2)}, u32[]{:S(2)}) async-start(bf16[32,32,1664]{2,1,0:T(8,128)(2,1)} %gather_fusion), calls=%async_computation | async-start | bytes 6815744 | tf_op jit(solution)/shard_map/all_to_all | solution.py:342
  15.9 1.4 collective-permute-start.1
  17.4 6.9 %collective-permute-start = (bf16[768,1536]{1,0:T(8,128)(2,1)}, bf16[768,1536]{1,0:T(8,128)(2,1)}, u32[]{:S(2)}, u32[]{:S(2)}) collective-permute-start(bf16[768,1536]{1,0:T(8,128)(2,1)} %bitcast.64), channel_id=1, source_target_pairs={{0,64},{64,128},{128,192},{1,65},{65,129},{129,193},{2,66},{66,130... | collective-permute-start | bytes 7077896 | tf_op jit(solution)/shard_map/ppermute | solution.py:344
  24.2 0.2 fusion.4
  24.5 0.2 fusion.5
  24.7 1.7 pad_maximum_fusion.1
  26.4 3.8 %collective-permute-start.2 = (bf16[768,1536]{1,0:T(8,128)(2,1)}, bf16[768,1536]{1,0:T(8,128)(2,1)S(1)}, u32[]{:S(2)}, u32[]{:S(2)}) collective-permute-start(bf16[768,1536]{1,0:T(8,128)(2,1)} %pad_maximum_fusion.1), channel_id=1, source_target_pairs={{0,4},{4,8},{8,12},{12,16},{16,20},{20,24},{24,28},{28,32},{32,36}... | collective-permute-start | bytes 7077896 | tf_op jit(solution)/shard_map/ppermute | solution.py:329
  30.2 1.6 pad_maximum_fusion.2
  31.8 1.9 collective-permute-start.3
  33.7 0.1 reshape.216
  33.8 0.3 fusion.6
  34.1 0.1 scatter.6
  34.2 0.8 copy.38
  34.9 1.2 reshape.256.wbd_ref
  36.1 71.6 %all-to-all-done = bf16[32,32,1664]{2,1,0:T(8,128)(2,1)} async-done(((bf16[32,32,1664]{2,1,0:T(8,128)(2,1)}), bf16[32,32,1664]{2,1,0:T(8,128)(2,1)}, u32[]{:S(2)}, u32[]{:S(2)}) %all-to-all-start) | async-done | bytes 3407904 | tf_op jit(solution)/shard_map/all_to_all | solution.py:342
  107.7 2.0 fusion.index_ref
  109.8 11.5 %shard_map.130 = (bf16[1024,768]{1,0:T(8,128)(2,1)}, f32[16,16,64]{2,1,0:T(8,128)}) custom-call(s32[32]{0:T(128)} %fusion.index_ref, bf16[1024,1664]{1,0:T(8,128)(2,1)} %bitcast.5.query_ref, bf16[768,1536]{1,0:T(8,128)(2,1)} %bitcast.52, bf16[768,1536]{1,0:T(8,128)(2,1)} %bitcast.57, bf16[256,768]{1,0:T(8,128)(2,1)} %reshape.256.wbd_ref), custom_call_target="tpu_custom_call" | custom-call | flops 1 | bytes 1 | tf_op jit(solution)/shard_map/pallas_call | solution.py:187
  121.3 1.7 reshape.273
  122.9 13.1 %all-to-all-start.1 = ((f32[16,1,1024]{2,1,0:T(1,128)}), f32[16,1,1024]{2,1,0:T(1,128)S(1)}, u32[]{:S(2)}, u32[]{:S(2)}) async-start(f32[16,1,1024]{2,1,0:T(1,128)} %reshape.273), calls=%async_computation.1 | async-start | bytes 131072 | tf_op jit(solution)/shard_map/all_to_all | solution.py:375
  136.1 5.8 %all-to-all-done.1 = f32[16,1,1024]{2,1,0:T(1,128)S(1)} async-done(((f32[16,1,1024]{2,1,0:T(1,128)}), f32[16,1,1024]{2,1,0:T(1,128)S(1)}, u32[]{:S(2)}, u32[]{:S(2)}) %all-to-all-start.1) | async-done | bytes 65568 | tf_op jit(solution)/shard_map/all_to_all | solution.py:375
  141.9 27.2 %all-to-all-start.2 = ((bf16[32,32,768]{2,1,0:T(8,128)(2,1)}), bf16[32,32,768]{2,1,0:T(8,128)(2,1)}, u32[]{:S(2)}, u32[]{:S(2)}) async-start(bf16[32,32,768]{2,1,0:T(8,128)(2,1)} %bitcast.67), calls=%async_computation.2 | async-start | bytes 3145728 | tf_op jit(solution)/shard_map/all_to_all | solution.py:387
  169.0 0.6 pad_maximum_fusion.4.edge_ref
  169.6 0.6 pad_maximum_fusion.5.edge_ref
  170.2 15.5 %shard_map.132 = (f32[768,384]{1,0:T(8,128)}, f32[768,384]{1,0:T(8,128)}, f32[768,384]{1,0:T(8,128)}, f32[16,384]{1,0:T(8,128)}, f32[16,384]{1,0:T(8,128)}, /*index=5*/f32[16,384]{1,0:T(8,128)}) custom-call(f32[2]{0:T(128)} %pad_maximum_fusion.5.edge_ref, bf16[768,1536]{1,0:T(8,128)(2,1)} %bitcast.65, bf16[768,1536]{1,0:T(8,128)(2,1)} %collective-permute-done.refs_1_, ...), custom_call_target="tpu_custom_call" | custom-call | flops 1 | bytes 1 | tf_op jit(solution)/shard_map/pallas_call | solution.py:119
  185.7 0.0 copy-start.12
  185.7 1.4 copy-done.2
  187.2 15.4 %shard_map.131 = (f32[768,384]{1,0:T(8,128)}, f32[768,384]{1,0:T(8,128)}, f32[768,384]{1,0:T(8,128)}, f32[16,384]{1,0:T(8,128)}, f32[16,384]{1,0:T(8,128)}, /*index=5*/f32[16,384]{1,0:T(8,128)}) custom-call(f32[2]{0:T(128)} %pad_maximum_fusion.4.edge_ref, bf16[768,1536]{1,0:T(8,128)(2,1)} %bitcast.66, bf16[768,1536]{1,0:T(8,128)(2,1)} %collective-permute-done.refs_1_, ...), custom_call_target="tpu_custom_call" | custom-call | flops 1 | bytes 1 | tf_op jit(solution)/shard_map/pallas_call | solution.py:119
  202.6 0.8 maximum_select_fusion
  203.3 24.5 %collective-permute-start.4 = (f32[16,768]{1,0:T(8,128)S(1)}, f32[16,768]{1,0:T(8,128)S(1)}, u32[]{:S(2)}, u32[]{:S(2)}) collective-permute-start(f32[16,768]{1,0:T(8,128)S(1)} %maximum_select_fusion), channel_id=1, source_target_pairs={{0,128},{64,192},{128,0},{192,64},{1,129},{65,193},{129,1},{193,65... | collective-permute-start | bytes 147464 | tf_op jit(solution)/shard_map/ppermute | solution.py:401
  227.8 0.5 broadcast.132
  228.4 0.8 reduce.18
  229.2 0.7 reshape.274.far_ref
  229.9 1.9 shard_map.133
  231.8 1.3 collective-permute-start.6
  233.1 1.3 collective-permute-start.5
  234.4 0.5 broadcast_select_fusion.flags
  235.0 0.1 mul.29
  235.1 4.0 %collective-permute-done.5.refs_8_ = f32[16,768]{1,0:T(8,128)S(1)} collective-permute-done((f32[16,768]{1,0:T(8,128)}, f32[16,768]{1,0:T(8,128)S(1)}, u32[]{:S(2)}, u32[]{:S(2)}) %collective-permute-start.5) | collective-permute-done | bytes 49184 | tf_op jit(solution)/shard_map/ppermute | solution.py:381
  239.1 0.6 copy-done.10
  239.7 3.5 %shard_map.136 = (f32[80,768]{1,0:T(8,128)}, f32[80,768]{1,0:T(8,128)}) custom-call(f32[2]{0:T(128)} %broadcast_select_fusion.flags, f32[16,768]{1,0:T(8,128)} %copy-done.8, f32[768,384]{1,0:T(8,128)} %get-tuple-element.59.refs_0_, f32[16,384]{1,0:T(8,128)} %get-tuple-element.55.refs_1_, f32[768,384]{1,0:T(8,128)} %get-tuple-element.60.refs_2_, ...), custom_call_target="tpu_custom_call" | custom-call | flops 1 | bytes 1 | tf_op jit(solution)/shard_map/pallas_call | solution.py:265
  243.1 1.3 collective-permute-start.7
  244.4 5.1 %collective-permute-start.8 = (f32[80,768]{1,0:T(8,128)}, f32[80,768]{1,0:T(8,128)S(1)}, u32[]{:S(2)}, u32[]{:S(2)}) collective-permute-start(f32[80,768]{1,0:T(8,128)} %get-tuple-element.64), channel_id=1, source_target_pairs={{0,64},{64,128},{128,192},{1,65},{65,129},{129,193},{2,66},{66,130... | collective-permute-start | bytes 737288 | tf_op jit(solution)/shard_map/ppermute | solution.py:415
  249.6 0.6 dynamic_slice.12
  250.9 0.7 pad_maximum_fusion.3.scalars
  251.5 3.1 %gather_fusion.1 = bf16[24,32,768]{2,1,0:T(8,128)(2,1)} fusion(bf16[32,32,768]{2,1,0:T(8,128)(2,1)} %all-to-all-done.2, s32[1024]{0:T(1024)S(1)} %pad_clamp_fusion), kind=kCustom, calls=%fused_computation.1 | custom fusion | bytes 2359392 | tf_op jit(solution)/shard_map/gather | solution.py:396
  254.6 3.9 %shard_map.135.p = f32[768,768]{1,0:T(8,128)} custom-call(f32[16,768]{1,0:T(8,128)} %get-tuple-element.50.base.l, f32[16,768]{1,0:T(8,128)} %get-tuple-element.51.far_l, bf16[768,768]{1,0:T(8,128)(2,1)} %bitcast.68, f32[768,384]{1,0:T(8,128)} %get-tuple-element.53.refs_0_, f32[16,384]{1,0:T(8,128)} %get-tuple-element.48.refs_0_.refs_1_, ...), custom_call_target="tpu_custom_call" | custom-call | flops 1 | bytes 1 | tf_op jit(solution)/shard_map/pallas_call | solution.py:265
  258.6 0.7 copy-done.4
  259.2 0.1 copy-done.5
  259.3 3.0 %shard_map.137 = (bf16[768,64]{1,0:T(8,128)(2,1)}, f32[256,128]{1,0:T(8,128)}) custom-call(f32[3]{0:T(128)} %pad_maximum_fusion.3.scalars, f32[768,768]{1,0:T(8,128)} %shard_map.135.p, f32[16,768]{1,0:T(8,128)} %get-tuple-element.50.base.l, f32[80,768]{1,0:T(8,128)} %copy-done.4, f32[80,768]{1,0:T(8,128)} %copy-done.5, bf16[768,64]{1,0:T(8,128)(2,1)} %bitcast.77), custom_call_target="tpu_custom_call" | custom-call | flops 1 | bytes 1 | tf_op jit(solution)/shard_map/pallas_call | solution.py:265
  262.3 17.0 %all-to-all-start.3 = ((f32[256,1,128]{2,1,0:T(1,128)}), f32[256,1,128]{2,1,0:T(1,128)S(1)}, u32[]{:S(2)}, u32[]{:S(2)}) async-start(f32[256,1,128]{2,1,0:T(1,128)} %bitcast.78), calls=%async_computation.3 | async-start | bytes 262144 | tf_op jit(solution)/shard_map/all_to_all | solution.py:438
  279.3 0.6 dynamic_slice.14
  280.5 11.6 %all-to-all-done.3 = f32[256,1,128]{2,1,0:T(1,128)S(1)} async-done(((f32[256,1,128]{2,1,0:T(1,128)}), f32[256,1,128]{2,1,0:T(1,128)S(1)}, u32[]{:S(2)}, u32[]{:S(2)}) %all-to-all-start.3) | async-done | bytes 131104 | tf_op jit(solution)/shard_map/all_to_all | solution.py:438
  292.1 0.1 slice_reduce_fusion
  292.2 0.6 fusion.7
  (44 shorter events, 0.2 us)
Async XLA Ops:
  3.5 2.1 copy-start.11
  8.3 15.9 %copy-start = (bf16[1,1,2,12,32,1536]{5,4,3,2,1,0:T(8,128)(2,1)S(1)}, bf16[1,1,2,12,32,1536]{5,4,3,2,1,0:T(8,128)(2,1)}, u32[]{:S(2)}) copy-start(bf16[1,1,2,12,32,1536]{5,4,3,2,1,0:T(8,128)(2,1)} %param.16) | copy-start | bytes 7077892
  8.3 99.4 %all-to-all-start = ((bf16[32,32,1664]{2,1,0:T(8,128)(2,1)}), bf16[32,32,1664]{2,1,0:T(8,128)(2,1)}, u32[]{:S(2)}, u32[]{:S(2)}) async-start(bf16[32,32,1664]{2,1,0:T(8,128)(2,1)} %gather_fusion), calls=%async_computation | async-start | bytes 6815744 | tf_op jit(solution)/shard_map/all_to_all | solution.py:342
  15.9 8.6 %copy-start.1 = (bf16[1,1,2,12,32,1536]{5,4,3,2,1,0:T(8,128)(2,1)S(1)}, bf16[1,1,2,12,32,1536]{5,4,3,2,1,0:T(8,128)(2,1)}, u32[]{:S(2)}) copy-start(bf16[1,1,2,12,32,1536]{5,4,3,2,1,0:T(8,128)(2,1)} %param.17) | copy-start | bytes 7077892
  15.9 120.1 %collective-permute-start.1 = (bf16[768,1536]{1,0:T(8,128)(2,1)}, bf16[768,1536]{1,0:T(8,128)(2,1)}, u32[]{:S(2)}, u32[]{:S(2)}) collective-permute-start(bf16[768,1536]{1,0:T(8,128)(2,1)} %bitcast.63), channel_id=1, source_target_pairs={{64,0},{128,64},{192,128},{65,1},{129,65},{193,129},{66,2},{130,66... | collective-permute-start | bytes 7077896 | tf_op jit(solution)/shard_map/ppermute | solution.py:345
  17.4 118.7 %collective-permute-start = (bf16[768,1536]{1,0:T(8,128)(2,1)}, bf16[768,1536]{1,0:T(8,128)(2,1)}, u32[]{:S(2)}, u32[]{:S(2)}) collective-permute-start(bf16[768,1536]{1,0:T(8,128)(2,1)} %bitcast.64), channel_id=1, source_target_pairs={{0,64},{64,128},{128,192},{1,65},{65,129},{129,193},{2,66},{66,130... | collective-permute-start | bytes 7077896 | tf_op jit(solution)/shard_map/ppermute | solution.py:344
  26.4 159.3 %collective-permute-start.2 = (bf16[768,1536]{1,0:T(8,128)(2,1)}, bf16[768,1536]{1,0:T(8,128)(2,1)S(1)}, u32[]{:S(2)}, u32[]{:S(2)}) collective-permute-start(bf16[768,1536]{1,0:T(8,128)(2,1)} %pad_maximum_fusion.1), channel_id=1, source_target_pairs={{0,4},{4,8},{8,12},{12,16},{16,20},{20,24},{24,28},{28,32},{32,36}... | collective-permute-start | bytes 7077896 | tf_op jit(solution)/shard_map/ppermute | solution.py:329
  30.2 3.5 %copy-start.3 = (bf16[1536,64]{0,1:T(8,128)(2,1)S(1)}, bf16[1536,64]{0,1:T(8,128)(2,1)}, u32[]{:S(2)}) copy-start(bf16[1536,64]{0,1:T(8,128)(2,1)} %param.18) | copy-start | bytes 589828
  31.8 138.4 %collective-permute-start.3 = (bf16[768,1536]{1,0:T(8,128)(2,1)}, bf16[768,1536]{1,0:T(8,128)(2,1)}, u32[]{:S(2)}, u32[]{:S(2)}) collective-permute-start(bf16[768,1536]{1,0:T(8,128)(2,1)} %pad_maximum_fusion.2), channel_id=1, source_target_pairs={{4,0},{8,4},{12,8},{16,12},{20,16},{24,20},{28,24},{32,28},{36,32}... | collective-permute-start | bytes 7077896 | tf_op jit(solution)/shard_map/ppermute | solution.py:330
  122.9 18.9 %all-to-all-start.1 = ((f32[16,1,1024]{2,1,0:T(1,128)}), f32[16,1,1024]{2,1,0:T(1,128)S(1)}, u32[]{:S(2)}, u32[]{:S(2)}) async-start(f32[16,1,1024]{2,1,0:T(1,128)} %reshape.273), calls=%async_computation.1 | async-start | bytes 131072 | tf_op jit(solution)/shard_map/all_to_all | solution.py:375
  141.9 109.7 %all-to-all-start.2 = ((bf16[32,32,768]{2,1,0:T(8,128)(2,1)}), bf16[32,32,768]{2,1,0:T(8,128)(2,1)}, u32[]{:S(2)}, u32[]{:S(2)}) async-start(bf16[32,32,768]{2,1,0:T(8,128)(2,1)} %bitcast.67), calls=%async_computation.2 | async-start | bytes 3145728 | tf_op jit(solution)/shard_map/all_to_all | solution.py:387
  185.7 16.9 %copy-start.6 = (f32[16,384]{1,0:T(8,128)S(1)}, f32[16,384]{1,0:T(8,128)}, u32[]{:S(2)}) copy-start(f32[16,384]{1,0:T(8,128)} %get-tuple-element.58.refs_7_) | copy-start | bytes 73732
  185.7 16.9 %copy-start.7 = (f32[16,384]{1,0:T(8,128)S(1)}, f32[16,384]{1,0:T(8,128)}, u32[]{:S(2)}) copy-start(f32[16,384]{1,0:T(8,128)} %get-tuple-element.56.refs_3_) | copy-start | bytes 73732
  185.7 48.7 %copy-start.12 = (f32[2]{0:T(128)S(1)}, f32[2]{0:T(128)}, u32[]{:S(2)}) copy-start(f32[2]{0:T(128)} %constant.145.clone) | copy-start | bytes 28
  185.7 48.7 %copy-start.13 = (f32[2]{0:T(128)S(1)}, f32[2]{0:T(128)}, u32[]{:S(2)}) copy-start(f32[2]{0:T(128)} %constant.144.clone) | copy-start | bytes 28
  185.7 1.4 copy-start.2
  203.3 31.7 %collective-permute-start.4 = (f32[16,768]{1,0:T(8,128)S(1)}, f32[16,768]{1,0:T(8,128)S(1)}, u32[]{:S(2)}, u32[]{:S(2)}) collective-permute-start(f32[16,768]{1,0:T(8,128)S(1)} %maximum_select_fusion), channel_id=1, source_target_pairs={{0,128},{64,192},{128,0},{192,64},{1,129},{65,193},{129,1},{193,65... | collective-permute-start | bytes 147464 | tf_op jit(solution)/shard_map/ppermute | solution.py:401
  231.8 3.2 %collective-permute-start.6 = (f32[16,768]{1,0:T(8,128)}, f32[16,768]{1,0:T(8,128)S(1)}, u32[]{:S(2)}, u32[]{:S(2)}) collective-permute-start(f32[16,768]{1,0:T(8,128)} %get-tuple-element.50.base.l), channel_id=1, source_target_pairs={{0,64},{64,128},{128,192},{1,65},{65,129},{129,193},{2,66},{66,130... | collective-permute-start | bytes 147464 | tf_op jit(solution)/shard_map/ppermute | solution.py:380
  233.1 5.9 %collective-permute-start.5 = (f32[16,768]{1,0:T(8,128)}, f32[16,768]{1,0:T(8,128)S(1)}, u32[]{:S(2)}, u32[]{:S(2)}) collective-permute-start(f32[16,768]{1,0:T(8,128)} %get-tuple-element.50.base.l), channel_id=1, source_target_pairs={{64,0},{128,64},{192,128},{65,1},{129,65},{193,129},{66,2},{130,66... | collective-permute-start | bytes 147464 | tf_op jit(solution)/shard_map/ppermute | solution.py:381
  235.0 4.0 %copy-start.8 = (f32[16,768]{1,0:T(8,128)}, f32[16,768]{1,0:T(8,128)S(1)}, u32[]{:S(2)}) copy-start(f32[16,768]{1,0:T(8,128)S(1)} %collective-permute-done.4.other) | copy-start | bytes 147460
  235.0 4.0 %copy-start.9 = (f32[16,768]{1,0:T(8,128)}, f32[16,768]{1,0:T(8,128)S(1)}, u32[]{:S(2)}) copy-start(f32[16,768]{1,0:T(8,128)S(1)} %collective-permute-done.6.refs_9_) | copy-start | bytes 147460
  239.1 0.6 copy-start.10
  239.7 9.9 %copy-start.14 = (s32[2]{0:T(128)S(1)}, s32[2]{0:T(128)}, u32[]{:S(2)}) copy-start(s32[2]{0:T(128)} %param.22) | copy-start | bytes 28
  243.1 15.4 %collective-permute-start.7 = (f32[80,768]{1,0:T(8,128)}, f32[80,768]{1,0:T(8,128)S(1)}, u32[]{:S(2)}, u32[]{:S(2)}) collective-permute-start(f32[80,768]{1,0:T(8,128)} %get-tuple-element.63), channel_id=1, source_target_pairs={{64,0},{128,64},{192,128},{65,1},{129,65},{193,129},{66,2},{130,66... | collective-permute-start | bytes 737288 | tf_op jit(solution)/shard_map/ppermute | solution.py:416
  244.4 14.1 %collective-permute-start.8 = (f32[80,768]{1,0:T(8,128)}, f32[80,768]{1,0:T(8,128)S(1)}, u32[]{:S(2)}, u32[]{:S(2)}) collective-permute-start(f32[80,768]{1,0:T(8,128)} %get-tuple-element.64), channel_id=1, source_target_pairs={{0,64},{64,128},{128,192},{1,65},{65,129},{129,193},{2,66},{66,130... | collective-permute-start | bytes 737288 | tf_op jit(solution)/shard_map/ppermute | solution.py:415
  258.5 20.7 %copy-start.15 = (s32[2]{0:T(128)S(1)}, s32[2]{0:T(128)}, u32[]{:S(2)}) copy-start(s32[2]{0:T(128)} %param.23) | copy-start | bytes 28
  258.5 0.7 copy-start.4
  258.6 0.8 copy-start.5
  262.3 29.8 %all-to-all-start.3 = ((f32[256,1,128]{2,1,0:T(1,128)}), f32[256,1,128]{2,1,0:T(1,128)S(1)}, u32[]{:S(2)}, u32[]{:S(2)}) async-start(f32[256,1,128]{2,1,0:T(1,128)} %bitcast.78), calls=%async_computation.3 | async-start | bytes 262144 | tf_op jit(solution)/shard_map/all_to_all | solution.py:438

commit v3 on v2

--- a/solution.py
+++ b/solution.py
@@ -131,7 +131,8 @@
     return out[:groups], out[groups:]
 
 
-def far_kernel(per_step, heads, index_ref, query_ref, key_ref, value_ref, wbd_ref, out_ref, lse_ref):
+def far_kernel(per_step, heads, index_ref, query_ref, key_ref, value_ref, wbd_ref, *refs):
+    out_ref, lse_ref = refs[-2:]
     step = pl.program_id(0)
     upper = lax.broadcasted_iota(jnp.int32, (2 * TILE, 2 * HD), 0) // TILE
     right = lane_iota((2 * TILE, 2 * HD)) // HD
@@ -178,7 +179,7 @@
         lse_ref[o] = turned[:, o * SLOTS * TILE : (o + 1) * SLOTS * TILE]
 
 
-def far_attention(index, received, key, value, wbd):
+def far_attention(index, received, key, value, wbd, after):
     count = index.shape[0]
     inner = key.shape[1]
     heads = inner // HD
@@ -194,7 +195,8 @@
                 pl.BlockSpec(key.shape, lambda i, _: (0, 0)),
                 pl.BlockSpec(value.shape, lambda i, _: (0, 0)),
                 pl.BlockSpec(wbd.shape, lambda i, _: (0, 0)),
-            ],
+            ]
+            + [pl.BlockSpec(memory_space=pl.ANY)] * len(after),
             out_specs=[
                 pl.BlockSpec((per_step * TILE, width), lambda i, _: (i, 0)),
                 pl.BlockSpec((per_step // SLOTS, LSE_ROWS, SLOTS * TILE), lambda i, _: (i, 0, 0)),
@@ -206,7 +208,7 @@
         ],
         compiler_params=pltpu.CompilerParams(vmem_limit_bytes=56 * MIB),
         cost_estimate=pl.CostEstimate(flops=1, bytes_accessed=1, transcendentals=0),
-    )(index, received, key, value, wbd)
+    )(index, received, key, value, wbd, *after)
 
 
 def log_sum(*parts):
@@ -259,9 +261,10 @@
             out[rows, cols] = own_weight[h : h + 1, :] * p[rows, :] + far_weight[h : h + 1, :] * far[rows, :]
 
 
-def whole(kernel, out_shape, cost, *operands, smem=0):
+def whole(kernel, out_shape, cost, *operands, smem=0, after=()):
     specs = [pl.BlockSpec(memory_space=pltpu.SMEM)] * smem
     specs += [pl.BlockSpec(memory_space=pltpu.VMEM)] * (len(operands) - smem)
+    specs += [pl.BlockSpec(memory_space=pl.ANY)] * len(after)
     return pl.pallas_call(
         kernel,
         in_specs=specs,
@@ -269,7 +272,7 @@
         out_shape=out_shape,
         compiler_params=pltpu.CompilerParams(vmem_limit_bytes=56 * MIB),
         cost_estimate=pl.CostEstimate(flops=1, bytes_accessed=1, transcendentals=0),
-    )(*operands)
+    )(*operands, *after)
 
 
 def scale_kernel(heads, chunks, flags, other, *refs):
@@ -339,10 +342,15 @@
     source = jnp.sum(jnp.where(chosen, ids[:, None], 0), axis=0)
     marks = jnp.broadcast_to(offsets.astype(jnp.bfloat16)[:, None, None], (tiles, tile_len, 128))
     payload = jnp.concatenate([query.reshape(tiles, tile_len, inner), marks], axis=2)[source]
+    payload = tie(payload, [halo_before, halo_after])
     received = lax.all_to_all(payload, "height", split_axis=0, concat_axis=0, tiled=True)
 
-    from_below = lax.ppermute(query, "tm", up_frames)
-    from_above = lax.ppermute(query, "tm", down_frames)
+    from_below = []
+    from_above = []
+    for r in range(rows_dev):
+        part = tie(query[r * row_tokens : (r + 1) * row_tokens], [halo_before, halo_after])
+        from_below.append(lax.ppermute(part, "tm", up_frames))
+        from_above.append(lax.ppermute(part, "tm", down_frames))
 
     wt = jnp.transpose(head_weight)
     paired = head_weight.reshape(heads // 2, 2, HD, PATCH)
@@ -363,15 +371,14 @@
         values = [before[2:], (value, r), after[2:]]
         return window_attention(edge, queries, block, keys, values, wt, columns, first)
 
-    own, ups, downs = [], [], []
+    own = []
     for r in range(rows_dev):
-        ps, ls = attend(r, [query, from_below, from_above], r)
-        for held, p, l in zip((own, downs, ups), ps, ls):
-            held.append((p, l))
+        (p,), (l,) = attend(r, [query], r)
+        own.append((p, l))
 
     index = received[:, 0, inner].astype(jnp.int32)
     received = received.reshape(slot_count * tile_len, inner + 128)
-    far_p, far_l = far_attention(index, received, key, value, wbd)
+    far_p, far_l = far_attention(index, received, key, value, wbd, [l for _, l in own])
     far_l = lax.all_to_all(far_l, "height", split_axis=0, concat_axis=0, tiled=True)
     flat = jax.ShapeDtypeStruct((LSE_ROWS, tokens), jnp.float32)
     far_l, base_lse = whole(
@@ -382,8 +389,14 @@
 
     swap = [(i, i + 2) for i in range(frames_n - 2)] + [(i + 2, i) for i in range(frames_n - 2)]
     low = frame < frames_n - 2
+    ups = []
+    downs = []
+    for r in range(rows_dev):
+        (pd, pu), (ld, lu) = attend(r, [from_below[r], from_above[r]], 0)
+        ups.append((pu, lu))
+        downs.append((pd, ld))
     width = far_p.shape[1]
-    far_p = tie(far_p, [from_below, from_above])
+    far_p = tie(far_p, [ups[0][1], from_below[-1], from_above[-1]])
     far_p = lax.all_to_all(
         far_p.reshape(slot_count, tile_len, width), "height", split_axis=0, concat_axis=0, tiled=True
     )

time: 297 us -> 292 us (0.983)
  waiting for transfers between devices: 93 us -> 76.8 us
  Pallas kernels: 54.7 us -> 70.5 us
  starting transfers between devices: 112 us -> 98.3 us
  local copies, waits for them, and re-layouts: 17 us -> 25.4 us
    all_to_all x1, waiting for transfers between devices: 71.6 us -> 46.8 us  [body(): lax.all_to_all(payload, 'height', split_axis=0, concat_axis=0, tiled=True)]
    ppermute x1, starting transfers between devices: 24.5 us -> 6.1 us  [body(): other = lax.ppermute(jnp.where(low, lse_u, lse_d), 'tm', swap)]
    pallas_call x2 -> x4, Pallas kernels: 30.9 us -> 46.7 us  [window_attention(): pl.pallas_call(functools.partial(window_kernel, groups, columns), grid=(s...]
    ppermute x1, waiting for transfers between devices: 0.01 us -> 11.7 us  [body(): halo_before = lax.ppermute(last, 'height', up_rows)]
    ppermute x1, waiting for transfers between devices: 0.01 us -> 5.93 us  [body(): halo_after = lax.ppermute(initial, 'height', down_rows)]
    all_to_all x1, waiting for transfers between devices: 5.8 us -> 0.01 us  [body(): lax.all_to_all(far_l, 'height', split_axis=0, concat_axis=0, tiled=True)]
    ppermute x2 -> x4, starting transfers between devices: 8.31 us -> 13.6 us  [the longest x2 11 us: body(): from_below.append(lax.ppermute(part, 'tm', up_frames))]
    ppermute x1, waiting for transfers between devices: 4.01 us -> 0.01 us  [body(): base_above = lax.ppermute(base_lse, 'tm', down_frames)]
  transfers between devices with their start and end apart: 13 -> 15, of which waited for: 4 -> 5; matrix products, arithmetic and copies ran while one was open for 6% -> 10% of each run, Pallas kernels for 17% -> 23%
where the time goes in v3:
time: 292 us; the launch traced here: 291 us
  starting transfers between devices  98.3 us (34%)
  waiting for transfers between devices  76.8 us (26%)
  Pallas kernels  70.5 us (24%)
  local copies, waits for them, and re-layouts  25.4 us (9%)
  other arithmetic  13.8 us (5%)
  between operations  6.02 us (2%)
    all_to_all x1, waiting for transfers between devices, body(): lax.all_to_all(payload, 'height', split_axis=0, concat_axis=0, tiled=True)  46.8 us
    pallas_call x4, Pallas kernels, window_attention(): pl.pallas_call(functools.partial(window_kernel, groups, columns), grid=(s...  46.7 us
    all_to_all x1, starting transfers between devices, body(): lax.all_to_all(far_p.reshape(slot_count, tile_len, width), 'height', spli...  23.5 us
    all_to_all x1, starting transfers between devices, body(): lax.all_to_all(squares, ('pair', 'tm', 'height'), split_axis=0, concat_ax...  18.8 us
    pallas_call x4, Pallas kernels, whole(): pl.pallas_call(kernel, in_specs=specs, out_specs=jax.tree.map(lambda _: p...  12.3 us
    ppermute x1, waiting for transfers between devices, body(): halo_before = lax.ppermute(last, 'height', up_rows)  11.7 us
    all_to_all x1, waiting for transfers between devices, body(): lax.all_to_all(squares, ('pair', 'tm', 'height'), split_axis=0, concat_ax...  11.6 us
    pallas_call x1, Pallas kernels, far_attention(): pl.pallas_call(functools.partial(far_kernel, per_step, heads), grid_spec=...  11.5 us
  transfers between devices with their start and end apart: 15, of which 5 were waited for; matrix products, arithmetic and copies ran while one was open for 10% of the time, Pallas kernels for 23%

profile of v3, /device:TPU:1, one launch (start us, length us, event | category | flops | bytes accessed | tf_op | source)
XLA Modules:
  0.0 290.7 jit_solution(2496258106685581445)
XLA Ops:
  0.6 2.0 fusion.6
  2.6 0.4 copy-done
  3.0 0.2 fusion.5
  3.2 1.6 pad_maximum_fusion.1
  4.9 4.6 %collective-permute-start = (bf16[768,1536]{1,0:T(8,128)(2,1)}, bf16[768,1536]{1,0:T(8,128)(2,1)}, u32[]{:S(2)}, u32[]{:S(2)}) collective-permute-start(bf16[768,1536]{1,0:T(8,128)(2,1)} %pad_maximum_fusion.1), channel_id=1, source_target_pairs={{0,4},{4,8},{8,12},{12,16},{16,20},{20,24},{24,28},{28,32},{32,36}... | collective-permute-start | bytes 7077896 | tf_op jit(solution)/shard_map/ppermute | solution.py:332
  9.5 1.6 pad_maximum_fusion.2
  11.1 3.2 %collective-permute-start.1 = (bf16[768,1536]{1,0:T(8,128)(2,1)}, bf16[768,1536]{1,0:T(8,128)(2,1)S(1)}, u32[]{:S(2)}, u32[]{:S(2)}) collective-permute-start(bf16[768,1536]{1,0:T(8,128)(2,1)} %pad_maximum_fusion.2), channel_id=1, source_target_pairs={{4,0},{8,4},{12,8},{16,12},{20,16},{24,20},{28,24},{32,28},{36,32}... | collective-permute-start | bytes 7077896 | tf_op jit(solution)/shard_map/ppermute | solution.py:333
  14.3 0.5 broadcast.131
  14.9 0.7 multiply_reduce_fusion
  15.7 0.2 convert_reduce_fusion
  16.1 3.4 %pad_maximum_fusion = bf16[24,32,1664]{2,1,0:T(8,128)(2,1)} fusion(bf16[24,32,128]{2,1,0:T(8,128)(2,1)S(1)} %broadcast_in_dim.14, bf16[24,32,1536]{2,1,0:T(8,128)(2,1)} %bitcast.72), kind=kLoop, calls=%fused_computation.2 | loop fusion | flops 5111808 | bytes 5111808 | tf_op jit(solution)/shard_map/concatenate | solution.py:344
  19.5 4.4 %gather_fusion = bf16[32,32,1664]{2,1,0:T(8,128)(2,1)} fusion(bf16[24,32,1664]{2,1,0:T(8,128)(2,1)} %pad_maximum_fusion, s32[1024]{0:T(1024)S(1)} %pad_clamp_fusion.1), kind=kCustom, calls=%fused_computation | custom fusion | bytes 6815872 | tf_op jit(solution)/shard_map/gather | solution.py:344
  23.9 11.7 %collective-permute-done.refs_1_.refs_4_.refs_2_.refs_5_ = bf16[768,1536]{1,0:T(8,128)(2,1)} collective-permute-done((bf16[768,1536]{1,0:T(8,128)(2,1)}, bf16[768,1536]{1,0:T(8,128)(2,1)}, u32[]{:S(2)}, u32[]{:S(2)}) %collective-permute-start) | collective-permute-done | bytes 2359328 | tf_op jit(solution)/shard_map/ppermute | solution.py:332
  35.6 5.9 %collective-permute-done.1.refs_2_.refs_3_.refs_6_.refs_4_.refs_7_ = bf16[768,1536]{1,0:T(8,128)(2,1)S(1)} collective-permute-done((bf16[768,1536]{1,0:T(8,128)(2,1)}, bf16[768,1536]{1,0:T(8,128)(2,1)S(1)}, u32[]{:S(2)}, u32[]{:S(2)}) %collective-permute-start.1) | collective-permute-done | bytes 2359328 | tf_op jit(solution)/shard_map/ppermute | solution.py:333
  41.5 1.5 copy-done.1
  43.0 6.7 %all-to-all-start = ((bf16[32,32,1664]{2,1,0:T(8,128)(2,1)}), bf16[32,32,1664]{2,1,0:T(8,128)(2,1)}, u32[]{:S(2)}, u32[]{:S(2)}) async-start(bf16[32,32,1664]{2,1,0:T(8,128)(2,1)} %shard_map.130), calls=%async_computation | async-start | bytes 6815744 | tf_op jit(solution)/shard_map/all_to_all | solution.py:346
  49.6 1.6 fusion.4
  51.2 5.9 %collective-permute-start.2 = (bf16[384,1536]{1,0:T(8,128)(2,1)}, bf16[384,1536]{1,0:T(8,128)(2,1)}, u32[]{:S(2)}, u32[]{:S(2)}) collective-permute-start(bf16[384,1536]{1,0:T(8,128)(2,1)} %shard_map.135), channel_id=1, source_target_pairs={{0,64},{64,128},{128,192},{1,65},{65,129},{129,193},{2,66},{66,130... | collective-permute-start | bytes 3538952 | tf_op jit(solution)/shard_map/ppermute | solution.py:352
  57.1 1.3 collective-permute-start.3
  58.5 5.1 %collective-permute-start.4 = (bf16[384,1536]{1,0:T(8,128)(2,1)}, bf16[384,1536]{1,0:T(8,128)(2,1)S(1)}, u32[]{:S(2)}, u32[]{:S(2)}) collective-permute-start(bf16[384,1536]{1,0:T(8,128)(2,1)} %shard_map.137), channel_id=1, source_target_pairs={{0,64},{64,128},{128,192},{1,65},{65,129},{129,193},{2,66},{66,130... | collective-permute-start | bytes 3538952 | tf_op jit(solution)/shard_map/ppermute | solution.py:352
  63.6 1.3 collective-permute-start.5
  64.9 0.3 fusion.7
  65.2 0.8 scatter.6
  66.0 0.7 bitcast_dynamic-update-slice_fusion
  66.7 2.3 copy.40
  69.0 1.2 reshape.258.wbd_ref
  70.2 0.7 pad_maximum_fusion.4.edge_ref
  70.9 0.6 pad_maximum_fusion.5.edge_ref
  71.5 11.6 %shard_map.131 = (f32[768,384]{1,0:T(8,128)}, f32[16,384]{1,0:T(8,128)}) custom-call(f32[2]{0:T(128)} %pad_maximum_fusion.4.edge_ref, bf16[768,1536]{1,0:T(8,128)(2,1)} %bitcast.73, bf16[768,1536]{1,0:T(8,128)(2,1)} %collective-permute-done.refs_1_.refs_4_.refs_2_.refs_5_, bf16[768,1536]{1,0:T(8,128)(2,1)} %bitcast.63, bf16[768,1536]{1,0:T(8,128)(2,1)} %bitcast.64, ...), custom_call_target="tpu_custom_call" | custom-call | flops 1 | bytes 1 | tf_op jit(solution)/shard_map/pallas_call | solution.py:119
  83.0 11.6 %shard_map.132 = (f32[768,384]{1,0:T(8,128)}, f32[16,384]{1,0:T(8,128)}) custom-call(f32[2]{0:T(128)} %pad_maximum_fusion.5.edge_ref, bf16[768,1536]{1,0:T(8,128)(2,1)} %bitcast.74, bf16[768,1536]{1,0:T(8,128)(2,1)} %bitcast.65, bf16[768,1536]{1,0:T(8,128)(2,1)} %bitcast.66, bf16[768,1536]{1,0:T(8,128)(2,1)} %copy-done.1, bf16[768,1536]{1,0:T(8,128)(2,1)} %bitcast.56, ...), custom_call_target="tpu_custom_call" | custom-call | flops 1 | bytes 1 | tf_op jit(solution)/shard_map/pallas_call | solution.py:119
  94.6 46.8 %all-to-all-done = bf16[32,32,1664]{2,1,0:T(8,128)(2,1)} async-done(((bf16[32,32,1664]{2,1,0:T(8,128)(2,1)}), bf16[32,32,1664]{2,1,0:T(8,128)(2,1)}, u32[]{:S(2)}, u32[]{:S(2)}) %all-to-all-start) | async-done | bytes 3407904 | tf_op jit(solution)/shard_map/all_to_all | solution.py:346
  141.4 2.0 fusion.index_ref
  143.4 11.5 %shard_map.133 = (bf16[1024,768]{1,0:T(8,128)(2,1)}, f32[16,16,64]{2,1,0:T(8,128)}) custom-call(s32[32]{0:T(128)} %fusion.index_ref, bf16[1024,1664]{1,0:T(8,128)(2,1)} %bitcast.9.query_ref, bf16[768,1536]{1,0:T(8,128)(2,1)} %bitcast.67, bf16[768,1536]{1,0:T(8,128)(2,1)} %bitcast.58, bf16[256,768]{1,0:T(8,128)(2,1)} %reshape.258.wbd_ref, ...), custom_call_target="tpu_custom_call" | custom-call | flops 1 | bytes 1 | tf_op jit(solution)/shard_map/pallas_call | solution.py:188
  154.9 1.7 reshape.275
  156.6 9.2 %all-to-all-start.1 = ((f32[16,1,1024]{2,1,0:T(1,128)}), f32[16,1,1024]{2,1,0:T(1,128)S(1)}, u32[]{:S(2)}, u32[]{:S(2)}) async-start(f32[16,1,1024]{2,1,0:T(1,128)} %reshape.275), calls=%async_computation.1 | async-start | bytes 131072 | tf_op jit(solution)/shard_map/all_to_all | solution.py:382
  165.8 11.7 %shard_map.136 = (f32[768,384]{1,0:T(8,128)}, f32[768,384]{1,0:T(8,128)}, f32[16,384]{1,0:T(8,128)}, f32[16,384]{1,0:T(8,128)}) custom-call(f32[2]{0:T(128)} %pad_maximum_fusion.4.edge_ref, bf16[384,1536]{1,0:T(8,128)(2,1)} %collective-permute-done.2.refs_0_, bf16[384,1536]{1,0:T(8,128)(2,1)} %collective-permute-done.3.refs_1_, ...), custom_call_target="tpu_custom_call" | custom-call | flops 1 | bytes 1 | tf_op jit(solution)/shard_map/pallas_call | solution.py:119
  177.6 1.0 copy-done.4
  178.6 0.4 copy-done.5
  179.0 23.5 %all-to-all-start.2 = ((bf16[32,32,768]{2,1,0:T(8,128)(2,1)}), bf16[32,32,768]{2,1,0:T(8,128)(2,1)S(1)}, u32[]{:S(2)}, u32[]{:S(2)}) async-start(bf16[32,32,768]{2,1,0:T(8,128)(2,1)} %bitcast.75), calls=%async_computation.2 | async-start | bytes 3145728 | tf_op jit(solution)/shard_map/all_to_all | solution.py:400
  202.5 11.8 %shard_map.140 = (f32[768,384]{1,0:T(8,128)}, f32[768,384]{1,0:T(8,128)}, f32[16,384]{1,0:T(8,128)}, f32[16,384]{1,0:T(8,128)}) custom-call(f32[2]{0:T(128)} %pad_maximum_fusion.5.edge_ref, bf16[384,1536]{1,0:T(8,128)(2,1)} %copy-done.4, bf16[384,1536]{1,0:T(8,128)(2,1)} %copy-done.5, bf16[768,1536]{1,0:T(8,128)(2,1)} %bitcast.70, ...), custom_call_target="tpu_custom_call" | custom-call | flops 1 | bytes 1 | tf_op jit(solution)/shard_map/pallas_call | solution.py:119
  214.3 0.8 maximum_select_fusion
  215.1 0.5 broadcast.132
  215.6 0.8 reduce.18
  216.4 0.7 reshape.276.far_ref
  217.1 6.1 %collective-permute-start.6 = (f32[16,768]{1,0:T(8,128)S(1)}, f32[16,768]{1,0:T(8,128)S(1)}, u32[]{:S(2)}, u32[]{:S(2)}) collective-permute-start(f32[16,768]{1,0:T(8,128)S(1)} %maximum_select_fusion), channel_id=1, source_target_pairs={{0,128},{64,192},{128,0},{192,64},{1,129},{65,193},{129,1},{193,65... | collective-permute-start | bytes 147464 | tf_op jit(solution)/shard_map/ppermute | solution.py:414
  223.2 1.9 shard_map.134
  225.2 1.3 collective-permute-start.7
  226.5 4.9 %collective-permute-start.8 = (f32[16,768]{1,0:T(8,128)}, f32[16,768]{1,0:T(8,128)S(1)}, u32[]{:S(2)}, u32[]{:S(2)}) collective-permute-start(f32[16,768]{1,0:T(8,128)} %get-tuple-element.50.base.l), channel_id=1, source_target_pairs={{0,64},{64,128},{128,192},{1,65},{65,129},{129,193},{2,66},{66,130... | collective-permute-start | bytes 147464 | tf_op jit(solution)/shard_map/ppermute | solution.py:387
  231.4 0.5 broadcast_select_fusion.flags
  232.0 0.8 collective-permute-done.8.refs_9_
  232.8 0.6 copy-done.12
  233.4 3.5 %shard_map.141 = (f32[80,768]{1,0:T(8,128)}, f32[80,768]{1,0:T(8,128)}) custom-call(f32[2]{0:T(128)} %broadcast_select_fusion.flags, f32[16,768]{1,0:T(8,128)} %copy-done.10, f32[768,384]{1,0:T(8,128)} %get-tuple-element.59.refs_0_, f32[16,384]{1,0:T(8,128)} %get-tuple-element.53.refs_1_, f32[768,384]{1,0:T(8,128)} %get-tuple-element.60.refs_2_, ...), custom_call_target="tpu_custom_call" | custom-call | flops 1 | bytes 1 | tf_op jit(solution)/shard_map/pallas_call | solution.py:268
  236.9 1.3 collective-permute-start.9
  238.2 5.1 %collective-permute-start.10 = (f32[80,768]{1,0:T(8,128)}, f32[80,768]{1,0:T(8,128)S(1)}, u32[]{:S(2)}, u32[]{:S(2)}) collective-permute-start(f32[80,768]{1,0:T(8,128)} %get-tuple-element.64), channel_id=1, source_target_pairs={{0,64},{64,128},{128,192},{1,65},{65,129},{129,193},{2,66},{66,130... | collective-permute-start | bytes 737288 | tf_op jit(solution)/shard_map/ppermute | solution.py:428
  243.4 0.6 dynamic_slice.12
  244.7 0.7 pad_maximum_fusion.3.scalars
  245.4 1.7 gather_fusion.1
  247.0 3.9 %shard_map.139.p = f32[768,768]{1,0:T(8,128)} custom-call(f32[16,768]{1,0:T(8,128)} %get-tuple-element.50.base.l, f32[16,768]{1,0:T(8,128)} %get-tuple-element.51.far_l, bf16[768,768]{1,0:T(8,128)(2,1)} %bitcast.82, f32[768,384]{1,0:T(8,128)} %get-tuple-element.54.refs_0_, f32[16,384]{1,0:T(8,128)} %get-tuple-element.47.refs_0_.refs_1_, ...), custom_call_target="tpu_custom_call" | custom-call | flops 1 | bytes 1 | tf_op jit(solution)/shard_map/pallas_call | solution.py:268
  251.0 0.7 copy-done.6
  251.8 3.0 %shard_map.142 = (bf16[768,64]{1,0:T(8,128)(2,1)}, f32[256,128]{1,0:T(8,128)}) custom-call(f32[3]{0:T(128)} %pad_maximum_fusion.3.scalars, f32[768,768]{1,0:T(8,128)} %shard_map.139.p, f32[16,768]{1,0:T(8,128)} %get-tuple-element.50.base.l, f32[80,768]{1,0:T(8,128)} %copy-done.6, f32[80,768]{1,0:T(8,128)} %copy-done.7, bf16[768,64]{1,0:T(8,128)(2,1)} %bitcast.89), custom_call_target="tpu_custom_call" | custom-call | flops 1 | bytes 1 | tf_op jit(solution)/shard_map/pallas_call | solution.py:268
  254.7 18.8 %all-to-all-start.3 = ((f32[256,1,128]{2,1,0:T(1,128)}), f32[256,1,128]{2,1,0:T(1,128)S(1)}, u32[]{:S(2)}, u32[]{:S(2)}) async-start(f32[256,1,128]{2,1,0:T(1,128)} %bitcast.90), calls=%async_computation.3 | async-start | bytes 262144 | tf_op jit(solution)/shard_map/all_to_all | solution.py:451
  273.6 0.6 dynamic_slice.14
  274.8 11.6 %all-to-all-done.3 = f32[256,1,128]{2,1,0:T(1,128)S(1)} async-done(((f32[256,1,128]{2,1,0:T(1,128)}), f32[256,1,128]{2,1,0:T(1,128)S(1)}, u32[]{:S(2)}, u32[]{:S(2)}) %all-to-all-start.3) | async-done | bytes 131104 | tf_op jit(solution)/shard_map/all_to_all | solution.py:451
  286.5 0.6 fusion.8
  (62 shorter events, 0.9 us)
Async XLA Ops:
  0.6 2.4 copy-start
  4.9 30.7 %collective-permute-start = (bf16[768,1536]{1,0:T(8,128)(2,1)}, bf16[768,1536]{1,0:T(8,128)(2,1)}, u32[]{:S(2)}, u32[]{:S(2)}) collective-permute-start(bf16[768,1536]{1,0:T(8,128)(2,1)} %pad_maximum_fusion.1), channel_id=1, source_target_pairs={{0,4},{4,8},{8,12},{12,16},{16,20},{20,24},{24,28},{28,32},{32,36}... | collective-permute-start | bytes 7077896 | tf_op jit(solution)/shard_map/ppermute | solution.py:332
  9.5 5.4 %copy-start.13 = (s32[1,1,2,12,1]{3,4,2,1,0:T(1,128)S(1)}, s32[1,1,2,12,1]{3,4,2,1,0:T(1,128)}, u32[]{:S(2)}) copy-start(s32[1,1,2,12,1]{3,4,2,1,0:T(1,128)} %param.20) | copy-start | bytes 292
  9.5 6.1 %copy-start.17 = (s32[1,1,2,12,1]{3,4,2,1,0:T(1,128)S(1)}, s32[1,1,2,12,1]{3,4,2,1,0:T(1,128)}, u32[]{:S(2)}) copy-start(s32[1,1,2,12,1]{3,4,2,1,0:T(1,128)} %param.21) | copy-start | bytes 292
  11.1 30.4 %collective-permute-start.1 = (bf16[768,1536]{1,0:T(8,128)(2,1)}, bf16[768,1536]{1,0:T(8,128)(2,1)S(1)}, u32[]{:S(2)}, u32[]{:S(2)}) collective-permute-start(bf16[768,1536]{1,0:T(8,128)(2,1)} %pad_maximum_fusion.2), channel_id=1, source_target_pairs={{4,0},{8,4},{12,8},{16,12},{20,16},{24,20},{28,24},{32,28},{36,32}... | collective-permute-start | bytes 7077896 | tf_op jit(solution)/shard_map/ppermute | solution.py:333
  15.9 3.6 %copy-start.14 = (s32[24]{0:T(128)}, s32[24]{0:T(128)S(1)}, u32[]{:S(2)}) copy-start(s32[24]{0:T(128)S(1)} %multiply_add_fusion.slot_ref) | copy-start | bytes 292
  41.5 1.5 copy-start.1
  43.0 6.7 %copy-start.2 = (bf16[1,1,2,12,32,1536]{5,4,3,2,1,0:T(8,128)(2,1)S(1)}, bf16[1,1,2,12,32,1536]{5,4,3,2,1,0:T(8,128)(2,1)}, u32[]{:S(2)}) copy-start(bf16[1,1,2,12,32,1536]{5,4,3,2,1,0:T(8,128)(2,1)} %param.15) | copy-start | bytes 7077892
  43.0 98.4 %all-to-all-start = ((bf16[32,32,1664]{2,1,0:T(8,128)(2,1)}), bf16[32,32,1664]{2,1,0:T(8,128)(2,1)}, u32[]{:S(2)}, u32[]{:S(2)}) async-start(bf16[32,32,1664]{2,1,0:T(8,128)(2,1)} %shard_map.130), calls=%async_computation | async-start | bytes 6815744 | tf_op jit(solution)/shard_map/all_to_all | solution.py:346
  51.2 114.6 %collective-permute-start.2 = (bf16[384,1536]{1,0:T(8,128)(2,1)}, bf16[384,1536]{1,0:T(8,128)(2,1)}, u32[]{:S(2)}, u32[]{:S(2)}) collective-permute-start(bf16[384,1536]{1,0:T(8,128)(2,1)} %shard_map.135), channel_id=1, source_target_pairs={{0,64},{64,128},{128,192},{1,65},{65,129},{129,193},{2,66},{66,130... | collective-permute-start | bytes 3538952 | tf_op jit(solution)/shard_map/ppermute | solution.py:352
  57.1 108.7 %collective-permute-start.3 = (bf16[384,1536]{1,0:T(8,128)(2,1)}, bf16[384,1536]{1,0:T(8,128)(2,1)}, u32[]{:S(2)}, u32[]{:S(2)}) collective-permute-start(bf16[384,1536]{1,0:T(8,128)(2,1)} %shard_map.135), channel_id=1, source_target_pairs={{64,0},{128,64},{192,128},{65,1},{129,65},{193,129},{66,2},{130,66... | collective-permute-start | bytes 3538952 | tf_op jit(solution)/shard_map/ppermute | solution.py:353
  58.4 6.4 %copy-start.3 = (bf16[1536,64]{0,1:T(8,128)(2,1)S(1)}, bf16[1536,64]{0,1:T(8,128)(2,1)}, u32[]{:S(2)}) copy-start(bf16[1536,64]{0,1:T(8,128)(2,1)} %param.18) | copy-start | bytes 589828
  58.5 119.1 %collective-permute-start.4 = (bf16[384,1536]{1,0:T(8,128)(2,1)}, bf16[384,1536]{1,0:T(8,128)(2,1)S(1)}, u32[]{:S(2)}, u32[]{:S(2)}) collective-permute-start(bf16[384,1536]{1,0:T(8,128)(2,1)} %shard_map.137), channel_id=1, source_target_pairs={{0,64},{64,128},{128,192},{1,65},{65,129},{129,193},{2,66},{66,130... | collective-permute-start | bytes 3538952 | tf_op jit(solution)/shard_map/ppermute | solution.py:352
  63.6 114.0 %collective-permute-start.5 = (bf16[384,1536]{1,0:T(8,128)(2,1)}, bf16[384,1536]{1,0:T(8,128)(2,1)S(1)}, u32[]{:S(2)}, u32[]{:S(2)}) collective-permute-start(bf16[384,1536]{1,0:T(8,128)(2,1)} %shard_map.137), channel_id=1, source_target_pairs={{64,0},{128,64},{192,128},{65,1},{129,65},{193,129},{66,2},{130,66... | collective-permute-start | bytes 3538952 | tf_op jit(solution)/shard_map/ppermute | solution.py:353
  156.6 22.4 %all-to-all-start.1 = ((f32[16,1,1024]{2,1,0:T(1,128)}), f32[16,1,1024]{2,1,0:T(1,128)S(1)}, u32[]{:S(2)}, u32[]{:S(2)}) async-start(f32[16,1,1024]{2,1,0:T(1,128)} %reshape.275), calls=%async_computation.1 | async-start | bytes 131072 | tf_op jit(solution)/shard_map/all_to_all | solution.py:382
  177.6 1.0 copy-start.4
  177.6 1.4 copy-start.5
  179.0 66.4 %all-to-all-start.2 = ((bf16[32,32,768]{2,1,0:T(8,128)(2,1)}), bf16[32,32,768]{2,1,0:T(8,128)(2,1)S(1)}, u32[]{:S(2)}, u32[]{:S(2)}) async-start(bf16[32,32,768]{2,1,0:T(8,128)(2,1)} %bitcast.75), calls=%async_computation.2 | async-start | bytes 3145728 | tf_op jit(solution)/shard_map/all_to_all | solution.py:400
  202.5 11.8 %copy-start.8 = (f32[16,384]{1,0:T(8,128)S(1)}, f32[16,384]{1,0:T(8,128)}, u32[]{:S(2)}) copy-start(f32[16,384]{1,0:T(8,128)} %get-tuple-element.53.refs_1_) | copy-start | bytes 73732
  202.5 11.8 %copy-start.9 = (f32[16,384]{1,0:T(8,128)S(1)}, f32[16,384]{1,0:T(8,128)}, u32[]{:S(2)}) copy-start(f32[16,384]{1,0:T(8,128)} %get-tuple-element.57.refs_5_) | copy-start | bytes 73732
  202.5 28.9 %copy-start.15 = (f32[2]{0:T(128)S(1)}, f32[2]{0:T(128)}, u32[]{:S(2)}) copy-start(f32[2]{0:T(128)} %constant.144.clone) | copy-start | bytes 28
  202.5 28.9 %copy-start.16 = (f32[2]{0:T(128)S(1)}, f32[2]{0:T(128)}, u32[]{:S(2)}) copy-start(f32[2]{0:T(128)} %constant.145.clone) | copy-start | bytes 28
  217.1 14.8 %collective-permute-start.6 = (f32[16,768]{1,0:T(8,128)S(1)}, f32[16,768]{1,0:T(8,128)S(1)}, u32[]{:S(2)}, u32[]{:S(2)}) collective-permute-start(f32[16,768]{1,0:T(8,128)S(1)} %maximum_select_fusion), channel_id=1, source_target_pairs={{0,128},{64,192},{128,0},{192,64},{1,129},{65,193},{129,1},{193,65... | collective-permute-start | bytes 147464 | tf_op jit(solution)/shard_map/ppermute | solution.py:414
  225.2 6.8 %collective-permute-start.7 = (f32[16,768]{1,0:T(8,128)}, f32[16,768]{1,0:T(8,128)S(1)}, u32[]{:S(2)}, u32[]{:S(2)}) collective-permute-start(f32[16,768]{1,0:T(8,128)} %get-tuple-element.50.base.l), channel_id=1, source_target_pairs={{64,0},{128,64},{192,128},{65,1},{129,65},{193,129},{66,2},{130,66... | collective-permute-start | bytes 147464 | tf_op jit(solution)/shard_map/ppermute | solution.py:388
  226.5 6.4 %collective-permute-start.8 = (f32[16,768]{1,0:T(8,128)}, f32[16,768]{1,0:T(8,128)S(1)}, u32[]{:S(2)}, u32[]{:S(2)}) collective-permute-start(f32[16,768]{1,0:T(8,128)} %get-tuple-element.50.base.l), channel_id=1, source_target_pairs={{0,64},{64,128},{128,192},{1,65},{65,129},{129,193},{2,66},{66,130... | collective-permute-start | bytes 147464 | tf_op jit(solution)/shard_map/ppermute | solution.py:387
  232.0 0.9 copy-start.10
  232.0 0.9 copy-start.11
  232.8 0.6 copy-start.12
  233.4 10.0 %copy-start.18 = (s32[2]{0:T(128)S(1)}, s32[2]{0:T(128)}, u32[]{:S(2)}) copy-start(s32[2]{0:T(128)} %param.22) | copy-start | bytes 28
  236.9 14.1 %collective-permute-start.9 = (f32[80,768]{1,0:T(8,128)}, f32[80,768]{1,0:T(8,128)S(1)}, u32[]{:S(2)}, u32[]{:S(2)}) collective-permute-start(f32[80,768]{1,0:T(8,128)} %get-tuple-element.63), channel_id=1, source_target_pairs={{64,0},{128,64},{192,128},{65,1},{129,65},{193,129},{66,2},{130,66... | collective-permute-start | bytes 737288 | tf_op jit(solution)/shard_map/ppermute | solution.py:429
  238.2 12.8 %collective-permute-start.10 = (f32[80,768]{1,0:T(8,128)}, f32[80,768]{1,0:T(8,128)S(1)}, u32[]{:S(2)}, u32[]{:S(2)}) collective-permute-start(f32[80,768]{1,0:T(8,128)} %get-tuple-element.64), channel_id=1, source_target_pairs={{0,64},{64,128},{128,192},{1,65},{65,129},{129,193},{2,66},{66,130... | collective-permute-start | bytes 737288 | tf_op jit(solution)/shard_map/ppermute | solution.py:428
  251.0 22.6 %copy-start.19 = (s32[2]{0:T(128)S(1)}, s32[2]{0:T(128)}, u32[]{:S(2)}) copy-start(s32[2]{0:T(128)} %param.23) | copy-start | bytes 28
  251.0 0.7 copy-start.6
  251.0 0.8 copy-start.7
  254.7 31.7 %all-to-all-start.3 = ((f32[256,1,128]{2,1,0:T(1,128)}), f32[256,1,128]{2,1,0:T(1,128)S(1)}, u32[]{:S(2)}, u32[]{:S(2)}) async-start(f32[256,1,128]{2,1,0:T(1,128)} %bitcast.90), calls=%async_computation.3 | async-start | bytes 262144 | tf_op jit(solution)/shard_map/all_to_all | solution.py:451

commit v4 on v3

--- a/solution.py
+++ b/solution.py
@@ -285,14 +285,19 @@
             cols = slice(c * tokens, (c + 1) * tokens)
             lse = l[...]
             weights = jnp.exp2(lse - log_sum(lse, base[:, cols], other[:, cols] + flags[side]))
-            out[:PATCH, cols] = weighted_sum(weights, p, heads)
-            out[PATCH:, cols] = lse
+            out[:PATCH, cols] = weighted_sum(weights, p, heads).astype(jnp.bfloat16)
+            for i in range(3):
+                part = lse.astype(jnp.bfloat16)
+                out[PATCH + LSE_ROWS * i : PATCH + LSE_ROWS * (i + 1), cols] = part
+                lse = lse - part.astype(jnp.float32)
 
 
 def final_kernel(heads, scalars, p, l, above, below, target, error_out, sum_out):
     lse = l[...]
-    sums = log_sum(lse, above[PATCH:, :] + scalars[1], below[PATCH:, :] + scalars[2])
-    out = weighted_sum(jnp.exp2(lse - sums), p, heads) + above[:PATCH, :] + below[:PATCH, :]
+    parts = [message[...].astype(jnp.float32) for message in (above, below)]
+    lses = [sum(m[PATCH + LSE_ROWS * i : PATCH + LSE_ROWS * (i + 1)] for i in range(3)) for m in parts]
+    sums = log_sum(lse, lses[0] + scalars[1], lses[1] + scalars[2])
+    out = weighted_sum(jnp.exp2(lse - sums), p, heads) + parts[0][:PATCH] + parts[1][:PATCH]
     error = jnp.transpose(out) - target[...].astype(jnp.float32)
     error_out[...] = (scalars[0] * error).astype(jnp.bfloat16)
     sum_out[...] = jnp.broadcast_to(jnp.sum(error * error, keepdims=True), sum_out.shape)
@@ -413,7 +418,7 @@
     lse_d = jnp.concatenate([l for _, l in downs], axis=1)
     other = lax.ppermute(jnp.where(low, lse_u, lse_d), "tm", swap)
     flags = jnp.where(low, jnp.array([0.0, NEG]), jnp.array([NEG, 0.0])).astype(jnp.float32)
-    shape = jax.ShapeDtypeStruct((PATCH + LSE_ROWS, tokens), jnp.float32)
+    shape = jax.ShapeDtypeStruct((PATCH + 3 * LSE_ROWS, tokens), jnp.bfloat16)
     to_above, to_below = whole(
         functools.partial(scale_kernel, heads, rows_dev),
         [shape, shape],

time: 292 us -> 289 us (0.990)
  transfers between devices with their start and end apart: 15 -> 15, of which waited for: 5 -> 4; matrix products, arithmetic and copies ran while one was open for 10% -> 10% of each run, Pallas kernels for 23% -> 23%
where the time goes in v4:
time: 289 us; the launch traced here: 288 us
  starting transfers between devices  96.3 us (33%)
  waiting for transfers between devices  76 us (26%)
  Pallas kernels  70.5 us (24%)
  local copies, waits for them, and re-layouts  25.3 us (9%)
  other arithmetic  13.8 us (5%)
  between operations  6 us (2%)
    all_to_all x1, waiting for transfers between devices, body(): lax.all_to_all(payload, 'height', split_axis=0, concat_axis=0, tiled=True)  46.8 us
    pallas_call x4, Pallas kernels, window_attention(): pl.pallas_call(functools.partial(window_kernel, groups, columns), grid=(s...  46.7 us
    all_to_all x1, starting transfers between devices, body(): lax.all_to_all(far_p.reshape(slot_count, tile_len, width), 'height', spli...  23.5 us
    all_to_all x1, starting transfers between devices, body(): lax.all_to_all(squares, ('pair', 'tm', 'height'), split_axis=0, concat_ax...  17.2 us
    pallas_call x4, Pallas kernels, whole(): pl.pallas_call(kernel, in_specs=specs, out_specs=jax.tree.map(lambda _: p...  12.3 us
    ppermute x1, waiting for transfers between devices, body(): halo_before = lax.ppermute(last, 'height', up_rows)  11.7 us
    all_to_all x1, waiting for transfers between devices, body(): lax.all_to_all(squares, ('pair', 'tm', 'height'), split_axis=0, concat_ax...  11.6 us
    pallas_call x1, Pallas kernels, far_attention(): pl.pallas_call(functools.partial(far_kernel, per_step, heads), grid_spec=...  11.5 us
  transfers between devices with their start and end apart: 15, of which 4 were waited for; matrix products, arithmetic and copies ran while one was open for 10% of the time, Pallas kernels for 23%

profile of v4, /device:TPU:1, one launch (start us, length us, event | category | flops | bytes accessed | tf_op | source)
XLA Modules:
  0.0 287.8 jit_solution(14886416849476714591)
XLA Ops:
  0.6 2.0 fusion.6
  2.6 0.4 copy-done
  3.0 0.2 fusion.5
  3.2 1.6 pad_maximum_fusion.1
  4.9 4.6 %collective-permute-start = (bf16[768,1536]{1,0:T(8,128)(2,1)}, bf16[768,1536]{1,0:T(8,128)(2,1)}, u32[]{:S(2)}, u32[]{:S(2)}) collective-permute-start(bf16[768,1536]{1,0:T(8,128)(2,1)} %pad_maximum_fusion.1), channel_id=1, source_target_pairs={{0,4},{4,8},{8,12},{12,16},{16,20},{20,24},{24,28},{28,32},{32,36}... | collective-permute-start | bytes 7077896 | tf_op jit(solution)/shard_map/ppermute | solution.py:337
  9.5 1.6 pad_maximum_fusion.2
  11.1 3.2 %collective-permute-start.1 = (bf16[768,1536]{1,0:T(8,128)(2,1)}, bf16[768,1536]{1,0:T(8,128)(2,1)S(1)}, u32[]{:S(2)}, u32[]{:S(2)}) collective-permute-start(bf16[768,1536]{1,0:T(8,128)(2,1)} %pad_maximum_fusion.2), channel_id=1, source_target_pairs={{4,0},{8,4},{12,8},{16,12},{20,16},{24,20},{28,24},{32,28},{36,32}... | collective-permute-start | bytes 7077896 | tf_op jit(solution)/shard_map/ppermute | solution.py:338
  14.3 0.5 broadcast.131
  14.9 0.7 multiply_reduce_fusion
  15.7 0.2 convert_reduce_fusion
  16.1 3.4 %pad_maximum_fusion = bf16[24,32,1664]{2,1,0:T(8,128)(2,1)} fusion(bf16[24,32,128]{2,1,0:T(8,128)(2,1)S(1)} %broadcast_in_dim.14, bf16[24,32,1536]{2,1,0:T(8,128)(2,1)} %bitcast.72), kind=kLoop, calls=%fused_computation.2 | loop fusion | flops 5111808 | bytes 5111808 | tf_op jit(solution)/shard_map/concatenate | solution.py:349
  19.5 4.4 %gather_fusion = bf16[32,32,1664]{2,1,0:T(8,128)(2,1)} fusion(bf16[24,32,1664]{2,1,0:T(8,128)(2,1)} %pad_maximum_fusion, s32[1024]{0:T(1024)S(1)} %pad_clamp_fusion.1), kind=kCustom, calls=%fused_computation | custom fusion | bytes 6815872 | tf_op jit(solution)/shard_map/gather | solution.py:349
  23.9 11.7 %collective-permute-done.refs_1_.refs_4_.refs_2_.refs_5_ = bf16[768,1536]{1,0:T(8,128)(2,1)} collective-permute-done((bf16[768,1536]{1,0:T(8,128)(2,1)}, bf16[768,1536]{1,0:T(8,128)(2,1)}, u32[]{:S(2)}, u32[]{:S(2)}) %collective-permute-start) | collective-permute-done | bytes 2359328 | tf_op jit(solution)/shard_map/ppermute | solution.py:337
  35.6 5.9 %collective-permute-done.1.refs_2_.refs_3_.refs_6_.refs_4_.refs_7_ = bf16[768,1536]{1,0:T(8,128)(2,1)S(1)} collective-permute-done((bf16[768,1536]{1,0:T(8,128)(2,1)}, bf16[768,1536]{1,0:T(8,128)(2,1)S(1)}, u32[]{:S(2)}, u32[]{:S(2)}) %collective-permute-start.1) | collective-permute-done | bytes 2359328 | tf_op jit(solution)/shard_map/ppermute | solution.py:338
  41.5 1.5 copy-done.1
  43.0 6.7 %all-to-all-start = ((bf16[32,32,1664]{2,1,0:T(8,128)(2,1)}), bf16[32,32,1664]{2,1,0:T(8,128)(2,1)}, u32[]{:S(2)}, u32[]{:S(2)}) async-start(bf16[32,32,1664]{2,1,0:T(8,128)(2,1)} %shard_map.130), calls=%async_computation | async-start | bytes 6815744 | tf_op jit(solution)/shard_map/all_to_all | solution.py:351
  49.6 1.6 fusion.4
  51.2 5.9 %collective-permute-start.2 = (bf16[384,1536]{1,0:T(8,128)(2,1)}, bf16[384,1536]{1,0:T(8,128)(2,1)}, u32[]{:S(2)}, u32[]{:S(2)}) collective-permute-start(bf16[384,1536]{1,0:T(8,128)(2,1)} %shard_map.135), channel_id=1, source_target_pairs={{0,64},{64,128},{128,192},{1,65},{65,129},{129,193},{2,66},{66,130... | collective-permute-start | bytes 3538952 | tf_op jit(solution)/shard_map/ppermute | solution.py:357
  57.1 1.3 collective-permute-start.3
  58.5 5.1 %collective-permute-start.4 = (bf16[384,1536]{1,0:T(8,128)(2,1)}, bf16[384,1536]{1,0:T(8,128)(2,1)S(1)}, u32[]{:S(2)}, u32[]{:S(2)}) collective-permute-start(bf16[384,1536]{1,0:T(8,128)(2,1)} %shard_map.137), channel_id=1, source_target_pairs={{0,64},{64,128},{128,192},{1,65},{65,129},{129,193},{2,66},{66,130... | collective-permute-start | bytes 3538952 | tf_op jit(solution)/shard_map/ppermute | solution.py:357
  63.6 1.3 collective-permute-start.5
  64.9 0.3 fusion.7
  65.2 0.8 scatter.6
  66.0 0.7 bitcast_dynamic-update-slice_fusion
  66.7 2.3 copy.40
  69.0 1.2 reshape.258.wbd_ref
  70.2 0.7 pad_maximum_fusion.4.edge_ref
  70.9 0.6 pad_maximum_fusion.5.edge_ref
  71.5 11.6 %shard_map.131 = (f32[768,384]{1,0:T(8,128)}, f32[16,384]{1,0:T(8,128)}) custom-call(f32[2]{0:T(128)} %pad_maximum_fusion.4.edge_ref, bf16[768,1536]{1,0:T(8,128)(2,1)} %bitcast.73, bf16[768,1536]{1,0:T(8,128)(2,1)} %collective-permute-done.refs_1_.refs_4_.refs_2_.refs_5_, bf16[768,1536]{1,0:T(8,128)(2,1)} %bitcast.63, bf16[768,1536]{1,0:T(8,128)(2,1)} %bitcast.64, ...), custom_call_target="tpu_custom_call" | custom-call | flops 1 | bytes 1 | tf_op jit(solution)/shard_map/pallas_call | solution.py:119
  83.0 11.6 %shard_map.132 = (f32[768,384]{1,0:T(8,128)}, f32[16,384]{1,0:T(8,128)}) custom-call(f32[2]{0:T(128)} %pad_maximum_fusion.5.edge_ref, bf16[768,1536]{1,0:T(8,128)(2,1)} %bitcast.74, bf16[768,1536]{1,0:T(8,128)(2,1)} %bitcast.65, bf16[768,1536]{1,0:T(8,128)(2,1)} %bitcast.66, bf16[768,1536]{1,0:T(8,128)(2,1)} %copy-done.1, bf16[768,1536]{1,0:T(8,128)(2,1)} %bitcast.56, ...), custom_call_target="tpu_custom_call" | custom-call | flops 1 | bytes 1 | tf_op jit(solution)/shard_map/pallas_call | solution.py:119
  94.6 46.8 %all-to-all-done = bf16[32,32,1664]{2,1,0:T(8,128)(2,1)} async-done(((bf16[32,32,1664]{2,1,0:T(8,128)(2,1)}), bf16[32,32,1664]{2,1,0:T(8,128)(2,1)}, u32[]{:S(2)}, u32[]{:S(2)}) %all-to-all-start) | async-done | bytes 3407904 | tf_op jit(solution)/shard_map/all_to_all | solution.py:351
  141.4 2.0 fusion.index_ref
  143.4 11.5 %shard_map.133 = (bf16[1024,768]{1,0:T(8,128)(2,1)}, f32[16,16,64]{2,1,0:T(8,128)}) custom-call(s32[32]{0:T(128)} %fusion.index_ref, bf16[1024,1664]{1,0:T(8,128)(2,1)} %bitcast.9.query_ref, bf16[768,1536]{1,0:T(8,128)(2,1)} %bitcast.67, bf16[768,1536]{1,0:T(8,128)(2,1)} %bitcast.58, bf16[256,768]{1,0:T(8,128)(2,1)} %reshape.258.wbd_ref, ...), custom_call_target="tpu_custom_call" | custom-call | flops 1 | bytes 1 | tf_op jit(solution)/shard_map/pallas_call | solution.py:188
  154.9 1.7 reshape.275
  156.6 9.2 %all-to-all-start.1 = ((f32[16,1,1024]{2,1,0:T(1,128)}), f32[16,1,1024]{2,1,0:T(1,128)S(1)}, u32[]{:S(2)}, u32[]{:S(2)}) async-start(f32[16,1,1024]{2,1,0:T(1,128)} %reshape.275), calls=%async_computation.1 | async-start | bytes 131072 | tf_op jit(solution)/shard_map/all_to_all | solution.py:387
  165.8 11.7 %shard_map.136 = (f32[768,384]{1,0:T(8,128)}, f32[768,384]{1,0:T(8,128)}, f32[16,384]{1,0:T(8,128)}, f32[16,384]{1,0:T(8,128)}) custom-call(f32[2]{0:T(128)} %pad_maximum_fusion.4.edge_ref, bf16[384,1536]{1,0:T(8,128)(2,1)} %collective-permute-done.2.refs_0_, bf16[384,1536]{1,0:T(8,128)(2,1)} %collective-permute-done.3.refs_1_, ...), custom_call_target="tpu_custom_call" | custom-call | flops 1 | bytes 1 | tf_op jit(solution)/shard_map/pallas_call | solution.py:119
  177.6 1.0 copy-done.4
  178.6 0.4 copy-done.5
  179.0 23.5 %all-to-all-start.2 = ((bf16[32,32,768]{2,1,0:T(8,128)(2,1)}), bf16[32,32,768]{2,1,0:T(8,128)(2,1)S(1)}, u32[]{:S(2)}, u32[]{:S(2)}) async-start(bf16[32,32,768]{2,1,0:T(8,128)(2,1)} %bitcast.75), calls=%async_computation.2 | async-start | bytes 3145728 | tf_op jit(solution)/shard_map/all_to_all | solution.py:405
  202.6 11.8 %shard_map.140 = (f32[768,384]{1,0:T(8,128)}, f32[768,384]{1,0:T(8,128)}, f32[16,384]{1,0:T(8,128)}, f32[16,384]{1,0:T(8,128)}) custom-call(f32[2]{0:T(128)} %pad_maximum_fusion.5.edge_ref, bf16[384,1536]{1,0:T(8,128)(2,1)} %copy-done.4, bf16[384,1536]{1,0:T(8,128)(2,1)} %copy-done.5, bf16[768,1536]{1,0:T(8,128)(2,1)} %bitcast.70, ...), custom_call_target="tpu_custom_call" | custom-call | flops 1 | bytes 1 | tf_op jit(solution)/shard_map/pallas_call | solution.py:119
  214.4 0.8 maximum_select_fusion
  215.2 0.5 broadcast.132
  215.7 0.8 reduce.18
  216.5 0.7 reshape.276.far_ref
  217.2 6.0 %collective-permute-start.6 = (f32[16,768]{1,0:T(8,128)S(1)}, f32[16,768]{1,0:T(8,128)S(1)}, u32[]{:S(2)}, u32[]{:S(2)}) collective-permute-start(f32[16,768]{1,0:T(8,128)S(1)} %maximum_select_fusion), channel_id=1, source_target_pairs={{0,128},{64,192},{128,0},{192,64},{1,129},{65,193},{129,1},{193,65... | collective-permute-start | bytes 147464 | tf_op jit(solution)/shard_map/ppermute | solution.py:419
  223.3 1.9 shard_map.134
  225.2 1.3 collective-permute-start.7
  226.5 4.9 %collective-permute-start.8 = (f32[16,768]{1,0:T(8,128)}, f32[16,768]{1,0:T(8,128)S(1)}, u32[]{:S(2)}, u32[]{:S(2)}) collective-permute-start(f32[16,768]{1,0:T(8,128)} %get-tuple-element.50.base.l), channel_id=1, source_target_pairs={{0,64},{64,128},{128,192},{1,65},{65,129},{129,193},{2,66},{66,130... | collective-permute-start | bytes 147464 | tf_op jit(solution)/shard_map/ppermute | solution.py:392
  231.4 0.5 broadcast_select_fusion.flags
  232.0 0.6 dynamic_slice.12
  233.3 0.6 copy-done.10
  233.9 3.5 %shard_map.141 = (bf16[112,768]{1,0:T(8,128)(2,1)}, bf16[112,768]{1,0:T(8,128)(2,1)}) custom-call(f32[2]{0:T(128)} %broadcast_select_fusion.flags, f32[16,768]{1,0:T(8,128)} %copy-done.10, f32[768,384]{1,0:T(8,128)} %get-tuple-element.59.refs_0_, f32[16,384]{1,0:T(8,128)} %get-tuple-element.53.refs_1_, f32[768,384]{1,0:T(8,128)} %get-tuple-element.60.refs_2_, ...), custom_call_target="tpu_custom_call" | custom-call | flops 1 | bytes 1 | tf_op jit(solution)/shard_map/pallas_call | solution.py:268
  237.4 1.3 collective-permute-start.9
  238.7 4.9 %collective-permute-start.10 = (bf16[112,768]{1,0:T(8,128)(2,1)}, bf16[112,768]{1,0:T(8,128)(2,1)S(1)}, u32[]{:S(2)}, u32[]{:S(2)}) collective-permute-start(bf16[112,768]{1,0:T(8,128)(2,1)} %get-tuple-element.64), channel_id=1, source_target_pairs={{0,64},{64,128},{128,192},{1,65},{65,129},{129,193},{2,66},{66,130... | collective-permute-start | bytes 516104 | tf_op jit(solution)/shard_map/ppermute | solution.py:433
  243.6 0.6 pad_maximum_fusion.3.scalars
  244.2 1.7 gather_fusion.1
  245.9 3.9 %shard_map.139.p = f32[768,768]{1,0:T(8,128)} custom-call(f32[16,768]{1,0:T(8,128)} %get-tuple-element.50.base.l, f32[16,768]{1,0:T(8,128)} %get-tuple-element.51.far_l, bf16[768,768]{1,0:T(8,128)(2,1)} %bitcast.82, f32[768,384]{1,0:T(8,128)} %get-tuple-element.54.refs_0_, f32[16,384]{1,0:T(8,128)} %get-tuple-element.47.refs_0_.refs_1_, ...), custom_call_target="tpu_custom_call" | custom-call | flops 1 | bytes 1 | tf_op jit(solution)/shard_map/pallas_call | solution.py:268
  249.9 0.6 copy-done.7
  250.6 2.9 %shard_map.142 = (bf16[768,64]{1,0:T(8,128)(2,1)}, f32[256,128]{1,0:T(8,128)}) custom-call(f32[3]{0:T(128)} %pad_maximum_fusion.3.scalars, f32[768,768]{1,0:T(8,128)} %shard_map.139.p, f32[16,768]{1,0:T(8,128)} %get-tuple-element.50.base.l, bf16[112,768]{1,0:T(8,128)(2,1)} %copy-done.7, bf16[112,768]{1,0:T(8,128)(2,1)} %copy-done.8, bf16[768,64]{1,0:T(8,128)(2,1)} %bitcast.89), custom_call_target="tpu_custom_call" | custom-call | flops 1 | bytes 1 | tf_op jit(solution)/shard_map/pallas_call | solution.py:268
  253.5 17.2 %all-to-all-start.3 = ((f32[256,1,128]{2,1,0:T(1,128)}), f32[256,1,128]{2,1,0:T(1,128)S(1)}, u32[]{:S(2)}, u32[]{:S(2)}) async-start(f32[256,1,128]{2,1,0:T(1,128)} %bitcast.90), calls=%async_computation.3 | async-start | bytes 262144 | tf_op jit(solution)/shard_map/all_to_all | solution.py:456
  270.7 0.6 dynamic_slice.14
  272.0 11.6 %all-to-all-done.3 = f32[256,1,128]{2,1,0:T(1,128)S(1)} async-done(((f32[256,1,128]{2,1,0:T(1,128)}), f32[256,1,128]{2,1,0:T(1,128)S(1)}, u32[]{:S(2)}, u32[]{:S(2)}) %all-to-all-start.3) | async-done | bytes 131104 | tf_op jit(solution)/shard_map/all_to_all | solution.py:456
  283.6 0.1 slice_reduce_fusion
  283.7 0.6 fusion.8
  (62 shorter events, 0.8 us)
Async XLA Ops:
  0.6 2.4 copy-start
  4.9 30.7 %collective-permute-start = (bf16[768,1536]{1,0:T(8,128)(2,1)}, bf16[768,1536]{1,0:T(8,128)(2,1)}, u32[]{:S(2)}, u32[]{:S(2)}) collective-permute-start(bf16[768,1536]{1,0:T(8,128)(2,1)} %pad_maximum_fusion.1), channel_id=1, source_target_pairs={{0,4},{4,8},{8,12},{12,16},{16,20},{20,24},{24,28},{28,32},{32,36}... | collective-permute-start | bytes 7077896 | tf_op jit(solution)/shard_map/ppermute | solution.py:337
  9.5 5.4 %copy-start.13 = (s32[1,1,2,12,1]{3,4,2,1,0:T(1,128)S(1)}, s32[1,1,2,12,1]{3,4,2,1,0:T(1,128)}, u32[]{:S(2)}) copy-start(s32[1,1,2,12,1]{3,4,2,1,0:T(1,128)} %param.20) | copy-start | bytes 292
  9.5 6.1 %copy-start.17 = (s32[1,1,2,12,1]{3,4,2,1,0:T(1,128)S(1)}, s32[1,1,2,12,1]{3,4,2,1,0:T(1,128)}, u32[]{:S(2)}) copy-start(s32[1,1,2,12,1]{3,4,2,1,0:T(1,128)} %param.21) | copy-start | bytes 292
  11.1 30.4 %collective-permute-start.1 = (bf16[768,1536]{1,0:T(8,128)(2,1)}, bf16[768,1536]{1,0:T(8,128)(2,1)S(1)}, u32[]{:S(2)}, u32[]{:S(2)}) collective-permute-start(bf16[768,1536]{1,0:T(8,128)(2,1)} %pad_maximum_fusion.2), channel_id=1, source_target_pairs={{4,0},{8,4},{12,8},{16,12},{20,16},{24,20},{28,24},{32,28},{36,32}... | collective-permute-start | bytes 7077896 | tf_op jit(solution)/shard_map/ppermute | solution.py:338
  15.9 3.6 %copy-start.14 = (s32[24]{0:T(128)}, s32[24]{0:T(128)S(1)}, u32[]{:S(2)}) copy-start(s32[24]{0:T(128)S(1)} %multiply_add_fusion.slot_ref) | copy-start | bytes 292
  41.5 1.5 copy-start.1
  43.0 6.7 %copy-start.2 = (bf16[1,1,2,12,32,1536]{5,4,3,2,1,0:T(8,128)(2,1)S(1)}, bf16[1,1,2,12,32,1536]{5,4,3,2,1,0:T(8,128)(2,1)}, u32[]{:S(2)}) copy-start(bf16[1,1,2,12,32,1536]{5,4,3,2,1,0:T(8,128)(2,1)} %param.15) | copy-start | bytes 7077892
  43.0 98.4 %all-to-all-start = ((bf16[32,32,1664]{2,1,0:T(8,128)(2,1)}), bf16[32,32,1664]{2,1,0:T(8,128)(2,1)}, u32[]{:S(2)}, u32[]{:S(2)}) async-start(bf16[32,32,1664]{2,1,0:T(8,128)(2,1)} %shard_map.130), calls=%async_computation | async-start | bytes 6815744 | tf_op jit(solution)/shard_map/all_to_all | solution.py:351
  51.2 114.6 %collective-permute-start.2 = (bf16[384,1536]{1,0:T(8,128)(2,1)}, bf16[384,1536]{1,0:T(8,128)(2,1)}, u32[]{:S(2)}, u32[]{:S(2)}) collective-permute-start(bf16[384,1536]{1,0:T(8,128)(2,1)} %shard_map.135), channel_id=1, source_target_pairs={{0,64},{64,128},{128,192},{1,65},{65,129},{129,193},{2,66},{66,130... | collective-permute-start | bytes 3538952 | tf_op jit(solution)/shard_map/ppermute | solution.py:357
  57.1 108.7 %collective-permute-start.3 = (bf16[384,1536]{1,0:T(8,128)(2,1)}, bf16[384,1536]{1,0:T(8,128)(2,1)}, u32[]{:S(2)}, u32[]{:S(2)}) collective-permute-start(bf16[384,1536]{1,0:T(8,128)(2,1)} %shard_map.135), channel_id=1, source_target_pairs={{64,0},{128,64},{192,128},{65,1},{129,65},{193,129},{66,2},{130,66... | collective-permute-start | bytes 3538952 | tf_op jit(solution)/shard_map/ppermute | solution.py:358
  58.4 6.4 %copy-start.3 = (bf16[1536,64]{0,1:T(8,128)(2,1)S(1)}, bf16[1536,64]{0,1:T(8,128)(2,1)}, u32[]{:S(2)}) copy-start(bf16[1536,64]{0,1:T(8,128)(2,1)} %param.18) | copy-start | bytes 589828
  58.5 119.1 %collective-permute-start.4 = (bf16[384,1536]{1,0:T(8,128)(2,1)}, bf16[384,1536]{1,0:T(8,128)(2,1)S(1)}, u32[]{:S(2)}, u32[]{:S(2)}) collective-permute-start(bf16[384,1536]{1,0:T(8,128)(2,1)} %shard_map.137), channel_id=1, source_target_pairs={{0,64},{64,128},{128,192},{1,65},{65,129},{129,193},{2,66},{66,130... | collective-permute-start | bytes 3538952 | tf_op jit(solution)/shard_map/ppermute | solution.py:357
  63.6 114.0 %collective-permute-start.5 = (bf16[384,1536]{1,0:T(8,128)(2,1)}, bf16[384,1536]{1,0:T(8,128)(2,1)S(1)}, u32[]{:S(2)}, u32[]{:S(2)}) collective-permute-start(bf16[384,1536]{1,0:T(8,128)(2,1)} %shard_map.137), channel_id=1, source_target_pairs={{64,0},{128,64},{192,128},{65,1},{129,65},{193,129},{66,2},{130,66... | collective-permute-start | bytes 3538952 | tf_op jit(solution)/shard_map/ppermute | solution.py:358
  156.6 22.4 %all-to-all-start.1 = ((f32[16,1,1024]{2,1,0:T(1,128)}), f32[16,1,1024]{2,1,0:T(1,128)S(1)}, u32[]{:S(2)}, u32[]{:S(2)}) async-start(f32[16,1,1024]{2,1,0:T(1,128)} %reshape.275), calls=%async_computation.1 | async-start | bytes 131072 | tf_op jit(solution)/shard_map/all_to_all | solution.py:387
  177.6 1.0 copy-start.4
  177.6 1.4 copy-start.5
  179.0 65.2 %all-to-all-start.2 = ((bf16[32,32,768]{2,1,0:T(8,128)(2,1)}), bf16[32,32,768]{2,1,0:T(8,128)(2,1)S(1)}, u32[]{:S(2)}, u32[]{:S(2)}) async-start(bf16[32,32,768]{2,1,0:T(8,128)(2,1)} %bitcast.75), calls=%async_computation.2 | async-start | bytes 3145728 | tf_op jit(solution)/shard_map/all_to_all | solution.py:405
  202.6 11.8 %copy-start.6 = (f32[16,384]{1,0:T(8,128)S(1)}, f32[16,384]{1,0:T(8,128)}, u32[]{:S(2)}) copy-start(f32[16,384]{1,0:T(8,128)} %get-tuple-element.53.refs_1_) | copy-start | bytes 73732
  202.6 11.8 %copy-start.9 = (f32[16,384]{1,0:T(8,128)S(1)}, f32[16,384]{1,0:T(8,128)}, u32[]{:S(2)}) copy-start(f32[16,384]{1,0:T(8,128)} %get-tuple-element.57.refs_5_) | copy-start | bytes 73732
  202.6 28.8 %copy-start.15 = (f32[2]{0:T(128)S(1)}, f32[2]{0:T(128)}, u32[]{:S(2)}) copy-start(f32[2]{0:T(128)} %constant.144.clone) | copy-start | bytes 28
  202.6 28.8 %copy-start.16 = (f32[2]{0:T(128)S(1)}, f32[2]{0:T(128)}, u32[]{:S(2)}) copy-start(f32[2]{0:T(128)} %constant.145.clone) | copy-start | bytes 28
  202.6 29.4 %copy-start.18 = (s32[2]{0:T(128)S(1)}, s32[2]{0:T(128)}, u32[]{:S(2)}) copy-start(s32[2]{0:T(128)} %param.22) | copy-start | bytes 28
  217.2 16.0 %collective-permute-start.6 = (f32[16,768]{1,0:T(8,128)S(1)}, f32[16,768]{1,0:T(8,128)S(1)}, u32[]{:S(2)}, u32[]{:S(2)}) collective-permute-start(f32[16,768]{1,0:T(8,128)S(1)} %maximum_select_fusion), channel_id=1, source_target_pairs={{0,128},{64,192},{128,0},{192,64},{1,129},{65,193},{129,1},{193,65... | collective-permute-start | bytes 147464 | tf_op jit(solution)/shard_map/ppermute | solution.py:419
  225.2 8.1 %collective-permute-start.7 = (f32[16,768]{1,0:T(8,128)}, f32[16,768]{1,0:T(8,128)S(1)}, u32[]{:S(2)}, u32[]{:S(2)}) collective-permute-start(f32[16,768]{1,0:T(8,128)} %get-tuple-element.50.base.l), channel_id=1, source_target_pairs={{64,0},{128,64},{192,128},{65,1},{129,65},{193,129},{66,2},{130,66... | collective-permute-start | bytes 147464 | tf_op jit(solution)/shard_map/ppermute | solution.py:393
  226.5 6.8 %collective-permute-start.8 = (f32[16,768]{1,0:T(8,128)}, f32[16,768]{1,0:T(8,128)S(1)}, u32[]{:S(2)}, u32[]{:S(2)}) collective-permute-start(f32[16,768]{1,0:T(8,128)} %get-tuple-element.50.base.l), channel_id=1, source_target_pairs={{0,64},{64,128},{128,192},{1,65},{65,129},{129,193},{2,66},{66,130... | collective-permute-start | bytes 147464 | tf_op jit(solution)/shard_map/ppermute | solution.py:392
  233.3 0.6 copy-start.10
  233.3 0.6 copy-start.11
  233.3 0.6 copy-start.12
  237.4 12.4 %collective-permute-start.9 = (bf16[112,768]{1,0:T(8,128)(2,1)}, bf16[112,768]{1,0:T(8,128)(2,1)S(1)}, u32[]{:S(2)}, u32[]{:S(2)}) collective-permute-start(bf16[112,768]{1,0:T(8,128)(2,1)} %get-tuple-element.63), channel_id=1, source_target_pairs={{64,0},{128,64},{192,128},{65,1},{129,65},{193,129},{66,2},{130,66... | collective-permute-start | bytes 516104 | tf_op jit(solution)/shard_map/ppermute | solution.py:434
  238.7 11.2 %collective-permute-start.10 = (bf16[112,768]{1,0:T(8,128)(2,1)}, bf16[112,768]{1,0:T(8,128)(2,1)S(1)}, u32[]{:S(2)}, u32[]{:S(2)}) collective-permute-start(bf16[112,768]{1,0:T(8,128)(2,1)} %get-tuple-element.64), channel_id=1, source_target_pairs={{0,64},{64,128},{128,192},{1,65},{65,129},{129,193},{2,66},{66,130... | collective-permute-start | bytes 516104 | tf_op jit(solution)/shard_map/ppermute | solution.py:433
  249.8 20.9 %copy-start.19 = (s32[2]{0:T(128)S(1)}, s32[2]{0:T(128)}, u32[]{:S(2)}) copy-start(s32[2]{0:T(128)} %param.23) | copy-start | bytes 28
  249.8 0.7 copy-start.7
  249.9 0.7 copy-start.8
  253.5 30.0 %all-to-all-start.3 = ((f32[256,1,128]{2,1,0:T(1,128)}), f32[256,1,128]{2,1,0:T(1,128)S(1)}, u32[]{:S(2)}, u32[]{:S(2)}) async-start(f32[256,1,128]{2,1,0:T(1,128)} %bitcast.90), calls=%async_computation.3 | async-start | bytes 262144 | tf_op jit(solution)/shard_map/all_to_all | solution.py:456
